TPU v7x, 256 devices: a whole 4x4x8 slice. The times are simulated.
256 devices in a mesh: engine: 16 (over y, x), seq: 16 (over z, core).
Axes of the slice: x: 4, y: 4, z: 8, core: 2. Of those that a mesh axis runs over, the one named last changes fastest.
Arguments:
- queries: bfloat16 [512, 4, 4096], P(('engine', 'seq')), may hold values from -16 to 16
- new_keys: bfloat16 [512, 4, 512], P(('engine', 'seq')), may hold values from -6 to 6
- new_values: bfloat16 [512, 4, 512], P(('engine', 'seq')), may hold values from -12 to 12
- suffix_keys: bfloat16 [512, 512, 512], P(('engine', 'seq')), may hold values from -6 to 6
- suffix_values: bfloat16 [512, 512, 512], P(('engine', 'seq')), may hold values from -12 to 12
- suffix_len: int32 [512], P(('engine', 'seq')), may hold values from 1 to 512, as said below
- sample_prompt: int32 [512, 1], P(('engine', 'seq')), may hold values from 0 to 15; in each aligned block of 32 rows (0 to 31, 32 to 63, ...) at most 3 rows name the same one
- prefix_keys: bfloat16 [16, 16384, 512], P('engine', 'seq'), may hold values from -6 to 6
- prefix_values: bfloat16 [16, 16384, 512], P('engine', 'seq'), may hold values from -12 to 12
Outputs:
- attended: bfloat16 [512, 4, 4096], P(('engine', 'seq'))
Inputs may be any that keep to these rules, and one draw needn't show every extreme that they name: `suffix_len`: every draw has a sample whose length is 512. `sample_prompt`: within the samples of one index of engine (aligned blocks of 32 samples) no prompt is named by more than 3 samples, a bound that some block reaches.
All inputs are finite; a program needn't handle non-finite values.
Results may differ from a plain program's by a relative error of at most 0.0022.
Values may be sent and summed in bfloat16 or wider, within the bound.
No kernel may reach another device: no remote copies, remote signals or barrier semaphores. Data moves between devices by JAX's collectives and lax.ppermute only.
A program may use at most 64 MiB of HBM per device.

v0:
```python
import jax
import jax.numpy as jnp
from jax import lax
from jax.sharding import PartitionSpec as P

HQ = 32
KVH = 4
HD = 128
GROUP = 8


def prefix_partial(received, prompt_keys, prompt_values, scaling):
    lead = received.shape[:3]
    row_count = lead[0] * lead[1] * lead[2]
    query_rows = received.reshape(row_count, KVH, GROUP * HD)
    outputs = []
    logs = []
    for group_index in range(KVH):
        group_queries = query_rows[:, group_index].reshape(row_count * GROUP, HD)
        group_keys = prompt_keys[:, group_index * HD : (group_index + 1) * HD]
        group_values = prompt_values[:, group_index * HD : (group_index + 1) * HD]
        scores = (
            lax.dot_general(
                group_queries,
                group_keys,
                (((1,), (1,)), ((), ())),
                preferred_element_type=jnp.float32,
            )
            * scaling
        )
        row_max = jnp.max(scores, axis=1)
        probs = jnp.exp(scores - row_max[:, None])
        row_sum = jnp.sum(probs, axis=1)
        block_out = (
            jnp.dot(probs.astype(jnp.bfloat16), group_values, preferred_element_type=jnp.float32)
            / row_sum[:, None]
        )
        outputs.append(block_out.reshape(row_count, GROUP, HD))
        logs.append((row_max + jnp.log(row_sum)).reshape(row_count, GROUP))
    block_out = jnp.stack(outputs, axis=1).reshape(lead + (HQ, HD))
    block_lse = jnp.stack(logs, axis=1).reshape(lead + (HQ,))
    return (block_out, block_lse)


def local(
    queries,
    new_keys,
    new_values,
    suffix_keys,
    suffix_values,
    suffix_len,
    sample_prompt,
    prefix_keys,
    prefix_values,
):
    scaling = HD ** (-0.5)
    samples = queries.shape[0]
    step_count = queries.shape[1]
    features = queries.shape[2]
    seq_count = lax.axis_size("seq")
    engine_count = lax.axis_size("engine")
    row_block = samples * seq_count
    capacity = (3 * row_block + 2 * engine_count - 1) // (2 * engine_count)
    row_queries = lax.all_gather(queries, "seq", axis=0, tiled=True)
    row_ids = lax.all_gather(sample_prompt, "seq", axis=0, tiled=True)[:, 0]
    one_hot = (row_ids[:, None] == jnp.arange(engine_count, dtype=jnp.int32)[None, :]).astype(
        jnp.int32
    )
    earlier = jnp.cumsum(one_hot, axis=0) - one_hot
    rank_within = jnp.sum(earlier * one_hot, axis=1)
    slot_index = row_ids * capacity + rank_within
    dispatch = (
        jnp.arange(engine_count * capacity, dtype=jnp.int32)[:, None] == slot_index[None, :]
    ).astype(jnp.bfloat16)
    packed = jnp.dot(
        dispatch,
        row_queries.reshape(row_block, step_count * features),
        preferred_element_type=jnp.float32,
    )
    packed = packed.astype(jnp.bfloat16).reshape(engine_count, capacity, step_count, features)
    prompt_keys = prefix_keys[0]
    prompt_values = prefix_values[0]
    block_out, block_lse = prefix_partial(
        lax.all_to_all(packed, "engine", split_axis=0, concat_axis=0, tiled=True),
        prompt_keys,
        prompt_values,
        scaling,
    )
    reply_out = lax.all_to_all(block_out, "engine", split_axis=0, concat_axis=0, tiled=True)
    reply_lse = lax.all_to_all(block_lse, "engine", split_axis=0, concat_axis=0, tiled=True)
    reply_out = reply_out.reshape((engine_count * capacity, step_count) + reply_out.shape[3:])
    reply_lse = reply_lse.reshape((engine_count * capacity, step_count) + reply_lse.shape[3:])
    sample_out = jnp.take(reply_out, slot_index, axis=0)
    sample_lse = jnp.take(reply_lse, slot_index, axis=0)
    spread_out, spread_lse = (
        lax.all_to_all(
            sample_out.reshape(seq_count, samples, step_count, HQ, HD),
            "seq",
            split_axis=0,
            concat_axis=0,
            tiled=True,
        ),
        lax.all_to_all(
            sample_lse.reshape(seq_count, samples, step_count, HQ),
            "seq",
            split_axis=0,
            concat_axis=0,
            tiled=True,
        ),
    )
    highest = jnp.max(spread_lse, axis=0)
    weight = jnp.exp(spread_lse - highest[None])
    weight_sum = jnp.sum(weight, axis=0)
    prefix_out = jnp.sum(weight[..., None] * spread_out, axis=0) / weight_sum[..., None]
    prefix_lse = highest + jnp.log(weight_sum)
    suffix_count = suffix_keys.shape[1]
    query_heads = queries.reshape(samples, step_count, KVH, GROUP, HD)
    cache_keys = suffix_keys.reshape(samples, suffix_count, KVH, HD)
    cache_values = suffix_values.reshape(samples, suffix_count, KVH, HD)
    fresh_keys = new_keys.reshape(samples, step_count, KVH, HD)
    fresh_values = new_values.reshape(samples, step_count, KVH, HD)
    cache_scores = (
        jnp.einsum("stgid,sjgd->stgij", query_heads, cache_keys, preferred_element_type=jnp.float32)
        * scaling
    )
    fresh_scores = (
        jnp.einsum("stgid,sugd->stgiu", query_heads, fresh_keys, preferred_element_type=jnp.float32)
        * scaling
    )
    live_mask = jnp.arange(suffix_count, dtype=jnp.int32)[None, :] < suffix_len[:, None]
    causal = jnp.arange(step_count)[None, :] <= jnp.arange(step_count)[:, None]
    cache_scores = jnp.where(live_mask[:, None, None, None, :], cache_scores, -jnp.inf)
    fresh_scores = jnp.where(causal[None, :, None, None, :], fresh_scores, -jnp.inf)
    row_max = jnp.maximum(jnp.max(cache_scores, axis=-1), jnp.max(fresh_scores, axis=-1))
    cache_probs = jnp.exp(cache_scores - row_max[..., None])
    fresh_probs = jnp.exp(fresh_scores - row_max[..., None])
    row_sum = jnp.sum(cache_probs, axis=-1) + jnp.sum(fresh_probs, axis=-1)
    suffix_out = (
        jnp.einsum(
            "stgij,sjgd->stgid",
            cache_probs.astype(jnp.bfloat16),
            cache_values,
            preferred_element_type=jnp.float32,
        )
        + jnp.einsum(
            "stgiu,sugd->stgid",
            fresh_probs.astype(jnp.bfloat16),
            fresh_values,
            preferred_element_type=jnp.float32,
        )
    ) / row_sum[..., None]
    suffix_lse = row_max + jnp.log(row_sum)
    suffix_out = suffix_out.reshape(samples, step_count, HQ, HD)
    suffix_lse = suffix_lse.reshape(samples, step_count, HQ)
    summit = jnp.maximum(prefix_lse, suffix_lse)
    prefix_weight = jnp.exp(prefix_lse - summit)
    suffix_weight = jnp.exp(suffix_lse - summit)
    combined = (prefix_weight[..., None] * prefix_out + suffix_weight[..., None] * suffix_out) / (
        prefix_weight + suffix_weight
    )[..., None]
    return combined.reshape(samples, step_count, features).astype(jnp.bfloat16)


def solution(mesh):
    return jax.shard_map(
        local,
        mesh=mesh,
        in_specs=(
            P(("engine", "seq"), None, None),
            P(("engine", "seq"), None, None),
            P(("engine", "seq"), None, None),
            P(("engine", "seq"), None, None),
            P(("engine", "seq"), None, None),
            P(("engine", "seq")),
            P(("engine", "seq"), None),
            P("engine", "seq", None),
            P("engine", "seq", None),
        ),
        out_specs=P(("engine", "seq"), None, None),
        check_vma=False,
    )
```

profile of v0, /device:TPU:1, one launch (start us, length us, event | category | flops | bytes accessed | tf_op | source)
XLA Modules:
  0.0 251.4 jit_solution(12246751631977765427)
XLA Ops:
  6.5 0.7 all-gather.2.cloned.1.call-update
  7.3 1.3 dynamic-slice
  9.2 0.8 bitcast_dynamic-update-slice_fusion
  9.9 14.7 %all-reduce = s32[32]{0:T(128)S(1)} all-reduce(s32[32]{0:T(128)S(1)} %bitcast_dynamic-update-slice_fusion), channel_id=1, replica_groups=mesh['engine'=16,'seq'=16] {'seq'}, use_global_device_ids=true, to_apply=%add | all-reduce | flops 32 | bytes 256 | tf_op jit(solution)/shard_map/eq | solution.py:66
  25.0 27.1 %all-gather.2.cloned.1.call-done = bf16[32,4,4096]{2,1,0:T(4,128)(2,1)} async-done(((bf16[2,4,4096]{2,1,0:T(4,128)(2,1)}), bf16[32,4,4096]{2,1,0:T(4,128)(2,1)}) %all-gather.2.cloned.1.call-update) | async-done | bytes 1048592 | tf_op jit(solution)/shard_map/all_gather | solution.py:64
  52.0 1.8 copy.84
  53.9 0.5 convolution_convert_fusion
  54.4 1.2 reshape.282
  55.6 28.5 %all_to_all.25 = bf16[16,3,4,4096]{3,2,1,0:T(4,128)(2,1)} all-to-all(bf16[16,3,4,4096]{3,2,1,0:T(4,128)(2,1)S(1)} %reshape.282), channel_id=1, replica_groups=mesh['engine'=16,'seq'=16] {'engine'}, dimensions={0} | all-to-all | bytes 3145728 | tf_op jit(solution)/shard_map/all_to_all | solution.py:84
  84.1 2.9 %reshape.283 = bf16[192,4,1024]{2,1,0:T(4,128)(2,1)S(1)} reshape(bf16[16,3,4,4096]{3,2,1,0:T(4,128)(2,1)} %all_to_all.25) | data formatting | bytes 3145728 | tf_op jit(solution)/shard_map/reshape | solution.py:15
  87.0 8.3 %slice_reduce_fusion.3 = (bf16[192,1024]{1,0:T(8,128)(2,1)S(1)}, bf16[192,1024]{1,0:T(8,128)(2,1)S(1)}, bf16[192,1024]{1,0:T(8,128)(2,1)S(1)}, bf16[192,1024]{1,0:T(8,128)(2,1)S(1)}) fusion(bf16[192,4,1024]{2,1,0:T(4,128)(2,1)S(1)} %reshape.283), kind=kLoop, calls=%fused_computation.56 | loop fusion | bytes 3145728 | tf_op jit(solution)/shard_map/slice | solution.py:19
  95.5 1.9 multiply_reduce_fusion.3
  97.4 1.1 fusion.1
  98.5 2.3 fusion.45
  101.0 1.0 multiply_reduce_fusion.2
  102.0 1.1 fusion.3
  103.1 3.1 %fusion.42 = f32[192,1,8,128]{3,2,1,0:T(8,128)} fusion(f32[1536,1024]{0,1:T(8,128)S(1)} %get-tuple-element.27, f32[1536]{0:T(1024)S(1)} %get-tuple-element.26, f32[1536]{0:T(1024)S(1)} %fusion.3, bf16[1024,512]{1,0:T(8,128)(2,1)} %bitcast.112), kind=kOutput, calls=%fused_computation.39 | convolution fusion | flops 407568384 | bytes 7352320 | tf_op jit(solution)/shard_map/dot_general | solution.py:35
  106.4 1.0 multiply_reduce_fusion.1
  107.4 1.1 fusion.5
  108.5 3.1 %fusion.39 = f32[192,1,8,128]{3,2,1,0:T(8,128)} fusion(f32[1536,1024]{0,1:T(8,128)S(1)} %get-tuple-element.25, f32[1536]{0:T(1024)S(1)} %get-tuple-element.24, f32[1536]{0:T(1024)S(1)} %fusion.5, bf16[1024,512]{1,0:T(8,128)(2,1)} %bitcast.113), kind=kOutput, calls=%fused_computation.38 | convolution fusion | flops 407568384 | bytes 7352320 | tf_op jit(solution)/shard_map/dot_general | solution.py:35
  111.7 1.2 multiply_reduce_fusion
  113.0 1.1 fusion.7
  114.0 3.2 %fusion.36 = f32[192,1,8,128]{3,2,1,0:T(8,128)} fusion(f32[1536,1024]{0,1:T(8,128)S(1)} %get-tuple-element.23, f32[1536]{0:T(1024)S(1)} %get-tuple-element.22, f32[1536]{0:T(1024)S(1)} %fusion.7, bf16[1024,512]{1,0:T(8,128)(2,1)} %bitcast.114), kind=kOutput, calls=%fused_computation.37 | convolution fusion | flops 407568384 | bytes 7352320 | tf_op jit(solution)/shard_map/dot_general | solution.py:35
  118.2 0.7 reshape.334
  119.0 3.5 %all-to-all-start.1 = ((f32[16,1,384]{2,1,0:T(1,128)}), f32[16,1,384]{2,1,0:T(1,128)S(1)}, u32[]{:S(2)}, u32[]{:S(2)}) async-start(f32[16,1,384]{2,1,0:T(1,128)} %reshape.334), calls=%async_computation.1 | async-start | bytes 49152 | tf_op jit(solution)/shard_map/all_to_all | solution.py:90
  122.5 3.1 %pad_maximum_fusion = f32[192,4,8,128]{3,2,1,0:T(8,128)} fusion(f32[192,1,8,128]{3,2,1,0:T(8,128)} %fusion.36, f32[192,1,8,128]{3,2,1,0:T(8,128)S(1)} %copy-done.4, f32[192,1,8,128]{3,2,1,0:T(8,128)S(1)} %copy-done.3, f32[192,1,8,128]{3,2,1,0:T(8,128)S(1)} %fusion.45), kind=kLoop, calls=%fused_computation.23 | loop fusion | flops 2359296 | bytes 6291456 | tf_op jit(solution)/shard_map/stack | solution.py:40
  125.6 3.3 %all-to-all-done.1 = f32[16,1,384]{2,1,0:T(1,128)S(1)} async-done(((f32[16,1,384]{2,1,0:T(1,128)}), f32[16,1,384]{2,1,0:T(1,128)S(1)}, u32[]{:S(2)}, u32[]{:S(2)}) %all-to-all-start.1) | async-done | bytes 24608 | tf_op jit(solution)/shard_map/all_to_all | solution.py:90
  128.9 3.7 %all-to-all-start.3 = ((f32[16,3,4,32,128]{4,3,2,1,0:T(8,128)}), f32[16,3,4,32,128]{4,3,2,1,0:T(8,128)S(1)}, u32[]{:S(2)}, u32[]{:S(2)}) async-start(f32[16,3,4,32,128]{4,3,2,1,0:T(8,128)} %bitcast.22), calls=%async_computation.3 | async-start | bytes 6291456 | tf_op jit(solution)/shard_map/all_to_all | solution.py:89
  132.7 0.5 broadcast.122
  133.2 0.7 reduce.12
  134.0 0.6 gather_fusion
  134.8 0.7 reshape.336
  135.5 37.7 %all-to-all-done.3 = f32[16,3,4,32,128]{4,3,2,1,0:T(8,128)S(1)} async-done(((f32[16,3,4,32,128]{4,3,2,1,0:T(8,128)}), f32[16,3,4,32,128]{4,3,2,1,0:T(8,128)S(1)}, u32[]{:S(2)}, u32[]{:S(2)}) %all-to-all-start.3) | async-done | bytes 3145760 | tf_op jit(solution)/shard_map/all_to_all | solution.py:89
  173.2 8.4 %all-to-all-start.2 = ((f32[16,1,256]{2,1,0:T(1,128)}), f32[16,1,256]{2,1,0:T(1,128)S(1)}, u32[]{:S(2)}, u32[]{:S(2)}) async-start(f32[16,1,256]{2,1,0:T(1,128)} %reshape.336), calls=%async_computation.2 | async-start | bytes 32768 | tf_op jit(solution)/shard_map/all_to_all | solution.py:103
  181.6 2.0 gather_fusion.1
  183.6 3.2 %broadcast_select_fusion = f32[16,2,4,32,128]{4,3,2,1,0:T(8,128)} fusion(f32[16,2,4,32,128]{4,3,2,1,0:T(8,128)} %bitcast.89, pred[16,2]{1,0:T(8,128)(4,1)S(1)} %broadcast_in_dim.42), kind=kLoop, calls=%fused_computation.52 | loop fusion | flops 524288 | bytes 4194336 | tf_op jit(solution)/shard_map/jit(_take)/select_n | solution.py:93
  186.8 2.1 all-to-all-done.2
  188.9 5.1 %all-to-all-start.4 = ((f32[16,2,4,32,128]{4,3,2,1,0:T(8,128)}), f32[16,2,4,32,128]{4,3,2,1,0:T(8,128)S(1)}, u32[]{:S(2)}, u32[]{:S(2)}) async-start(f32[16,2,4,32,128]{4,3,2,1,0:T(8,128)} %broadcast_select_fusion), calls=%async_computation.4 | async-start | bytes 4194304 | tf_op jit(solution)/shard_map/all_to_all | solution.py:96
  194.1 1.1 reshape.286
  195.4 0.4 fusion.96
  195.8 1.8 fusion.95
  197.7 0.7 copy-done.5
  198.7 1.3 reshape.291
  200.3 1.4 fusion.51
  201.8 0.7 reduce.13
  202.9 40.1 %all-to-all-done.4 = f32[16,2,4,32,128]{4,3,2,1,0:T(8,128)S(1)} async-done(((f32[16,2,4,32,128]{4,3,2,1,0:T(8,128)}), f32[16,2,4,32,128]{4,3,2,1,0:T(8,128)S(1)}, u32[]{:S(2)}, u32[]{:S(2)}) %all-to-all-start.4) | async-done | bytes 2097184 | tf_op jit(solution)/shard_map/all_to_all | solution.py:96
  243.0 0.7 multiply_reduce_fusion.4
  243.9 0.7 fusion.72
  (65 shorter events, 3.8 us)
Async XLA Ops:
  6.5 193.5 %copy-start = (bf16[2,4,512]{2,1,0:T(4,128)(2,1)S(1)}, bf16[2,4,512]{2,1,0:T(4,128)(2,1)}, u32[]{:S(2)}) copy-start(bf16[2,4,512]{2,1,0:T(4,128)(2,1)} %param.11) | copy-start | bytes 24580
  6.5 45.5 %all-gather.2.cloned.1.call-start = ((), (), s32[]{:S(2)}) async-start(), calls=%async_computation.5 | async-start | bytes 1114112 | tf_op jit(solution)/shard_map/all_gather | solution.py:64
  98.5 2.5 %copy-start.1 = (bf16[1,1024,512]{2,1,0:T(8,128)(2,1)S(1)}, bf16[1,1024,512]{2,1,0:T(8,128)(2,1)}, u32[]{:S(2)}) copy-start(bf16[1,1024,512]{2,1,0:T(8,128)(2,1)} %param.16) | copy-start | bytes 3145732
  114.0 8.5 %copy-start.3 = (f32[192,1,8,128]{3,2,1,0:T(8,128)S(1)}, f32[192,1,8,128]{3,2,1,0:T(8,128)}, u32[]{:S(2)}) copy-start(f32[192,1,8,128]{3,2,1,0:T(8,128)} %fusion.42) | copy-start | bytes 2359300
  114.0 8.5 %copy-start.4 = (f32[192,1,8,128]{3,2,1,0:T(8,128)S(1)}, f32[192,1,8,128]{3,2,1,0:T(8,128)}, u32[]{:S(2)}) copy-start(f32[192,1,8,128]{3,2,1,0:T(8,128)} %fusion.39) | copy-start | bytes 2359300
  119.0 9.9 %all-to-all-start.1 = ((f32[16,1,384]{2,1,0:T(1,128)}), f32[16,1,384]{2,1,0:T(1,128)S(1)}, u32[]{:S(2)}, u32[]{:S(2)}) async-start(f32[16,1,384]{2,1,0:T(1,128)} %reshape.334), calls=%async_computation.1 | async-start | bytes 49152 | tf_op jit(solution)/shard_map/all_to_all | solution.py:90
  128.9 44.3 %all-to-all-start.3 = ((f32[16,3,4,32,128]{4,3,2,1,0:T(8,128)}), f32[16,3,4,32,128]{4,3,2,1,0:T(8,128)S(1)}, u32[]{:S(2)}, u32[]{:S(2)}) async-start(f32[16,3,4,32,128]{4,3,2,1,0:T(8,128)} %bitcast.22), calls=%async_computation.3 | async-start | bytes 6291456 | tf_op jit(solution)/shard_map/all_to_all | solution.py:89
  173.2 15.7 %all-to-all-start.2 = ((f32[16,1,256]{2,1,0:T(1,128)}), f32[16,1,256]{2,1,0:T(1,128)S(1)}, u32[]{:S(2)}, u32[]{:S(2)}) async-start(f32[16,1,256]{2,1,0:T(1,128)} %reshape.336), calls=%async_computation.2 | async-start | bytes 32768 | tf_op jit(solution)/shard_map/all_to_all | solution.py:103
  181.6 12.5 %copy-start.6 = (bf16[2,4,4096]{2,1,0:T(4,128)(2,1)S(1)}, bf16[2,4,4096]{2,1,0:T(4,128)(2,1)}, u32[]{:S(2)}) copy-start(bf16[2,4,4096]{2,1,0:T(4,128)(2,1)} %param.9) | copy-start | bytes 196612
  183.6 10.6 %copy-start.2 = (bf16[2,512,512]{2,1,0:T(8,128)(2,1)S(1)}, bf16[2,512,512]{2,1,0:T(8,128)(2,1)}, u32[]{:S(2)}) copy-start(bf16[2,512,512]{2,1,0:T(8,128)(2,1)} %param.12) | copy-start | bytes 3145732
  183.6 11.7 %copy-start.7 = (s32[2]{0:T(128)S(1)}, s32[2]{0:T(128)}, u32[]{:S(2)}) copy-start(s32[2]{0:T(128)} %param.14) | copy-start | bytes 28
  183.6 11.8 %copy-start.8 = (bf16[2,4,512]{2,1,0:T(4,128)(2,1)S(1)}, bf16[2,4,512]{2,1,0:T(4,128)(2,1)}, u32[]{:S(2)}) copy-start(bf16[2,4,512]{2,1,0:T(4,128)(2,1)} %param.10) | copy-start | bytes 24580
  188.9 54.1 %all-to-all-start.4 = ((f32[16,2,4,32,128]{4,3,2,1,0:T(8,128)}), f32[16,2,4,32,128]{4,3,2,1,0:T(8,128)S(1)}, u32[]{:S(2)}, u32[]{:S(2)}) async-start(f32[16,2,4,32,128]{4,3,2,1,0:T(8,128)} %broadcast_select_fusion), calls=%async_computation.4 | async-start | bytes 4194304 | tf_op jit(solution)/shard_map/all_to_all | solution.py:96
  197.6 0.8 copy-start.5
Sparse Core Ops, SparseCore 0:
  9.2 42.8 all-gather.1
where the time goes:
time: 252 us; the launch traced here: 251 us
  waiting for transfers between devices  111 us (44%)
  blocking collectives  43.2 us (17%)
  local copies, waits for them, and re-layouts  26.3 us (10%)
  matrix products  21.3 us (8%)
  starting transfers between devices  20.8 us (8%)
  other arithmetic  14.5 us (6%)
  between operations  14.5 us (6%)
    all_to_all x1, waiting for transfers between devices, local(): lax.all_to_all(sample_out.reshape(seq_count, samples, step_count, HQ, HD)...  40.1 us
    all_to_all x1, waiting for transfers between devices, local(): lax.all_to_all(block_out, 'engine', split_axis=0, concat_axis=0, tiled=True)  37.7 us
    all_to_all x1, blocking collectives, local(): lax.all_to_all(packed, 'engine', split_axis=0, concat_axis=0, tiled=True)  28.5 us
    all_gather x1, waiting for transfers between devices, local(): row_queries = lax.all_gather(queries, 'seq', axis=0, tiled=True)  27.1 us
    eq x1, blocking collectives, local(): row_ids[:, None] == jnp.arange(engine_count, dtype=jnp.int32)[None, :]  14.7 us
    dot_general x4, matrix products, prefix_partial(): jnp.dot(probs.astype(jnp.bfloat16), group_values, preferred_element_type=...  11.8 us
    all_to_all x1, starting transfers between devices, local(): lax.all_to_all(sample_lse.reshape(seq_count, samples, step_count, HQ), 's...  8.4 us
    slice x1, local copies, waits for them, and re-layouts, prefix_partial(): group_queries = query_rows[:, group_index].reshape(row_count * GROUP, HD)  8.27 us
  transfers between devices with their start and end apart: 5, of which 5 were waited for; matrix products, arithmetic and copies ran while one was open for 9% of the time, Pallas kernels for 0%

commit v1 on v0

v1 whole, which is shorter than its diff:
```python
import functools
import math

import jax
import jax.numpy as jnp
from jax import lax
from jax.experimental import pallas as pl
from jax.experimental.pallas import tpu as pltpu
from jax.sharding import PartitionSpec as P

KVH = 4
GROUP = 8
HD = 128
CAPE = 3
SCALING = HD ** (-0.5)
LOG2E = math.log2(math.e)
LN2 = math.log(2.0)
LSE_ONE = float(2**20)
VMEM = pl.BlockSpec(memory_space=pltpu.VMEM)
SMEM = pl.BlockSpec(memory_space=pltpu.SMEM)


def params(mib):
    return pltpu.CompilerParams(vmem_limit_bytes=mib * 1024 * 1024)


def shape(dims, dtype):
    return jax.ShapeDtypeStruct(dims, dtype)


def prepare_kernel(prompt_ref, queries_ref, rows_ref, payload_ref):
    samples, steps, features = queries_ref.shape
    heads = features // HD
    part = heads * steps // KVH
    extra = payload_ref.shape[1] - samples * part
    lanes = lax.broadcasted_iota(jnp.int32, (extra, HD), 1)
    note = jnp.zeros((extra, HD), jnp.int32)
    for sample in range(samples):
        note = jnp.where(lanes == sample, prompt_ref[sample], note)
    note = note.astype(jnp.float32).astype(jnp.bfloat16)
    for sample in range(samples):
        for first in range(0, heads, 4):
            tile = jnp.concatenate(
                [
                    queries_ref[sample, :, (first + i) * HD : (first + i + 1) * HD].astype(jnp.float32)
                    for i in range(4)
                ],
                axis=0,
            ).astype(jnp.bfloat16)
            row = first * steps
            rows_ref[sample, row : row + 4 * steps] = tile
            group, row = row // part, row % part
            for place in range(group, payload_ref.shape[0], KVH):
                payload_ref[place, sample * part + row : sample * part + row + 4 * steps] = tile
    for place in range(payload_ref.shape[0]):
        payload_ref[place, samples * part :] = note


def split_kernel(head_ref, k_ref, v_ref, *refs):
    outs, sems = refs[:-1], refs[-1]
    copies = []
    for place, out in enumerate(outs):
        head = jnp.bitwise_xor(head_ref[0], place)
        cols = pl.ds(pl.multiple_of(head * HD, HD), HD)
        for which, array in enumerate((k_ref, v_ref)):
            copies.append(
                pltpu.make_async_copy(array.at[0, :, cols], out.at[which], sems.at[place, which])
            )
    for copy in copies:
        copy.start()
    for copy in copies:
        copy.wait()


def pack_kernel(samples, pick_ref, received_ref, packed_ref):
    part = packed_ref.shape[1] // CAPE
    for slot in range(packed_ref.shape[0] * CAPE):
        sample = pick_ref[slot]
        packed_ref[slot // CAPE, (slot % CAPE) * part : (slot % CAPE + 1) * part] = received_ref[
            sample // samples, pl.ds(pl.multiple_of((sample % samples) * part, part), part)
        ]


def block_attention(rows, keys, values):
    raw = lax.dot_general(rows, keys, (((1,), (1,)), ((), ())), preferred_element_type=jnp.float32)
    top = jnp.max(raw, axis=1, keepdims=True)
    probs = jnp.exp2((raw - top) * (SCALING * LOG2E))
    total = jnp.sum(probs, axis=1, keepdims=True)
    acc = jnp.dot(probs.astype(jnp.bfloat16), values, preferred_element_type=jnp.float32)
    return acc, top, total


def encode(out):
    largest = jnp.max(jnp.abs(out), axis=1, keepdims=True)
    power = jnp.floor(jnp.log2(jnp.maximum(largest, 2.0**-112) * 1.0001)) + 1.0
    code = jnp.clip(jnp.round(out * jnp.exp2(15.0 - power)), -32767.0, 32767.0)
    return code.astype(jnp.int32), power.astype(jnp.int32)


def prefix_kernel(chunk, q_ref, *refs):
    blocks, reply_ref = refs[:-1], refs[-1]
    slots, per = q_ref.shape[0], q_ref.shape[1]
    rows_of = per // 2
    body = CAPE * rows_of

    def step(index, _):
        rows = q_ref[pl.ds(index * chunk, chunk)].reshape(chunk * per, HD)
        parts = [block_attention(rows, block[0], block[1]) for block in blocks]
        top = functools.reduce(jnp.maximum, [part[1] for part in parts])
        weights = [jnp.exp2((part[1] - top) * (SCALING * LOG2E)) for part in parts]
        total = functools.reduce(jnp.add, [w * part[2] for w, part in zip(weights, parts)])
        out = functools.reduce(jnp.add, [w * part[0] for w, part in zip(weights, parts)]) / total
        log = top * SCALING + jnp.log(total)
        code, power = encode(out)
        code = code.reshape(chunk, per, HD)
        packed = jnp.bitwise_or(
            jnp.left_shift(code[:, :rows_of], 16), jnp.bitwise_and(code[:, rows_of:], 0xFFFF)
        )
        row = lax.broadcasted_iota(jnp.int32, (chunk, per, HD), 1)
        lane = lax.broadcasted_iota(jnp.int32, (chunk, per, HD), 2)
        log = jnp.round(log * LSE_ONE).astype(jnp.int32).reshape(chunk, per, 1)
        note = jnp.where(lane == row, log, 0)
        note = jnp.where(lane == row + per, power.reshape(chunk, per, 1), note)
        note = jnp.sum(note, axis=1)
        for part in range(chunk // CAPE):
            dest = index * (chunk // CAPE) + part
            here = slice(part * CAPE, (part + 1) * CAPE)
            reply_ref[dest, 0:body] = packed[here].reshape(body, HD)
            reply_ref[dest, body : body + CAPE] = note[here]
        return 0

    lax.fori_loop(0, slots // chunk, step, 0)


def select_kernel(samples, slot_ref, reply_ref, chosen_ref):
    body = (chosen_ref.shape[1] - 8) // samples
    for sample in range(chosen_ref.shape[0] * samples):
        slot = slot_ref[sample]
        place, which = slot // CAPE, slot % CAPE
        start = (sample % samples) * body
        chosen_ref[sample // samples, start : start + body] = reply_ref[
            place, pl.ds(pl.multiple_of(which * body, body), body)
        ]
        note = samples * body + sample % samples
        chosen_ref[sample // samples, note : note + 1] = reply_ref[
            place, pl.ds(CAPE * body + which, 1)
        ]


def suffix_kernel(length_ref, rows_ref, fresh_k_ref, fresh_v_ref, k_ref, v_ref, out_ref, log_ref):
    samples, positions = k_ref.shape[0], k_ref.shape[1]
    fresh = fresh_k_ref.shape[1]
    per = rows_ref.shape[1] // KVH
    steps = per // GROUP
    column = lax.broadcasted_iota(jnp.int32, (per, positions), 1)
    step = lax.rem(lax.broadcasted_iota(jnp.int32, (per, fresh), 0), steps)
    causal = lax.broadcasted_iota(jnp.int32, (per, fresh), 1) <= step
    for sample in range(samples):
        live = column < length_ref[sample]
        for group in range(KVH):
            cols = slice(group * HD, (group + 1) * HD)
            rows = rows_ref[sample, group * per : (group + 1) * per]
            dims = (((1,), (1,)), ((), ()))
            cache_raw = lax.dot_general(
                rows, k_ref[sample, :, cols], dims, preferred_element_type=jnp.float32
            )
            fresh_raw = lax.dot_general(
                rows, fresh_k_ref[sample, :, cols], dims, preferred_element_type=jnp.float32
            )
            cache_raw = jnp.where(live, cache_raw, -jnp.inf)
            fresh_raw = jnp.where(causal, fresh_raw, -jnp.inf)
            top = jnp.maximum(
                jnp.max(cache_raw, axis=1, keepdims=True), jnp.max(fresh_raw, axis=1, keepdims=True)
            )
            cache_probs = jnp.exp2((cache_raw - top) * (SCALING * LOG2E))
            fresh_probs = jnp.exp2((fresh_raw - top) * (SCALING * LOG2E))
            total = jnp.sum(cache_probs, axis=1, keepdims=True) + jnp.sum(
                fresh_probs, axis=1, keepdims=True
            )
            acc = jnp.dot(
                cache_probs.astype(jnp.bfloat16),
                v_ref[sample, :, cols],
                preferred_element_type=jnp.float32,
            ) + jnp.dot(
                fresh_probs.astype(jnp.bfloat16),
                fresh_v_ref[sample, :, cols],
                preferred_element_type=jnp.float32,
            )
            here = slice(group * per, (group + 1) * per)
            out_ref[sample, here] = acc / total
            log_ref[sample, here] = jnp.broadcast_to(top * SCALING + jnp.log(total), (per, HD))


def combine_kernel(chosen_ref, suffix_out_ref, suffix_log_ref, out_ref):
    places, samples = chosen_ref.shape[0], suffix_out_ref.shape[0]
    steps = out_ref.shape[1]
    body = (chosen_ref.shape[1] - 8) // samples
    per = 2 * body
    row = lax.broadcasted_iota(jnp.int32, (per, HD), 0)
    lane = lax.broadcasted_iota(jnp.int32, (per, HD), 1)

    def turn(note, offset):
        spread = jnp.broadcast_to(note, (per, HD))
        return jnp.sum(jnp.where(lane == row + offset, spread, 0.0), axis=1, keepdims=True)

    for sample in range(samples):
        for group in range(KVH):
            logs, scales, codes = [], [], []
            for place in range(group, places, KVH):
                packed = chosen_ref[place, sample * body : (sample + 1) * body]
                high = jnp.right_shift(packed, 16)
                low = jnp.right_shift(jnp.left_shift(packed, 16), 16)
                codes.append(jnp.concatenate([high, low], axis=0).astype(jnp.float32))
                at = samples * body + sample
                note = chosen_ref[place, at : at + 1].astype(jnp.float32)
                logs.append(turn(note, 0) * (1.0 / LSE_ONE))
                scales.append(jnp.exp2(turn(note, per) - 15.0))
            peak = functools.reduce(jnp.maximum, logs)
            weights = [jnp.exp(log - peak) for log in logs]
            weight_sum = functools.reduce(jnp.add, weights)
            prefix = functools.reduce(
                jnp.add, [(w * s) * c for w, s, c in zip(weights, scales, codes)]
            )
            prefix_log = peak + jnp.log(weight_sum)
            first = group * per
            suffix_log = suffix_log_ref[sample, first : first + per][:, 0:1]
            suffix = suffix_out_ref[sample, first : first + per]
            top = jnp.maximum(prefix_log, suffix_log)
            prefix_weight = jnp.exp(prefix_log - top)
            suffix_weight = jnp.exp(suffix_log - top)
            whole = prefix_weight + suffix_weight
            result = (prefix_weight / (weight_sum * whole)) * prefix + (
                suffix_weight / whole
            ) * suffix
            for i in range(per // steps):
                head = first // steps + i
                out_ref[sample, :, head * HD : (head + 1) * HD] = result[
                    i * steps : (i + 1) * steps
                ].astype(jnp.bfloat16)


def local(
    queries,
    new_keys,
    new_values,
    suffix_keys,
    suffix_values,
    suffix_len,
    sample_prompt,
    prefix_keys,
    prefix_values,
):
    samples, steps, features = queries.shape
    heads = features // HD
    per = GROUP * steps
    seq_count = lax.axis_size("seq")
    engine_count = lax.axis_size("engine")
    positions = prefix_keys.shape[1]

    head_id = lax.rem(lax.axis_index("seq"), KVH).reshape(1)
    heads_of_block = pl.pallas_call(
        split_kernel,
        out_shape=[shape((2, positions, HD), jnp.bfloat16)] * KVH,
        in_specs=[SMEM] + [pl.BlockSpec(memory_space=pl.ANY)] * 2,
        out_specs=[VMEM] * KVH,
        scratch_shapes=[pltpu.SemaphoreType.DMA((KVH, 2))],
        name="split",
    )(head_id, prefix_keys, prefix_values)

    def swap(array, near, swapped):
        pairs = []
        for place in range(seq_count):
            chip, core = place // 2, place % 2
            chip = (chip + near * (2 * core - 1)) % (seq_count // 2)
            pairs.append((place, 2 * chip + (1 - core if swapped else core)))
        return lax.ppermute(array, "seq", pairs)

    blocks = [
        heads_of_block[0],
        swap(heads_of_block[1], 0, True),
        swap(heads_of_block[2], 1, False),
        swap(heads_of_block[3], 1, True),
    ]

    rows, payload = pl.pallas_call(
        prepare_kernel,
        out_shape=(
            shape((samples, heads * steps, HD), jnp.bfloat16),
            shape((seq_count, samples * per + 8, HD), jnp.bfloat16),
        ),
        in_specs=[SMEM, VMEM],
        out_specs=(VMEM, VMEM),
        name="prepare",
    )(sample_prompt.reshape(samples), queries)
    received = lax.all_to_all(payload, "seq", split_axis=0, concat_axis=0, tiled=True)

    ids = received[:, samples * per, 0:samples].astype(jnp.int32).reshape(seq_count * samples)
    order = jnp.arange(seq_count * samples, dtype=jnp.int32)
    same = (ids[:, None] == ids[None, :]) & (order[None, :] < order[:, None])
    slot = ids * CAPE + jnp.sum(same.astype(jnp.int32), axis=1)
    places = jnp.arange(engine_count * CAPE, dtype=jnp.int32)
    pick = jnp.sum(jnp.where(slot[None, :] == places[:, None], order[None, :], 0), axis=1)

    packed = pl.pallas_call(
        functools.partial(pack_kernel, samples),
        out_shape=shape((engine_count, CAPE * per, HD), jnp.bfloat16),
        in_specs=[SMEM, VMEM],
        out_specs=VMEM,
        name="pack",
    )(pick, received)
    dispatched = lax.all_to_all(packed, "engine", split_axis=0, concat_axis=0, tiled=True)

    fresh_pad = ((0, 0), (0, 16 - steps), (0, 0))
    suffix_out, suffix_log = pl.pallas_call(
        suffix_kernel,
        out_shape=(
            shape((samples, heads * steps, HD), jnp.float32),
            shape((samples, heads * steps, HD), jnp.float32),
        ),
        in_specs=[SMEM] + [VMEM] * 5,
        out_specs=(VMEM, VMEM),
        compiler_params=params(24),
        name="suffix",
    )(
        suffix_len,
        rows,
        jnp.pad(new_keys, fresh_pad),
        jnp.pad(new_values, fresh_pad),
        suffix_keys,
        suffix_values,
    )

    reply = pl.pallas_call(
        functools.partial(prefix_kernel, 4 * CAPE),
        out_shape=shape((engine_count, CAPE * per // 2 + 8, HD), jnp.int32),
        in_specs=[VMEM] * (1 + KVH),
        out_specs=VMEM,
        compiler_params=params(48),
        name="prefix",
    )(dispatched.reshape(engine_count * CAPE, per, HD), *blocks)
    returned = lax.all_to_all(reply, "engine", split_axis=0, concat_axis=0, tiled=True)

    chosen = pl.pallas_call(
        functools.partial(select_kernel, samples),
        out_shape=shape((seq_count, samples * per // 2 + 8, HD), jnp.int32),
        in_specs=[SMEM, VMEM],
        out_specs=VMEM,
        name="select",
    )(slot, returned)
    gathered = lax.all_to_all(chosen, "seq", split_axis=0, concat_axis=0, tiled=True)

    return pl.pallas_call(
        combine_kernel,
        out_shape=shape((samples, steps, features), jnp.bfloat16),
        in_specs=[VMEM] * 3,
        out_specs=VMEM,
        compiler_params=params(24),
        name="combine",
    )(gathered, suffix_out, suffix_log)


def solution(mesh):
    return jax.shard_map(
        local,
        mesh=mesh,
        in_specs=(
            P(("engine", "seq"), None, None),
            P(("engine", "seq"), None, None),
            P(("engine", "seq"), None, None),
            P(("engine", "seq"), None, None),
            P(("engine", "seq"), None, None),
            P(("engine", "seq")),
            P(("engine", "seq"), None),
            P("engine", "seq", None),
            P("engine", "seq", None),
        ),
        out_specs=P(("engine", "seq"), None, None),
        check_vma=False,
    )
```

time: 252 us -> 90.9 us (0.36)
  waiting for transfers between devices: 111 us -> 27.3 us
  blocking collectives: 43.2 us -> 13.5 us
  local copies, waits for them, and re-layouts: 26.3 us -> 0.9 us
  Pallas kernels: 0 us -> 23.4 us
  matrix products: 21.3 us -> 0 us
  between operations: 14.5 us -> 0.16 us
  other arithmetic: 14.5 us -> 0.87 us
  starting transfers between devices: 20.8 us -> 24.2 us
    all_to_all x4 -> x3, waiting for transfers between devices: 83.2 us -> 27.3 us  [the longest x1 10.5 us: local(): lax.all_to_all(packed, 'engine', split_axis=0, concat_axis=0, tiled=True)]
    all_gather x1 -> x0, waiting for transfers between devices: 27.1 us -> none  [local(): row_queries = lax.all_gather(queries, 'seq', axis=0, tiled=True)]
    pallas_call x0 -> x7, Pallas kernels: none -> 23.4 us  [the longest x1 10.9 us: local(): pl.pallas_call(functools.partial(prefix_kernel, 4 * CAPE), out_shape=shap...]
    dot_general x13 -> x0, matrix products: 21.3 us -> none  [the longest x4 11.8 us: prefix_partial(): jnp.dot(probs.astype(jnp.bfloat16), group_values, preferred_element_type=...]
    all_to_all x1, blocking collectives: 28.5 us -> 13.5 us  [local(): lax.all_to_all(reply, 'engine', split_axis=0, concat_axis=0, tiled=True)]
    eq x1 -> x0, blocking collectives: 14.7 us -> none  [local(): row_ids[:, None] == jnp.arange(engine_count, dtype=jnp.int32)[None, :]]
    slice x1 -> x0, local copies, waits for them, and re-layouts: 8.27 us -> none  [prefix_partial(): group_queries = query_rows[:, group_index].reshape(row_count * GROUP, HD)]
    reshape x7 -> x0, local copies, waits for them, and re-layouts: 6.92 us -> none  [the longest x1 2.89 us: prefix_partial(): query_rows = received.reshape(row_count, KVH, GROUP * HD)]
  transfers between devices with their start and end apart: 5 -> 6, of which waited for: 5 -> 3; matrix products, arithmetic and copies ran while one was open for 9% -> 1% of each run, Pallas kernels for 0% -> 9%
where the time goes in v1:
time: 90.9 us; the launch traced here: 90.3 us
  waiting for transfers between devices  27.3 us (30%)
  starting transfers between devices  24.2 us (27%)
  Pallas kernels  23.4 us (26%)
  blocking collectives  13.5 us (15%)
    all_to_all x1, blocking collectives, local(): lax.all_to_all(reply, 'engine', split_axis=0, concat_axis=0, tiled=True)  13.5 us
    pallas_call x1, Pallas kernels, local(): pl.pallas_call(functools.partial(prefix_kernel, 4 * CAPE), out_shape=shap...  10.9 us
    all_to_all x1, waiting for transfers between devices, local(): lax.all_to_all(packed, 'engine', split_axis=0, concat_axis=0, tiled=True)  10.5 us
    all_to_all x1, starting transfers between devices, local(): lax.all_to_all(payload, 'seq', split_axis=0, concat_axis=0, tiled=True)  9.98 us
    all_to_all x1, waiting for transfers between devices, local(): lax.all_to_all(chosen, 'seq', split_axis=0, concat_axis=0, tiled=True)  9.44 us
    all_to_all x1, waiting for transfers between devices, local(): lax.all_to_all(payload, 'seq', split_axis=0, concat_axis=0, tiled=True)  7.34 us
    all_to_all x1, starting transfers between devices, local(): lax.all_to_all(packed, 'engine', split_axis=0, concat_axis=0, tiled=True)  6.89 us
    all_to_all x1, starting transfers between devices, local(): lax.all_to_all(chosen, 'seq', split_axis=0, concat_axis=0, tiled=True)  5.14 us
  transfers between devices with their start and end apart: 6, of which 3 were waited for; matrix products, arithmetic and copies ran while one was open for 1% of the time, Pallas kernels for 9%

profile of v1, /device:TPU:1, one launch (start us, length us, event | category | flops | bytes accessed | tf_op | source)
XLA Modules:
  0.0 90.3 jit_solution(3773292822968173134)
XLA Ops:
  0.0 1.6 %prepare.1 = (bf16[2,128,128]{2,1,0:T(8,128)(2,1)}, bf16[16,72,128]{2,1,0:T(8,128)(2,1)}) custom-call(s32[2]{0:T(128)} %bitcast.4, bf16[2,4,4096]{2,1,0:T(4,128)(2,1)} %queries_ref.1), custom_call_target="tpu_custom_call" | custom-call | tf_op jit(solution)/shard_map/prepare/pallas_call | solution.py:285
  1.6 10.0 %all-to-all-start = ((bf16[16,72,128]{2,1,0:T(8,128)(2,1)}), bf16[16,72,128]{2,1,0:T(8,128)(2,1)S(1)}, u32[]{:S(2)}, u32[]{:S(2)}) async-start(bf16[16,72,128]{2,1,0:T(8,128)(2,1)} %get-tuple-element.13), calls=%async_computation | async-start | bytes 589824 | tf_op jit(solution)/shard_map/all_to_all | solution.py:295
  11.6 2.9 %split.1 = (bf16[2,1024,128]{2,1,0:T(8,128)(2,1)}, bf16[2,1024,128]{2,1,0:T(8,128)(2,1)}, bf16[2,1024,128]{2,1,0:T(8,128)(2,1)}, bf16[2,1024,128]{2,1,0:T(8,128)(2,1)}) custom-call(s32[1]{0:T(128)} %bitcast.2.head_ref, bf16[1,1024,512]{2,1,0:T(8,128)(2,1)} %k_ref.2, bf16[1,1024,512]{2,1,0:T(8,128)(2,1)} %v_ref.2), custom_call_target="tpu_custom_call" | custom-call | tf_op jit(solution)/shard_map/split/pallas_call | solution.py:261
  14.6 0.2 collective-permute-start
  14.8 1.6 %collective-permute-start.1 = (bf16[2,1024,128]{2,1,0:T(8,128)(2,1)}, bf16[2,1024,128]{2,1,0:T(8,128)(2,1)S(1)}, u32[]{:S(2)}, u32[]{:S(2)}) collective-permute-start(bf16[2,1024,128]{2,1,0:T(8,128)(2,1)} %get-tuple-element.16), channel_id=1, source_target_pairs={{0,14},{1,3},{2,0},{3,5},{4,2},{5,7},{6,4},{7,9},{8,6},{9,11},{10,... | collective-permute-start | bytes 1572872 | tf_op jit(solution)/shard_map/ppermute | solution.py:276
  16.4 0.4 collective-permute-start.2
  16.8 7.3 %all-to-all-done.received_ref = bf16[16,72,128]{2,1,0:T(8,128)(2,1)S(1)} async-done(((bf16[16,72,128]{2,1,0:T(8,128)(2,1)}), bf16[16,72,128]{2,1,0:T(8,128)(2,1)S(1)}, u32[]{:S(2)}, u32[]{:S(2)}) %all-to-all-start) | async-done | bytes 294944 | tf_op jit(solution)/shard_map/all_to_all | solution.py:295
  24.1 0.0 copy-start.5
  24.2 0.1 reshape.33
  24.3 0.2 convert_reduce_fusion
  24.4 0.0 copy-start.8
  24.5 0.7 select_reduce_fusion.pick_ref
  25.1 0.0 copy-done.5
  25.1 0.0 copy-done.8
  25.1 2.0 %pack.1 = bf16[16,96,128]{2,1,0:T(8,128)(2,1)} custom-call(s32[48]{0:T(128)} %select_reduce_fusion.pick_ref, bf16[16,72,128]{2,1,0:T(8,128)(2,1)} %copy-done.5), custom_call_target="tpu_custom_call" | custom-call | tf_op jit(solution)/shard_map/pack/pallas_call | solution.py:304
  27.2 0.0 copy-start.2
  27.2 6.9 %all-to-all-start.1 = ((bf16[16,96,128]{2,1,0:T(8,128)(2,1)}), bf16[16,96,128]{2,1,0:T(8,128)(2,1)S(1)}, u32[]{:S(2)}, u32[]{:S(2)}) async-start(bf16[16,96,128]{2,1,0:T(8,128)(2,1)} %pack.1), calls=%async_computation.1 | async-start | bytes 786432 | tf_op jit(solution)/shard_map/all_to_all | solution.py:311
  34.1 0.0 collective-permute-done.refs_1_
  34.1 0.0 collective-permute-done.1.refs_2_
  34.1 0.0 collective-permute-done.2.refs_3_
  34.1 10.5 %all-to-all-done.1 = bf16[16,96,128]{2,1,0:T(8,128)(2,1)S(1)} async-done(((bf16[16,96,128]{2,1,0:T(8,128)(2,1)}), bf16[16,96,128]{2,1,0:T(8,128)(2,1)S(1)}, u32[]{:S(2)}, u32[]{:S(2)}) %all-to-all-start.1) | async-done | bytes 393248 | tf_op jit(solution)/shard_map/all_to_all | solution.py:311
  44.6 0.0 copy-done.2
  44.6 10.9 %prefix.1 = s32[16,56,128]{2,1,0:T(8,128)S(1)} custom-call(bf16[48,32,128]{2,1,0:T(8,128)(2,1)S(1)} %bitcast.3, bf16[2,1024,128]{2,1,0:T(8,128)(2,1)S(1)} %copy-done.2, bf16[2,1024,128]{2,1,0:T(8,128)(2,1)S(1)} %collective-permute-done.refs_1_, bf16[2,1024,128]{2,1,0:T(8,128)(2,1)S(1)} %collective-permute-done.1.refs_2_, ...), custom_call_target="tpu_custom_call" | custom-call | tf_op jit(solution)/shard_map/prefix/pallas_call | solution.py:333
  55.5 0.0 copy-start
  55.5 0.0 copy-start.1
  55.5 13.5 %all_to_all.20.reply_ref = s32[16,56,128]{2,1,0:T(8,128)} all-to-all(s32[16,56,128]{2,1,0:T(8,128)S(1)} %prefix.1), channel_id=1, replica_groups=mesh['engine'=16,'seq'=16] {'engine'}, dimensions={0} | all-to-all | bytes 917504 | tf_op jit(solution)/shard_map/all_to_all | solution.py:341
  69.0 2.0 %select.5 = s32[16,40,128]{2,1,0:T(8,128)} custom-call(s32[32]{0:T(128)} %copy-done.8, s32[16,56,128]{2,1,0:T(8,128)} %all_to_all.20.reply_ref), custom_call_target="tpu_custom_call" | custom-call | tf_op jit(solution)/shard_map/select/pallas_call | solution.py:343
  71.0 0.0 copy-start.6
  71.0 0.0 copy-start.7
  71.0 5.1 %all-to-all-start.3 = ((s32[16,40,128]{2,1,0:T(8,128)}), s32[16,40,128]{2,1,0:T(8,128)S(1)}, u32[]{:S(2)}, u32[]{:S(2)}) async-start(s32[16,40,128]{2,1,0:T(8,128)} %select.5), calls=%async_computation.3 | async-start | bytes 655360 | tf_op jit(solution)/shard_map/all_to_all | solution.py:350
  76.1 0.0 copy-done.6
  76.2 0.0 copy-start.3
  76.2 0.0 copy-done.7
  76.2 0.0 copy-start.4
  76.2 0.0 copy-done
  76.2 0.0 copy-done.1
  76.2 0.8 copy-done.3
  77.0 0.0 copy-done.4
  77.0 2.7 %suffix.1 = (f32[2,128,128]{2,1,0:T(8,128)S(1)}, f32[2,128,128]{2,1,0:T(8,128)S(1)}) custom-call(s32[2]{0:T(128)S(1)} %copy-done.4, bf16[2,128,128]{2,1,0:T(8,128)(2,1)S(1)} %copy-done.3, bf16[2,16,512]{2,1,0:T(8,128)(2,1)S(1)} %pad.7.fresh_k_ref, bf16[2,16,512]{2,1,0:T(8,128)(2,1)S(1)} %pad.8.fresh_v_ref, bf16[2,512,512]{2,1,0:T(8,128)(2,1)S(1)} %copy-done, ...), custom_call_target="tpu_custom_call" | custom-call | tf_op jit(solution)/shard_map/suffix/pallas_call | solution.py:314
  79.7 9.4 %all-to-all-done.3.chosen_ref = s32[16,40,128]{2,1,0:T(8,128)S(1)} async-done(((s32[16,40,128]{2,1,0:T(8,128)}), s32[16,40,128]{2,1,0:T(8,128)S(1)}, u32[]{:S(2)}, u32[]{:S(2)}) %all-to-all-start.3) | async-done | bytes 327712 | tf_op jit(solution)/shard_map/all_to_all | solution.py:350
  89.2 1.1 %combine.1 = bf16[2,4,4096]{2,1,0:T(4,128)(2,1)} custom-call(s32[16,40,128]{2,1,0:T(8,128)S(1)} %all-to-all-done.3.chosen_ref, f32[2,128,128]{2,1,0:T(8,128)S(1)} %get-tuple-element.19.suffix_out_ref, f32[2,128,128]{2,1,0:T(8,128)S(1)} %get-tuple-element.20.suffix_log_ref), custom_call_target="tpu_custom_call" | custom-call | tf_op jit(solution)/shard_map/combine/pallas_call | solution.py:352
  (4 shorter events, 0.1 us)
Async XLA Ops:
  1.6 22.5 %all-to-all-start = ((bf16[16,72,128]{2,1,0:T(8,128)(2,1)}), bf16[16,72,128]{2,1,0:T(8,128)(2,1)S(1)}, u32[]{:S(2)}, u32[]{:S(2)}) async-start(bf16[16,72,128]{2,1,0:T(8,128)(2,1)} %get-tuple-element.13), calls=%async_computation | async-start | bytes 589824 | tf_op jit(solution)/shard_map/all_to_all | solution.py:295
  14.6 19.5 %collective-permute-start = (bf16[2,1024,128]{2,1,0:T(8,128)(2,1)}, bf16[2,1024,128]{2,1,0:T(8,128)(2,1)S(1)}, u32[]{:S(2)}, u32[]{:S(2)}) collective-permute-start(bf16[2,1024,128]{2,1,0:T(8,128)(2,1)} %get-tuple-element.15), channel_id=1, source_target_pairs={{0,1},{1,0},{2,3},{3,2},{4,5},{5,4},{6,7},{7,6},{8,9},{9,8},{10,11... | collective-permute-start | bytes 1572872 | tf_op jit(solution)/shard_map/ppermute | solution.py:276
  14.8 19.3 %collective-permute-start.1 = (bf16[2,1024,128]{2,1,0:T(8,128)(2,1)}, bf16[2,1024,128]{2,1,0:T(8,128)(2,1)S(1)}, u32[]{:S(2)}, u32[]{:S(2)}) collective-permute-start(bf16[2,1024,128]{2,1,0:T(8,128)(2,1)} %get-tuple-element.16), channel_id=1, source_target_pairs={{0,14},{1,3},{2,0},{3,5},{4,2},{5,7},{6,4},{7,9},{8,6},{9,11},{10,... | collective-permute-start | bytes 1572872 | tf_op jit(solution)/shard_map/ppermute | solution.py:276
  16.4 17.7 %collective-permute-start.2 = (bf16[2,1024,128]{2,1,0:T(8,128)(2,1)}, bf16[2,1024,128]{2,1,0:T(8,128)(2,1)S(1)}, u32[]{:S(2)}, u32[]{:S(2)}) collective-permute-start(bf16[2,1024,128]{2,1,0:T(8,128)(2,1)} %get-tuple-element.17), channel_id=1, source_target_pairs={{0,15},{1,2},{2,1},{3,4},{4,3},{5,6},{6,5},{7,8},{8,7},{9,10},{10,... | collective-permute-start | bytes 1572872 | tf_op jit(solution)/shard_map/ppermute | solution.py:276
  24.1 1.0 %copy-start.5 = (bf16[16,72,128]{2,1,0:T(8,128)(2,1)}, bf16[16,72,128]{2,1,0:T(8,128)(2,1)S(1)}, u32[]{:S(2)}) copy-start(bf16[16,72,128]{2,1,0:T(8,128)(2,1)S(1)} %all-to-all-done.received_ref) | copy-start | bytes 884740
  24.4 0.7 copy-start.8
  27.2 17.4 %copy-start.2 = (bf16[2,1024,128]{2,1,0:T(8,128)(2,1)S(1)}, bf16[2,1024,128]{2,1,0:T(8,128)(2,1)}, u32[]{:S(2)}) copy-start(bf16[2,1024,128]{2,1,0:T(8,128)(2,1)} %get-tuple-element.14.refs_0_) | copy-start | bytes 1572868
  27.2 17.4 %all-to-all-start.1 = ((bf16[16,96,128]{2,1,0:T(8,128)(2,1)}), bf16[16,96,128]{2,1,0:T(8,128)(2,1)S(1)}, u32[]{:S(2)}, u32[]{:S(2)}) async-start(bf16[16,96,128]{2,1,0:T(8,128)(2,1)} %pack.1), calls=%async_computation.1 | async-start | bytes 786432 | tf_op jit(solution)/shard_map/all_to_all | solution.py:311
  55.5 20.7 %copy-start = (bf16[2,512,512]{2,1,0:T(8,128)(2,1)S(1)}, bf16[2,512,512]{2,1,0:T(8,128)(2,1)}, u32[]{:S(2)}) copy-start(bf16[2,512,512]{2,1,0:T(8,128)(2,1)} %k_ref.3) | copy-start | bytes 3145732
  55.5 20.7 %copy-start.1 = (bf16[2,512,512]{2,1,0:T(8,128)(2,1)S(1)}, bf16[2,512,512]{2,1,0:T(8,128)(2,1)}, u32[]{:S(2)}) copy-start(bf16[2,512,512]{2,1,0:T(8,128)(2,1)} %v_ref.3) | copy-start | bytes 3145732
  71.0 5.1 %copy-start.6 = (bf16[2,4,512]{2,1,0:T(4,128)(2,1)S(1)}, bf16[2,4,512]{2,1,0:T(4,128)(2,1)}, u32[]{:S(2)}) copy-start(bf16[2,4,512]{2,1,0:T(4,128)(2,1)} %param.10) | copy-start | bytes 24580
  71.0 5.2 %copy-start.7 = (bf16[2,4,512]{2,1,0:T(4,128)(2,1)S(1)}, bf16[2,4,512]{2,1,0:T(4,128)(2,1)}, u32[]{:S(2)}) copy-start(bf16[2,4,512]{2,1,0:T(4,128)(2,1)} %param.11) | copy-start | bytes 24580
  71.0 18.2 %all-to-all-start.3 = ((s32[16,40,128]{2,1,0:T(8,128)}), s32[16,40,128]{2,1,0:T(8,128)S(1)}, u32[]{:S(2)}, u32[]{:S(2)}) async-start(s32[16,40,128]{2,1,0:T(8,128)} %select.5), calls=%async_computation.3 | async-start | bytes 655360 | tf_op jit(solution)/shard_map/all_to_all | solution.py:350
  76.2 0.8 copy-start.3
  76.2 0.8 copy-start.4

commit v2 on v1

--- a/solution.py
+++ b/solution.py
@@ -72,17 +72,28 @@
         copy.wait()
 
 
-def pack_kernel(samples, pick_ref, received_ref, packed_ref):
-    part = packed_ref.shape[1] // CAPE
-    for slot in range(packed_ref.shape[0] * CAPE):
-        sample = pick_ref[slot]
-        packed_ref[slot // CAPE, (slot % CAPE) * part : (slot % CAPE + 1) * part] = received_ref[
-            sample // samples, pl.ds(pl.multiple_of((sample % samples) * part, part), part)
-        ]
-
-
-def block_attention(rows, keys, values):
-    raw = lax.dot_general(rows, keys, (((1,), (1,)), ((), ())), preferred_element_type=jnp.float32)
+def pack_kernel(samples, received_ref, packed_ref, slots_ref, counts_ref):
+    prompts, part = packed_ref.shape[0], packed_ref.shape[1] // CAPE
+    packed_ref[...] = jnp.zeros(packed_ref.shape, packed_ref.dtype)
+    for prompt in range(prompts):
+        counts_ref[prompt] = 0
+    for place in range(received_ref.shape[0]):
+        note = received_ref[place, samples * part :].astype(jnp.float32).astype(jnp.int32)
+        for sample in range(samples):
+            prompt = note[0, sample]
+            rank = counts_ref[prompt]
+            counts_ref[prompt] = rank + 1
+            slots_ref[place * samples + sample] = prompt * 4 + rank
+            packed_ref[prompt, pl.ds(pl.multiple_of(rank * part, part), part)] = received_ref[
+                place, sample * part : (sample + 1) * part
+            ]
+
+
+def block_scores(rows, keys):
+    return lax.dot_general(rows, keys, (((1,), (1,)), ((), ())), preferred_element_type=jnp.float32)
+
+
+def block_attention(raw, values):
     top = jnp.max(raw, axis=1, keepdims=True)
     probs = jnp.exp2((raw - top) * (SCALING * LOG2E))
     total = jnp.sum(probs, axis=1, keepdims=True)
@@ -105,11 +116,17 @@
 
     def step(index, _):
         rows = q_ref[pl.ds(index * chunk, chunk)].reshape(chunk * per, HD)
-        parts = [block_attention(rows, block[0], block[1]) for block in blocks]
+        parts, raw = [], block_scores(rows, blocks[0][0])
+        for place, block in enumerate(blocks):
+            ready = raw
+            if place + 1 < len(blocks):
+                raw = block_scores(rows, blocks[place + 1][0])
+            parts.append(block_attention(ready, block[1]))
         top = functools.reduce(jnp.maximum, [part[1] for part in parts])
         weights = [jnp.exp2((part[1] - top) * (SCALING * LOG2E)) for part in parts]
         total = functools.reduce(jnp.add, [w * part[2] for w, part in zip(weights, parts)])
-        out = functools.reduce(jnp.add, [w * part[0] for w, part in zip(weights, parts)]) / total
+        share = 1.0 / total
+        out = functools.reduce(jnp.add, [(w * share) * part[0] for w, part in zip(weights, parts)])
         log = top * SCALING + jnp.log(total)
         code, power = encode(out)
         code = code.reshape(chunk, per, HD)
@@ -132,19 +149,17 @@
     lax.fori_loop(0, slots // chunk, step, 0)
 
 
-def select_kernel(samples, slot_ref, reply_ref, chosen_ref):
+def select_kernel(samples, slots_ref, reply_ref, chosen_ref):
     body = (chosen_ref.shape[1] - 8) // samples
     for sample in range(chosen_ref.shape[0] * samples):
-        slot = slot_ref[sample]
-        place, which = slot // CAPE, slot % CAPE
-        start = (sample % samples) * body
-        chosen_ref[sample // samples, start : start + body] = reply_ref[
-            place, pl.ds(pl.multiple_of(which * body, body), body)
+        slot = slots_ref[sample]
+        prompt, rank = lax.shift_right_logical(slot, 2), lax.bitwise_and(slot, 3)
+        place, start = sample // samples, (sample % samples) * body
+        chosen_ref[place, start : start + body] = reply_ref[
+            prompt, pl.ds(pl.multiple_of(rank * body, body), body)
         ]
         note = samples * body + sample % samples
-        chosen_ref[sample // samples, note : note + 1] = reply_ref[
-            place, pl.ds(CAPE * body + which, 1)
-        ]
+        chosen_ref[place, note : note + 1] = reply_ref[prompt, pl.ds(CAPE * body + rank, 1)]
 
 
 def suffix_kernel(length_ref, rows_ref, fresh_k_ref, fresh_v_ref, k_ref, v_ref, out_ref, log_ref):
@@ -261,9 +276,10 @@
     heads_of_block = pl.pallas_call(
         split_kernel,
         out_shape=[shape((2, positions, HD), jnp.bfloat16)] * KVH,
-        in_specs=[SMEM] + [pl.BlockSpec(memory_space=pl.ANY)] * 2,
+        in_specs=[SMEM] + [pl.BlockSpec(memory_space=pltpu.HBM)] * 2,
         out_specs=[VMEM] * KVH,
         scratch_shapes=[pltpu.SemaphoreType.DMA((KVH, 2))],
+        compiler_params=params(4),
         name="split",
     )(head_id, prefix_keys, prefix_values)
 
@@ -294,22 +310,6 @@
     )(sample_prompt.reshape(samples), queries)
     received = lax.all_to_all(payload, "seq", split_axis=0, concat_axis=0, tiled=True)
 
-    ids = received[:, samples * per, 0:samples].astype(jnp.int32).reshape(seq_count * samples)
-    order = jnp.arange(seq_count * samples, dtype=jnp.int32)
-    same = (ids[:, None] == ids[None, :]) & (order[None, :] < order[:, None])
-    slot = ids * CAPE + jnp.sum(same.astype(jnp.int32), axis=1)
-    places = jnp.arange(engine_count * CAPE, dtype=jnp.int32)
-    pick = jnp.sum(jnp.where(slot[None, :] == places[:, None], order[None, :], 0), axis=1)
-
-    packed = pl.pallas_call(
-        functools.partial(pack_kernel, samples),
-        out_shape=shape((engine_count, CAPE * per, HD), jnp.bfloat16),
-        in_specs=[SMEM, VMEM],
-        out_specs=VMEM,
-        name="pack",
-    )(pick, received)
-    dispatched = lax.all_to_all(packed, "engine", split_axis=0, concat_axis=0, tiled=True)
-
     fresh_pad = ((0, 0), (0, 16 - steps), (0, 0))
     suffix_out, suffix_log = pl.pallas_call(
         suffix_kernel,
@@ -319,7 +319,7 @@
         ),
         in_specs=[SMEM] + [VMEM] * 5,
         out_specs=(VMEM, VMEM),
-        compiler_params=params(24),
+        compiler_params=params(12),
         name="suffix",
     )(
         suffix_len,
@@ -330,12 +330,30 @@
         suffix_values,
     )
 
+    received, suffix_out, suffix_log = lax.optimization_barrier(
+        (received, suffix_out, suffix_log)
+    )
+
+    packed, slots = pl.pallas_call(
+        functools.partial(pack_kernel, samples),
+        out_shape=(
+            shape((engine_count, CAPE * per, HD), jnp.bfloat16),
+            shape((seq_count * samples,), jnp.int32),
+        ),
+        in_specs=[VMEM],
+        out_specs=(VMEM, SMEM),
+        scratch_shapes=[pltpu.SMEM((engine_count,), jnp.int32)],
+        compiler_params=params(4),
+        name="pack",
+    )(received)
+    dispatched = lax.all_to_all(packed, "engine", split_axis=0, concat_axis=0, tiled=True)
+
     reply = pl.pallas_call(
-        functools.partial(prefix_kernel, 4 * CAPE),
+        functools.partial(prefix_kernel, 8 * CAPE),
         out_shape=shape((engine_count, CAPE * per // 2 + 8, HD), jnp.int32),
         in_specs=[VMEM] * (1 + KVH),
         out_specs=VMEM,
-        compiler_params=params(48),
+        compiler_params=params(32),
         name="prefix",
     )(dispatched.reshape(engine_count * CAPE, per, HD), *blocks)
     returned = lax.all_to_all(reply, "engine", split_axis=0, concat_axis=0, tiled=True)
@@ -345,8 +363,9 @@
         out_shape=shape((seq_count, samples * per // 2 + 8, HD), jnp.int32),
         in_specs=[SMEM, VMEM],
         out_specs=VMEM,
+        compiler_params=params(4),
         name="select",
-    )(slot, returned)
+    )(slots, returned)
     gathered = lax.all_to_all(chosen, "seq", split_axis=0, concat_axis=0, tiled=True)
 
     return pl.pallas_call(
@@ -354,7 +373,7 @@
         out_shape=shape((samples, steps, features), jnp.bfloat16),
         in_specs=[VMEM] * 3,
         out_specs=VMEM,
-        compiler_params=params(24),
+        compiler_params=params(6),
         name="combine",
     )(gathered, suffix_out, suffix_log)
 

time: 90.9 us -> 84.1 us (0.925)
  blocking collectives: 13.5 us -> 29.9 us
  waiting for transfers between devices: 27.3 us -> 13.6 us
  Pallas kernels: 23.4 us -> 17.7 us
  starting transfers between devices: 24.2 us -> 19.1 us
  local copies, waits for them, and re-layouts: 0.9 us -> 3.1 us
    all_to_all x0 -> x1, blocking collectives: none -> 17.5 us  [local(): lax.all_to_all(chosen, 'seq', split_axis=0, concat_axis=0, tiled=True)]
    all_to_all x1 -> x0, waiting for transfers between devices: 9.44 us -> none  [local(): lax.all_to_all(chosen, 'seq', split_axis=0, concat_axis=0, tiled=True)]
    all_to_all x1 -> x0, starting transfers between devices: 5.14 us -> none  [local(): lax.all_to_all(chosen, 'seq', split_axis=0, concat_axis=0, tiled=True)]
    all_to_all x1, waiting for transfers between devices: 7.34 us -> 3.03 us  [local(): lax.all_to_all(payload, 'seq', split_axis=0, concat_axis=0, tiled=True)]
    pallas_call x2, Pallas kernels: 12.9 us -> 10.1 us  [the longest x1 9.04 us: local(): pl.pallas_call(functools.partial(prefix_kernel, 8 * CAPE), out_shape=shap...]
    unnamed x18 -> x16, local copies, waits for them, and re-layouts: 0.8 us -> 3.08 us
    pallas_call x1, Pallas kernels: 2.95 us -> 1.43 us  [local(): pl.pallas_call(split_kernel, out_shape=[shape((2, positions, HD), jnp.bfl...]
    pallas_call x1, Pallas kernels: 1.99 us -> 0.62 us  [local(): pl.pallas_call(functools.partial(select_kernel, samples), out_shape=shape...]
  transfers between devices with their start and end apart: 6 -> 5, of which waited for: 3 -> 2; matrix products, arithmetic and copies ran while one was open for 1% -> 0% of each run, Pallas kernels for 9% -> 6%
where the time goes in v2:
time: 84.1 us; the launch traced here: 83.6 us
  blocking collectives  29.9 us (36%)
  starting transfers between devices  19.1 us (23%)
  Pallas kernels  17.7 us (21%)
  waiting for transfers between devices  13.6 us (16%)
  local copies, waits for them, and re-layouts  3.1 us (4%)
    all_to_all x1, blocking collectives, local(): lax.all_to_all(chosen, 'seq', split_axis=0, concat_axis=0, tiled=True)  17.5 us
    all_to_all x1, blocking collectives, local(): lax.all_to_all(reply, 'engine', split_axis=0, concat_axis=0, tiled=True)  12.5 us
    all_to_all x1, waiting for transfers between devices, local(): lax.all_to_all(packed, 'engine', split_axis=0, concat_axis=0, tiled=True)  10.6 us
    all_to_all x1, starting transfers between devices, local(): lax.all_to_all(payload, 'seq', split_axis=0, concat_axis=0, tiled=True)  10.1 us
    pallas_call x1, Pallas kernels, local(): pl.pallas_call(functools.partial(prefix_kernel, 8 * CAPE), out_shape=shap...  9.04 us
    all_to_all x1, starting transfers between devices, local(): lax.all_to_all(packed, 'engine', split_axis=0, concat_axis=0, tiled=True)  6.77 us
    unnamed x16, local copies, waits for them, and re-layouts  3.08 us
    all_to_all x1, waiting for transfers between devices, local(): lax.all_to_all(payload, 'seq', split_axis=0, concat_axis=0, tiled=True)  3.03 us
  transfers between devices with their start and end apart: 5, of which 2 were waited for; matrix products, arithmetic and copies ran while one was open for 0% of the time, Pallas kernels for 6%

profile of v2, /device:TPU:1, one launch (start us, length us, event | category | flops | bytes accessed | tf_op | source)
XLA Modules:
  0.0 83.6 jit_solution(11750206375176267671)
XLA Ops:
  0.0 1.6 %prepare.1 = (bf16[2,128,128]{2,1,0:T(8,128)(2,1)}, bf16[16,72,128]{2,1,0:T(8,128)(2,1)}) custom-call(s32[2]{0:T(128)} %bitcast.4, bf16[2,4,4096]{2,1,0:T(4,128)(2,1)} %queries_ref.1), custom_call_target="tpu_custom_call" | custom-call | tf_op jit(solution)/shard_map/prepare/pallas_call | solution.py:301
  1.6 0.0 copy-start.6
  1.6 10.1 %all-to-all-start = ((bf16[16,72,128]{2,1,0:T(8,128)(2,1)}), bf16[16,72,128]{2,1,0:T(8,128)(2,1)S(1)}, u32[]{:S(2)}, u32[]{:S(2)}) async-start(bf16[16,72,128]{2,1,0:T(8,128)(2,1)} %get-tuple-element.18), calls=%async_computation | async-start | bytes 589824 | tf_op jit(solution)/shard_map/all_to_all | solution.py:311
  11.7 0.0 copy-start
  11.8 1.2 %copy-done = bf16[1,1024,512]{2,1,0:T(8,128)(2,1)S(1)} copy-done((bf16[1,1024,512]{2,1,0:T(8,128)(2,1)S(1)}, bf16[1,1024,512]{2,1,0:T(8,128)(2,1)}, u32[]{:S(2)}) %copy-start) | copy-done | bytes 1048600
  13.0 0.0 copy-start.1
  13.0 1.2 %copy-done.1 = bf16[1,1024,512]{2,1,0:T(8,128)(2,1)S(1)} copy-done((bf16[1,1024,512]{2,1,0:T(8,128)(2,1)S(1)}, bf16[1,1024,512]{2,1,0:T(8,128)(2,1)}, u32[]{:S(2)}) %copy-start.1) | copy-done | bytes 1048600
  14.2 0.0 copy-start.7
  14.2 0.0 copy-start.2
  14.2 0.0 copy-start.3
  14.2 1.4 %split.1 = (bf16[2,1024,128]{2,1,0:T(8,128)(2,1)S(1)}, bf16[2,1024,128]{2,1,0:T(8,128)(2,1)}, bf16[2,1024,128]{2,1,0:T(8,128)(2,1)}, bf16[2,1024,128]{2,1,0:T(8,128)(2,1)S(1)}) custom-call(s32[1]{0:T(128)} %bitcast.2.head_ref, bf16[1,1024,512]{2,1,0:T(8,128)(2,1)S(1)} %copy-done, bf16[1,1024,512]{2,1,0:T(8,128)(2,1)S(1)} %copy-done.1), custom_call_target="tpu_custom_call" | custom-call | tf_op jit(solution)/shard_map/split/pallas_call | solution.py:276
  15.6 0.0 copy-start.4
  15.7 0.2 collective-permute-start
  15.8 1.6 %collective-permute-start.1 = (bf16[2,1024,128]{2,1,0:T(8,128)(2,1)}, bf16[2,1024,128]{2,1,0:T(8,128)(2,1)S(1)}, u32[]{:S(2)}, u32[]{:S(2)}) collective-permute-start(bf16[2,1024,128]{2,1,0:T(8,128)(2,1)} %get-tuple-element.27), channel_id=1, source_target_pairs={{0,14},{1,3},{2,0},{3,5},{4,2},{5,7},{6,4},{7,9},{8,6},{9,11},{10,... | collective-permute-start | bytes 1572872 | tf_op jit(solution)/shard_map/ppermute | solution.py:292
  17.5 0.4 collective-permute-start.2
  17.9 0.0 copy-done.6
  17.9 0.0 copy-done.7
  17.9 0.0 copy-start.5
  17.9 0.0 copy-done.2
  17.9 0.0 copy-done.3
  18.0 0.0 copy-done.4
  18.0 0.6 copy-done.5
  18.6 2.7 %suffix.1 = (f32[2,128,128]{2,1,0:T(8,128)S(1)}, f32[2,128,128]{2,1,0:T(8,128)S(1)}) custom-call(s32[2]{0:T(128)S(1)} %copy-done.5, bf16[2,128,128]{2,1,0:T(8,128)(2,1)S(1)} %copy-done.4, bf16[2,16,512]{2,1,0:T(8,128)(2,1)S(1)} %pad.7.fresh_k_ref, bf16[2,16,512]{2,1,0:T(8,128)(2,1)S(1)} %pad.8.fresh_v_ref, bf16[2,512,512]{2,1,0:T(8,128)(2,1)S(1)} %copy-done.2, ...), custom_call_target="tpu_custom_call" | custom-call | tf_op jit(solution)/shard_map/suffix/pallas_call | solution.py:314
  21.3 3.0 %all-to-all-done.received_ref = bf16[16,72,128]{2,1,0:T(8,128)(2,1)S(1)} async-done(((bf16[16,72,128]{2,1,0:T(8,128)(2,1)}), bf16[16,72,128]{2,1,0:T(8,128)(2,1)S(1)}, u32[]{:S(2)}, u32[]{:S(2)}) %all-to-all-start) | async-done | bytes 294944 | tf_op jit(solution)/shard_map/all_to_all | solution.py:311
  24.4 1.0 %pack.1 = (bf16[16,96,128]{2,1,0:T(8,128)(2,1)}, s32[32]{0:T(128)S(1)}) custom-call(bf16[16,72,128]{2,1,0:T(8,128)(2,1)S(1)} %all-to-all-done.received_ref), custom_call_target="tpu_custom_call" | custom-call | tf_op jit(solution)/shard_map/pack/pallas_call | solution.py:337
  25.4 6.8 %all-to-all-start.1 = ((bf16[16,96,128]{2,1,0:T(8,128)(2,1)}), bf16[16,96,128]{2,1,0:T(8,128)(2,1)S(1)}, u32[]{:S(2)}, u32[]{:S(2)}) async-start(bf16[16,96,128]{2,1,0:T(8,128)(2,1)} %get-tuple-element.24), calls=%async_computation.1 | async-start | bytes 786432 | tf_op jit(solution)/shard_map/all_to_all | solution.py:349
  32.2 0.0 collective-permute-done.refs_1_
  32.2 0.0 collective-permute-done.1.refs_2_
  32.2 0.0 collective-permute-done.2.refs_3_
  32.2 10.6 %all-to-all-done.1 = bf16[16,96,128]{2,1,0:T(8,128)(2,1)S(1)} async-done(((bf16[16,96,128]{2,1,0:T(8,128)(2,1)}), bf16[16,96,128]{2,1,0:T(8,128)(2,1)S(1)}, u32[]{:S(2)}, u32[]{:S(2)}) %all-to-all-start.1) | async-done | bytes 393248 | tf_op jit(solution)/shard_map/all_to_all | solution.py:349
  42.8 9.0 %prefix.1 = s32[16,56,128]{2,1,0:T(8,128)S(1)} custom-call(bf16[48,32,128]{2,1,0:T(8,128)(2,1)S(1)} %bitcast.3, bf16[2,1024,128]{2,1,0:T(8,128)(2,1)S(1)} %get-tuple-element.25.refs_0_, bf16[2,1024,128]{2,1,0:T(8,128)(2,1)S(1)} %collective-permute-done.refs_1_, bf16[2,1024,128]{2,1,0:T(8,128)(2,1)S(1)} %collective-permute-done.1.refs_2_, ...), custom_call_target="tpu_custom_call" | custom-call | tf_op jit(solution)/shard_map/prefix/pallas_call | solution.py:351
  51.9 12.5 %all_to_all.20.reply_ref = s32[16,56,128]{2,1,0:T(8,128)S(1)} all-to-all(s32[16,56,128]{2,1,0:T(8,128)S(1)} %prefix.1), channel_id=1, replica_groups=mesh['engine'=16,'seq'=16] {'engine'}, dimensions={0} | all-to-all | bytes 917504 | tf_op jit(solution)/shard_map/all_to_all | solution.py:359
  64.4 0.6 select.5
  65.0 17.5 %all_to_all.21.chosen_ref = s32[16,40,128]{2,1,0:T(8,128)S(1)} all-to-all(s32[16,40,128]{2,1,0:T(8,128)S(1)} %select.5), channel_id=1, replica_groups=mesh['engine'=16,'seq'=16] {'seq'}, dimensions={0} | all-to-all | bytes 655360 | tf_op jit(solution)/shard_map/all_to_all | solution.py:369
  82.4 1.1 %combine.1 = bf16[2,4,4096]{2,1,0:T(4,128)(2,1)} custom-call(s32[16,40,128]{2,1,0:T(8,128)S(1)} %all_to_all.21.chosen_ref, f32[2,128,128]{2,1,0:T(8,128)S(1)} %get-tuple-element.29.suffix_out_ref, f32[2,128,128]{2,1,0:T(8,128)S(1)} %get-tuple-element.30.suffix_log_ref), custom_call_target="tpu_custom_call" | custom-call | tf_op jit(solution)/shard_map/combine/pallas_call | solution.py:371
  (2 shorter events, 0.0 us)
Async XLA Ops:
  1.6 16.3 %copy-start.6 = (bf16[2,4,512]{2,1,0:T(4,128)(2,1)S(1)}, bf16[2,4,512]{2,1,0:T(4,128)(2,1)}, u32[]{:S(2)}) copy-start(bf16[2,4,512]{2,1,0:T(4,128)(2,1)} %param.10) | copy-start | bytes 24580
  1.6 22.7 %all-to-all-start = ((bf16[16,72,128]{2,1,0:T(8,128)(2,1)}), bf16[16,72,128]{2,1,0:T(8,128)(2,1)S(1)}, u32[]{:S(2)}, u32[]{:S(2)}) async-start(bf16[16,72,128]{2,1,0:T(8,128)(2,1)} %get-tuple-element.18), calls=%async_computation | async-start | bytes 589824 | tf_op jit(solution)/shard_map/all_to_all | solution.py:311
  11.7 1.2 %copy-start = (bf16[1,1024,512]{2,1,0:T(8,128)(2,1)S(1)}, bf16[1,1024,512]{2,1,0:T(8,128)(2,1)}, u32[]{:S(2)}) copy-start(bf16[1,1024,512]{2,1,0:T(8,128)(2,1)} %k_ref.3) | copy-start | bytes 3145732
  13.0 1.2 %copy-start.1 = (bf16[1,1024,512]{2,1,0:T(8,128)(2,1)S(1)}, bf16[1,1024,512]{2,1,0:T(8,128)(2,1)}, u32[]{:S(2)}) copy-start(bf16[1,1024,512]{2,1,0:T(8,128)(2,1)} %v_ref.3) | copy-start | bytes 3145732
  14.2 3.7 %copy-start.7 = (bf16[2,4,512]{2,1,0:T(4,128)(2,1)S(1)}, bf16[2,4,512]{2,1,0:T(4,128)(2,1)}, u32[]{:S(2)}) copy-start(bf16[2,4,512]{2,1,0:T(4,128)(2,1)} %param.11) | copy-start | bytes 24580
  14.2 3.7 %copy-start.2 = (bf16[2,512,512]{2,1,0:T(8,128)(2,1)S(1)}, bf16[2,512,512]{2,1,0:T(8,128)(2,1)}, u32[]{:S(2)}) copy-start(bf16[2,512,512]{2,1,0:T(8,128)(2,1)} %k_ref.2) | copy-start | bytes 3145732
  14.2 3.7 %copy-start.3 = (bf16[2,512,512]{2,1,0:T(8,128)(2,1)S(1)}, bf16[2,512,512]{2,1,0:T(8,128)(2,1)}, u32[]{:S(2)}) copy-start(bf16[2,512,512]{2,1,0:T(8,128)(2,1)} %v_ref.2) | copy-start | bytes 3145732
  15.6 2.3 %copy-start.4 = (bf16[2,128,128]{2,1,0:T(8,128)(2,1)S(1)}, bf16[2,128,128]{2,1,0:T(8,128)(2,1)}, u32[]{:S(2)}) copy-start(bf16[2,128,128]{2,1,0:T(8,128)(2,1)} %get-tuple-element.19.rows_ref) | copy-start | bytes 196612
  15.7 16.5 %collective-permute-start = (bf16[2,1024,128]{2,1,0:T(8,128)(2,1)}, bf16[2,1024,128]{2,1,0:T(8,128)(2,1)S(1)}, u32[]{:S(2)}, u32[]{:S(2)}) collective-permute-start(bf16[2,1024,128]{2,1,0:T(8,128)(2,1)} %get-tuple-element.26), channel_id=1, source_target_pairs={{0,1},{1,0},{2,3},{3,2},{4,5},{5,4},{6,7},{7,6},{8,9},{9,8},{10,11... | collective-permute-start | bytes 1572872 | tf_op jit(solution)/shard_map/ppermute | solution.py:292
  15.8 16.4 %collective-permute-start.1 = (bf16[2,1024,128]{2,1,0:T(8,128)(2,1)}, bf16[2,1024,128]{2,1,0:T(8,128)(2,1)S(1)}, u32[]{:S(2)}, u32[]{:S(2)}) collective-permute-start(bf16[2,1024,128]{2,1,0:T(8,128)(2,1)} %get-tuple-element.27), channel_id=1, source_target_pairs={{0,14},{1,3},{2,0},{3,5},{4,2},{5,7},{6,4},{7,9},{8,6},{9,11},{10,... | collective-permute-start | bytes 1572872 | tf_op jit(solution)/shard_map/ppermute | solution.py:292
  17.5 14.7 %collective-permute-start.2 = (bf16[2,1024,128]{2,1,0:T(8,128)(2,1)S(1)}, bf16[2,1024,128]{2,1,0:T(8,128)(2,1)S(1)}, u32[]{:S(2)}, u32[]{:S(2)}) collective-permute-start(bf16[2,1024,128]{2,1,0:T(8,128)(2,1)S(1)} %get-tuple-element.28), channel_id=1, source_target_pairs={{0,15},{1,2},{2,1},{3,4},{4,3},{5,6},{6,5},{7,8},{8,7},{9,10},{10,... | collective-permute-start | bytes 1572872 | tf_op jit(solution)/shard_map/ppermute | solution.py:292
  17.9 0.7 copy-start.5
  25.4 17.4 %all-to-all-start.1 = ((bf16[16,96,128]{2,1,0:T(8,128)(2,1)}), bf16[16,96,128]{2,1,0:T(8,128)(2,1)S(1)}, u32[]{:S(2)}, u32[]{:S(2)}) async-start(bf16[16,96,128]{2,1,0:T(8,128)(2,1)} %get-tuple-element.24), calls=%async_computation.1 | async-start | bytes 786432 | tf_op jit(solution)/shard_map/all_to_all | solution.py:349

commit v3 on v2

--- a/solution.py
+++ b/solution.py
@@ -95,7 +95,7 @@
 
 def block_attention(raw, values):
     top = jnp.max(raw, axis=1, keepdims=True)
-    probs = jnp.exp2((raw - top) * (SCALING * LOG2E))
+    probs = jnp.exp2(raw * (SCALING * LOG2E) - top * (SCALING * LOG2E))
     total = jnp.sum(probs, axis=1, keepdims=True)
     acc = jnp.dot(probs.astype(jnp.bfloat16), values, preferred_element_type=jnp.float32)
     return acc, top, total
@@ -330,10 +330,6 @@
         suffix_values,
     )
 
-    received, suffix_out, suffix_log = lax.optimization_barrier(
-        (received, suffix_out, suffix_log)
-    )
-
     packed, slots = pl.pallas_call(
         functools.partial(pack_kernel, samples),
         out_shape=(
@@ -348,8 +344,12 @@
     )(received)
     dispatched = lax.all_to_all(packed, "engine", split_axis=0, concat_axis=0, tiled=True)
 
+    dispatched, suffix_out, suffix_log = lax.optimization_barrier(
+        (dispatched, suffix_out, suffix_log)
+    )
+
     reply = pl.pallas_call(
-        functools.partial(prefix_kernel, 8 * CAPE),
+        functools.partial(prefix_kernel, 16 * CAPE),
         out_shape=shape((engine_count, CAPE * per // 2 + 8, HD), jnp.int32),
         in_specs=[VMEM] * (1 + KVH),
         out_specs=VMEM,

time: 84.1 us -> 86.8 us (1.032)
  local copies, waits for them, and re-layouts: 3.1 us -> 5.93 us
  waiting for transfers between devices: 13.6 us -> 11.4 us
  Pallas kernels: 17.7 us -> 19.7 us
    all_to_all x1, waiting for transfers between devices: 10.6 us -> 5.13 us  [local(): lax.all_to_all(packed, 'engine', split_axis=0, concat_axis=0, tiled=True)]
    all_to_all x1, waiting for transfers between devices: 3.03 us -> 6.31 us  [local(): lax.all_to_all(payload, 'seq', split_axis=0, concat_axis=0, tiled=True)]
    unnamed x16 -> x24, local copies, waits for them, and re-layouts: 3.08 us -> 5.18 us
    pallas_call x1, Pallas kernels: 9.04 us -> 11.1 us  [local(): pl.pallas_call(functools.partial(prefix_kernel, 16 * CAPE), out_shape=sha...]
  transfers between devices with their start and end apart: 5 -> 5, of which waited for: 2 -> 2; matrix products, arithmetic and copies ran while one was open for 0% -> 1% of each run, Pallas kernels for 6% -> 6%
where the time goes in v3:
time: 86.8 us; the launch traced here: 86.2 us
  blocking collectives  29.9 us (34%)
  Pallas kernels  19.7 us (23%)
  starting transfers between devices  19.1 us (22%)
  waiting for transfers between devices  11.4 us (13%)
  local copies, waits for them, and re-layouts  5.93 us (7%)
    all_to_all x1, blocking collectives, local(): lax.all_to_all(chosen, 'seq', split_axis=0, concat_axis=0, tiled=True)  17.5 us
    all_to_all x1, blocking collectives, local(): lax.all_to_all(reply, 'engine', split_axis=0, concat_axis=0, tiled=True)  12.5 us
    pallas_call x1, Pallas kernels, local(): pl.pallas_call(functools.partial(prefix_kernel, 16 * CAPE), out_shape=sha...  11.1 us
    all_to_all x1, starting transfers between devices, local(): lax.all_to_all(payload, 'seq', split_axis=0, concat_axis=0, tiled=True)  9.98 us
    all_to_all x1, starting transfers between devices, local(): lax.all_to_all(packed, 'engine', split_axis=0, concat_axis=0, tiled=True)  6.89 us
    all_to_all x1, waiting for transfers between devices, local(): lax.all_to_all(payload, 'seq', split_axis=0, concat_axis=0, tiled=True)  6.31 us
    unnamed x24, local copies, waits for them, and re-layouts  5.18 us
    all_to_all x1, waiting for transfers between devices, local(): lax.all_to_all(packed, 'engine', split_axis=0, concat_axis=0, tiled=True)  5.13 us
  transfers between devices with their start and end apart: 5, of which 2 were waited for; matrix products, arithmetic and copies ran while one was open for 1% of the time, Pallas kernels for 6%

profile of v3, /device:TPU:1, one launch (start us, length us, event | category | flops | bytes accessed | tf_op | source)
XLA Modules:
  0.0 86.2 jit_solution(1659537728004419128)
XLA Ops:
  0.0 1.6 %prepare.1 = (bf16[2,128,128]{2,1,0:T(8,128)(2,1)}, bf16[16,72,128]{2,1,0:T(8,128)(2,1)}) custom-call(s32[2]{0:T(128)} %bitcast.4, bf16[2,4,4096]{2,1,0:T(4,128)(2,1)} %queries_ref.1), custom_call_target="tpu_custom_call" | custom-call | tf_op jit(solution)/shard_map/prepare/pallas_call | solution.py:301
  1.6 10.0 %all-to-all-start = ((bf16[16,72,128]{2,1,0:T(8,128)(2,1)}), bf16[16,72,128]{2,1,0:T(8,128)(2,1)S(1)}, u32[]{:S(2)}, u32[]{:S(2)}) async-start(bf16[16,72,128]{2,1,0:T(8,128)(2,1)} %get-tuple-element.18), calls=%async_computation | async-start | bytes 589824 | tf_op jit(solution)/shard_map/all_to_all | solution.py:311
  11.6 0.0 copy-start
  11.6 1.2 %copy-done = bf16[1,1024,512]{2,1,0:T(8,128)(2,1)S(1)} copy-done((bf16[1,1024,512]{2,1,0:T(8,128)(2,1)S(1)}, bf16[1,1024,512]{2,1,0:T(8,128)(2,1)}, u32[]{:S(2)}) %copy-start) | copy-done | bytes 1048600
  12.8 0.0 copy-start.1
  12.8 1.2 %copy-done.1 = bf16[1,1024,512]{2,1,0:T(8,128)(2,1)S(1)} copy-done((bf16[1,1024,512]{2,1,0:T(8,128)(2,1)S(1)}, bf16[1,1024,512]{2,1,0:T(8,128)(2,1)}, u32[]{:S(2)}) %copy-start.1) | copy-done | bytes 1048600
  14.1 0.0 copy-start.3
  14.1 1.6 %split.1 = (bf16[2,1024,128]{2,1,0:T(8,128)(2,1)S(1)}, bf16[2,1024,128]{2,1,0:T(8,128)(2,1)}, bf16[2,1024,128]{2,1,0:T(8,128)(2,1)}, bf16[2,1024,128]{2,1,0:T(8,128)(2,1)}) custom-call(s32[1]{0:T(128)} %bitcast.2.head_ref, bf16[1,1024,512]{2,1,0:T(8,128)(2,1)S(1)} %copy-done, bf16[1,1024,512]{2,1,0:T(8,128)(2,1)S(1)} %copy-done.1), custom_call_target="tpu_custom_call" | custom-call | tf_op jit(solution)/shard_map/split/pallas_call | solution.py:276
  15.7 0.0 copy-start.2
  15.7 0.2 collective-permute-start
  15.9 1.6 %collective-permute-start.1 = (bf16[2,1024,128]{2,1,0:T(8,128)(2,1)}, bf16[2,1024,128]{2,1,0:T(8,128)(2,1)}, u32[]{:S(2)}, u32[]{:S(2)}) collective-permute-start(bf16[2,1024,128]{2,1,0:T(8,128)(2,1)} %get-tuple-element.27), channel_id=1, source_target_pairs={{0,14},{1,3},{2,0},{3,5},{4,2},{5,7},{6,4},{7,9},{8,6},{9,11},{10,... | collective-permute-start | bytes 1572872 | tf_op jit(solution)/shard_map/ppermute | solution.py:292
  17.5 0.4 collective-permute-start.2
  17.9 6.3 %all-to-all-done.received_ref = bf16[16,72,128]{2,1,0:T(8,128)(2,1)S(1)} async-done(((bf16[16,72,128]{2,1,0:T(8,128)(2,1)}), bf16[16,72,128]{2,1,0:T(8,128)(2,1)S(1)}, u32[]{:S(2)}, u32[]{:S(2)}) %all-to-all-start) | async-done | bytes 294944 | tf_op jit(solution)/shard_map/all_to_all | solution.py:311
  24.2 0.8 pack.1
  25.1 0.0 copy-start.4
  25.1 0.8 copy-done.4
  25.8 0.0 copy-start.11
  25.8 6.9 %all-to-all-start.1 = ((bf16[16,96,128]{2,1,0:T(8,128)(2,1)}), bf16[16,96,128]{2,1,0:T(8,128)(2,1)S(1)}, u32[]{:S(2)}, u32[]{:S(2)}) async-start(bf16[16,96,128]{2,1,0:T(8,128)(2,1)} %copy-done.4), calls=%async_computation.1 | async-start | bytes 786432 | tf_op jit(solution)/shard_map/all_to_all | solution.py:345
  32.7 0.0 copy-done.11
  32.8 0.0 copy-start.9
  32.8 0.7 pad.8.fresh_v_ref
  33.5 0.0 copy-start.10
  33.5 0.0 copy-done.3
  33.5 0.0 copy-done.2
  33.5 0.1 copy-done.9
  33.6 0.6 copy-done.10
  34.2 2.7 %suffix.1 = (f32[2,128,128]{2,1,0:T(8,128)S(1)}, f32[2,128,128]{2,1,0:T(8,128)S(1)}) custom-call(s32[2]{0:T(128)S(1)} %copy-done.10, bf16[2,128,128]{2,1,0:T(8,128)(2,1)S(1)} %copy-done.9, bf16[2,16,512]{2,1,0:T(8,128)(2,1)S(1)} %pad.7.fresh_k_ref, bf16[2,16,512]{2,1,0:T(8,128)(2,1)S(1)} %pad.8.fresh_v_ref, bf16[2,512,512]{2,1,0:T(8,128)(2,1)S(1)} %copy-done.2, ...), custom_call_target="tpu_custom_call" | custom-call | tf_op jit(solution)/shard_map/suffix/pallas_call | solution.py:314
  36.9 0.0 copy-start.5
  36.9 0.7 copy-done.5
  37.6 0.0 copy-start.7
  37.6 0.6 copy-done.7
  38.3 5.1 %all-to-all-done.1 = bf16[16,96,128]{2,1,0:T(8,128)(2,1)S(1)} async-done(((bf16[16,96,128]{2,1,0:T(8,128)(2,1)}), bf16[16,96,128]{2,1,0:T(8,128)(2,1)S(1)}, u32[]{:S(2)}, u32[]{:S(2)}) %all-to-all-start.1) | async-done | bytes 393248 | tf_op jit(solution)/shard_map/all_to_all | solution.py:345
  43.4 0.0 collective-permute-done.refs_1_
  43.4 0.0 collective-permute-done.1.refs_2_
  43.4 0.0 collective-permute-done.2.refs_3_
  43.4 11.1 %prefix.1 = s32[16,56,128]{2,1,0:T(8,128)S(1)} custom-call(bf16[48,32,128]{2,1,0:T(8,128)(2,1)S(1)} %bitcast.3, bf16[2,1024,128]{2,1,0:T(8,128)(2,1)S(1)} %get-tuple-element.25.refs_0_, bf16[2,1024,128]{2,1,0:T(8,128)(2,1)S(1)} %collective-permute-done.refs_1_, bf16[2,1024,128]{2,1,0:T(8,128)(2,1)} %collective-permute-done.1.refs_2_, ...), custom_call_target="tpu_custom_call" | custom-call | tf_op jit(solution)/shard_map/prefix/pallas_call | solution.py:351
  54.5 12.5 %all_to_all.20.reply_ref = s32[16,56,128]{2,1,0:T(8,128)S(1)} all-to-all(s32[16,56,128]{2,1,0:T(8,128)S(1)} %prefix.1), channel_id=1, replica_groups=mesh['engine'=16,'seq'=16] {'engine'}, dimensions={0} | all-to-all | bytes 917504 | tf_op jit(solution)/shard_map/all_to_all | solution.py:359
  67.0 0.6 select.5
  67.6 0.0 copy-start.6
  67.6 0.0 copy-start.8
  67.6 17.5 %all_to_all.21.chosen_ref = s32[16,40,128]{2,1,0:T(8,128)S(1)} all-to-all(s32[16,40,128]{2,1,0:T(8,128)S(1)} %select.5), channel_id=1, replica_groups=mesh['engine'=16,'seq'=16] {'seq'}, dimensions={0} | all-to-all | bytes 655360 | tf_op jit(solution)/shard_map/all_to_all | solution.py:369
  85.1 0.0 copy-done.6
  85.1 0.0 copy-done.8
  85.1 1.1 %combine.1 = bf16[2,4,4096]{2,1,0:T(4,128)(2,1)} custom-call(s32[16,40,128]{2,1,0:T(8,128)S(1)} %all_to_all.21.chosen_ref, f32[2,128,128]{2,1,0:T(8,128)S(1)} %copy-done.6, f32[2,128,128]{2,1,0:T(8,128)S(1)} %copy-done.8), custom_call_target="tpu_custom_call" | custom-call | tf_op jit(solution)/shard_map/combine/pallas_call | solution.py:371
  (1 shorter events, 0.0 us)
Async XLA Ops:
  1.6 22.6 %all-to-all-start = ((bf16[16,72,128]{2,1,0:T(8,128)(2,1)}), bf16[16,72,128]{2,1,0:T(8,128)(2,1)S(1)}, u32[]{:S(2)}, u32[]{:S(2)}) async-start(bf16[16,72,128]{2,1,0:T(8,128)(2,1)} %get-tuple-element.18), calls=%async_computation | async-start | bytes 589824 | tf_op jit(solution)/shard_map/all_to_all | solution.py:311
  11.6 1.2 %copy-start = (bf16[1,1024,512]{2,1,0:T(8,128)(2,1)S(1)}, bf16[1,1024,512]{2,1,0:T(8,128)(2,1)}, u32[]{:S(2)}) copy-start(bf16[1,1024,512]{2,1,0:T(8,128)(2,1)} %k_ref.3) | copy-start | bytes 3145732
  12.8 1.2 %copy-start.1 = (bf16[1,1024,512]{2,1,0:T(8,128)(2,1)S(1)}, bf16[1,1024,512]{2,1,0:T(8,128)(2,1)}, u32[]{:S(2)}) copy-start(bf16[1,1024,512]{2,1,0:T(8,128)(2,1)} %v_ref.3) | copy-start | bytes 3145732
  14.1 19.5 %copy-start.3 = (bf16[2,512,512]{2,1,0:T(8,128)(2,1)S(1)}, bf16[2,512,512]{2,1,0:T(8,128)(2,1)}, u32[]{:S(2)}) copy-start(bf16[2,512,512]{2,1,0:T(8,128)(2,1)} %v_ref.2) | copy-start | bytes 3145732
  15.7 17.9 %copy-start.2 = (bf16[2,512,512]{2,1,0:T(8,128)(2,1)S(1)}, bf16[2,512,512]{2,1,0:T(8,128)(2,1)}, u32[]{:S(2)}) copy-start(bf16[2,512,512]{2,1,0:T(8,128)(2,1)} %k_ref.2) | copy-start | bytes 3145732
  15.7 27.7 %collective-permute-start = (bf16[2,1024,128]{2,1,0:T(8,128)(2,1)}, bf16[2,1024,128]{2,1,0:T(8,128)(2,1)S(1)}, u32[]{:S(2)}, u32[]{:S(2)}) collective-permute-start(bf16[2,1024,128]{2,1,0:T(8,128)(2,1)} %get-tuple-element.26), channel_id=1, source_target_pairs={{0,1},{1,0},{2,3},{3,2},{4,5},{5,4},{6,7},{7,6},{8,9},{9,8},{10,11... | collective-permute-start | bytes 1572872 | tf_op jit(solution)/shard_map/ppermute | solution.py:292
  15.9 27.5 %collective-permute-start.1 = (bf16[2,1024,128]{2,1,0:T(8,128)(2,1)}, bf16[2,1024,128]{2,1,0:T(8,128)(2,1)}, u32[]{:S(2)}, u32[]{:S(2)}) collective-permute-start(bf16[2,1024,128]{2,1,0:T(8,128)(2,1)} %get-tuple-element.27), channel_id=1, source_target_pairs={{0,14},{1,3},{2,0},{3,5},{4,2},{5,7},{6,4},{7,9},{8,6},{9,11},{10,... | collective-permute-start | bytes 1572872 | tf_op jit(solution)/shard_map/ppermute | solution.py:292
  17.5 25.9 %collective-permute-start.2 = (bf16[2,1024,128]{2,1,0:T(8,128)(2,1)}, bf16[2,1024,128]{2,1,0:T(8,128)(2,1)}, u32[]{:S(2)}, u32[]{:S(2)}) collective-permute-start(bf16[2,1024,128]{2,1,0:T(8,128)(2,1)} %get-tuple-element.28), channel_id=1, source_target_pairs={{0,15},{1,2},{2,1},{3,4},{4,3},{5,6},{6,5},{7,8},{8,7},{9,10},{10,... | collective-permute-start | bytes 1572872 | tf_op jit(solution)/shard_map/ppermute | solution.py:292
  25.1 0.8 copy-start.4
  25.8 6.9 %copy-start.11 = (bf16[2,4,512]{2,1,0:T(4,128)(2,1)S(1)}, bf16[2,4,512]{2,1,0:T(4,128)(2,1)}, u32[]{:S(2)}) copy-start(bf16[2,4,512]{2,1,0:T(4,128)(2,1)} %param.10) | copy-start | bytes 24580
  25.8 17.5 %all-to-all-start.1 = ((bf16[16,96,128]{2,1,0:T(8,128)(2,1)}), bf16[16,96,128]{2,1,0:T(8,128)(2,1)S(1)}, u32[]{:S(2)}, u32[]{:S(2)}) async-start(bf16[16,96,128]{2,1,0:T(8,128)(2,1)} %copy-done.4), calls=%async_computation.1 | async-start | bytes 786432 | tf_op jit(solution)/shard_map/all_to_all | solution.py:345
  32.8 0.8 copy-start.9
  33.5 0.7 copy-start.10
  36.9 0.7 copy-start.5
  37.6 0.6 copy-start.7
  67.6 17.5 %copy-start.6 = (f32[2,128,128]{2,1,0:T(8,128)S(1)}, f32[2,128,128]{2,1,0:T(8,128)}, u32[]{:S(2)}) copy-start(f32[2,128,128]{2,1,0:T(8,128)} %copy-done.5) | copy-start | bytes 393220
  67.6 17.5 %copy-start.8 = (f32[2,128,128]{2,1,0:T(8,128)S(1)}, f32[2,128,128]{2,1,0:T(8,128)}, u32[]{:S(2)}) copy-start(f32[2,128,128]{2,1,0:T(8,128)} %copy-done.7) | copy-start | bytes 393220

commit v4 on v3

--- a/solution.py
+++ b/solution.py
@@ -89,16 +89,8 @@
             ]
 
 
-def block_scores(rows, keys):
+def scores(rows, keys):
     return lax.dot_general(rows, keys, (((1,), (1,)), ((), ())), preferred_element_type=jnp.float32)
-
-
-def block_attention(raw, values):
-    top = jnp.max(raw, axis=1, keepdims=True)
-    probs = jnp.exp2(raw * (SCALING * LOG2E) - top * (SCALING * LOG2E))
-    total = jnp.sum(probs, axis=1, keepdims=True)
-    acc = jnp.dot(probs.astype(jnp.bfloat16), values, preferred_element_type=jnp.float32)
-    return acc, top, total
 
 
 def encode(out):
@@ -109,57 +101,71 @@
 
 
 def prefix_kernel(chunk, q_ref, *refs):
-    blocks, reply_ref = refs[:-1], refs[-1]
+    blocks, (reply_ref, raw_ref, probs_ref, acc_ref) = refs[:-4], refs[-4:]
     slots, per = q_ref.shape[0], q_ref.shape[1]
     rows_of = per // 2
-    body = CAPE * rows_of
+    row = lax.broadcasted_iota(jnp.int32, (per, HD), 0)
+    lane = lax.broadcasted_iota(jnp.int32, (per, HD), 1)
 
     def step(index, _):
         rows = q_ref[pl.ds(index * chunk, chunk)].reshape(chunk * per, HD)
-        parts, raw = [], block_scores(rows, blocks[0][0])
+        raw_ref[0] = scores(rows, blocks[0][0])
+        tops, sums = [], []
         for place, block in enumerate(blocks):
-            ready = raw
+            turn = place % 2
             if place + 1 < len(blocks):
-                raw = block_scores(rows, blocks[place + 1][0])
-            parts.append(block_attention(ready, block[1]))
-        top = functools.reduce(jnp.maximum, [part[1] for part in parts])
-        weights = [jnp.exp2((part[1] - top) * (SCALING * LOG2E)) for part in parts]
-        total = functools.reduce(jnp.add, [w * part[2] for w, part in zip(weights, parts)])
-        share = 1.0 / total
-        out = functools.reduce(jnp.add, [(w * share) * part[0] for w, part in zip(weights, parts)])
-        log = top * SCALING + jnp.log(total)
-        code, power = encode(out)
-        code = code.reshape(chunk, per, HD)
-        packed = jnp.bitwise_or(
-            jnp.left_shift(code[:, :rows_of], 16), jnp.bitwise_and(code[:, rows_of:], 0xFFFF)
-        )
-        row = lax.broadcasted_iota(jnp.int32, (chunk, per, HD), 1)
-        lane = lax.broadcasted_iota(jnp.int32, (chunk, per, HD), 2)
-        log = jnp.round(log * LSE_ONE).astype(jnp.int32).reshape(chunk, per, 1)
-        note = jnp.where(lane == row, log, 0)
-        note = jnp.where(lane == row + per, power.reshape(chunk, per, 1), note)
-        note = jnp.sum(note, axis=1)
-        for part in range(chunk // CAPE):
-            dest = index * (chunk // CAPE) + part
-            here = slice(part * CAPE, (part + 1) * CAPE)
-            reply_ref[dest, 0:body] = packed[here].reshape(body, HD)
-            reply_ref[dest, body : body + CAPE] = note[here]
+                raw_ref[1 - turn] = scores(rows, blocks[place + 1][0])
+            for slot in range(chunk):
+                here = slice(slot * per, (slot + 1) * per)
+                raw = raw_ref[turn, here]
+                top = jnp.max(raw, axis=1, keepdims=True)
+                probs = jnp.exp2((raw - top) * (SCALING * LOG2E))
+                probs_ref[turn, here] = probs.astype(jnp.bfloat16)
+                tops.append(top)
+                sums.append(jnp.sum(probs, axis=1, keepdims=True))
+            acc_ref[place] = jnp.dot(
+                probs_ref[turn], block[1], preferred_element_type=jnp.float32
+            )
+        for slot in range(chunk):
+            here = slice(slot * per, (slot + 1) * per)
+            top = functools.reduce(jnp.maximum, tops[slot::chunk])
+            weights = [jnp.exp2((one - top) * (SCALING * LOG2E)) for one in tops[slot::chunk]]
+            total = functools.reduce(
+                jnp.add, [w * one for w, one in zip(weights, sums[slot::chunk])]
+            )
+            share = 1.0 / total
+            out = functools.reduce(
+                jnp.add, [(w * share) * acc_ref[place, here] for place, w in enumerate(weights)]
+            )
+            log = jnp.round((top * SCALING + jnp.log(total)) * LSE_ONE).astype(jnp.int32)
+            code, power = encode(out)
+            packed = jnp.bitwise_or(
+                jnp.left_shift(code[:rows_of], 16), jnp.bitwise_and(code[rows_of:], 0xFFFF)
+            )
+            note = jnp.where(lane == row, log, 0)
+            note = jnp.where(lane == row + per, power, note)
+            note = jnp.sum(note, axis=0, keepdims=True)
+            dest, rank = index * (chunk // CAPE) + slot // CAPE, slot % CAPE
+            for part in range(rows_of // 4):
+                reply_ref[dest, rank * (rows_of // 4) + part] = packed[part * 4 : part * 4 + 4]
+            reply_ref[dest, CAPE * (rows_of // 4), rank : rank + 1] = note
         return 0
 
     lax.fori_loop(0, slots // chunk, step, 0)
 
 
 def select_kernel(samples, slots_ref, reply_ref, chosen_ref):
-    body = (chosen_ref.shape[1] - 8) // samples
+    body = (chosen_ref.shape[1] - 1) // samples
     for sample in range(chosen_ref.shape[0] * samples):
         slot = slots_ref[sample]
         prompt, rank = lax.shift_right_logical(slot, 2), lax.bitwise_and(slot, 3)
-        place, start = sample // samples, (sample % samples) * body
-        chosen_ref[place, start : start + body] = reply_ref[
-            prompt, pl.ds(pl.multiple_of(rank * body, body), body)
+        place, which = sample // samples, sample % samples
+        chosen_ref[place, which * body : (which + 1) * body] = reply_ref[
+            prompt, pl.ds(rank * body, body)
         ]
-        note = samples * body + sample % samples
-        chosen_ref[place, note : note + 1] = reply_ref[prompt, pl.ds(CAPE * body + rank, 1)]
+        chosen_ref[place, samples * body, which : which + 1] = reply_ref[
+            prompt, CAPE * body, pl.ds(rank, 1)
+        ]
 
 
 def suffix_kernel(length_ref, rows_ref, fresh_k_ref, fresh_v_ref, k_ref, v_ref, out_ref, log_ref):
@@ -209,8 +215,8 @@
 def combine_kernel(chosen_ref, suffix_out_ref, suffix_log_ref, out_ref):
     places, samples = chosen_ref.shape[0], suffix_out_ref.shape[0]
     steps = out_ref.shape[1]
-    body = (chosen_ref.shape[1] - 8) // samples
-    per = 2 * body
+    body = (chosen_ref.shape[1] - 1) // samples
+    per = 8 * body
     row = lax.broadcasted_iota(jnp.int32, (per, HD), 0)
     lane = lax.broadcasted_iota(jnp.int32, (per, HD), 1)
 
@@ -222,12 +228,13 @@
         for group in range(KVH):
             logs, scales, codes = [], [], []
             for place in range(group, places, KVH):
-                packed = chosen_ref[place, sample * body : (sample + 1) * body]
+                packed = jnp.concatenate(
+                    [chosen_ref[place, sample * body + part] for part in range(body)], axis=0
+                )
                 high = jnp.right_shift(packed, 16)
                 low = jnp.right_shift(jnp.left_shift(packed, 16), 16)
                 codes.append(jnp.concatenate([high, low], axis=0).astype(jnp.float32))
-                at = samples * body + sample
-                note = chosen_ref[place, at : at + 1].astype(jnp.float32)
+                note = chosen_ref[place, samples * body, sample : sample + 1].astype(jnp.float32)
                 logs.append(turn(note, 0) * (1.0 / LSE_ONE))
                 scales.append(jnp.exp2(turn(note, per) - 15.0))
             peak = functools.reduce(jnp.maximum, logs)
@@ -348,19 +355,25 @@
         (dispatched, suffix_out, suffix_log)
     )
 
+    chunk = 8 * CAPE
     reply = pl.pallas_call(
-        functools.partial(prefix_kernel, 16 * CAPE),
-        out_shape=shape((engine_count, CAPE * per // 2 + 8, HD), jnp.int32),
+        functools.partial(prefix_kernel, chunk),
+        out_shape=shape((engine_count, CAPE * per // 8 + 1, 4, HD), jnp.int32),
         in_specs=[VMEM] * (1 + KVH),
         out_specs=VMEM,
-        compiler_params=params(32),
+        scratch_shapes=[
+            pltpu.VMEM((2, chunk * per, positions), jnp.float32),
+            pltpu.VMEM((2, chunk * per, positions), jnp.bfloat16),
+            pltpu.VMEM((KVH, chunk * per, HD), jnp.float32),
+        ],
+        compiler_params=params(28),
         name="prefix",
     )(dispatched.reshape(engine_count * CAPE, per, HD), *blocks)
     returned = lax.all_to_all(reply, "engine", split_axis=0, concat_axis=0, tiled=True)
 
     chosen = pl.pallas_call(
         functools.partial(select_kernel, samples),
-        out_shape=shape((seq_count, samples * per // 2 + 8, HD), jnp.int32),
+        out_shape=shape((seq_count, samples * per // 8 + 1, 4, HD), jnp.int32),
         in_specs=[SMEM, VMEM],
         out_specs=VMEM,
         compiler_params=params(4),

time: 86.8 us -> 85 us (0.979)
  Pallas kernels: 19.7 us -> 18.8 us
  blocking collectives: 29.9 us -> 29 us
where the time goes in v4:
time: 85 us; the launch traced here: 84.5 us
  blocking collectives  29 us (34%)
  starting transfers between devices  19.1 us (22%)
  Pallas kernels  18.8 us (22%)
  waiting for transfers between devices  11.4 us (13%)
  local copies, waits for them, and re-layouts  5.93 us (7%)
    all_to_all x1, blocking collectives, local(): lax.all_to_all(chosen, 'seq', split_axis=0, concat_axis=0, tiled=True)  16.9 us
    all_to_all x1, blocking collectives, local(): lax.all_to_all(reply, 'engine', split_axis=0, concat_axis=0, tiled=True)  12.1 us
    pallas_call x1, Pallas kernels, local(): pl.pallas_call(functools.partial(prefix_kernel, chunk), out_shape=shape((...  10.2 us
    all_to_all x1, starting transfers between devices, local(): lax.all_to_all(payload, 'seq', split_axis=0, concat_axis=0, tiled=True)  9.98 us
    all_to_all x1, starting transfers between devices, local(): lax.all_to_all(packed, 'engine', split_axis=0, concat_axis=0, tiled=True)  6.89 us
    all_to_all x1, waiting for transfers between devices, local(): lax.all_to_all(payload, 'seq', split_axis=0, concat_axis=0, tiled=True)  6.31 us
    unnamed x24, local copies, waits for them, and re-layouts  5.18 us
    all_to_all x1, waiting for transfers between devices, local(): lax.all_to_all(packed, 'engine', split_axis=0, concat_axis=0, tiled=True)  5.13 us
  transfers between devices with their start and end apart: 5, of which 2 were waited for; matrix products, arithmetic and copies ran while one was open for 1% of the time, Pallas kernels for 6%

profile of v4, /device:TPU:1, one launch (start us, length us, event | category | flops | bytes accessed | tf_op | source)
XLA Modules:
  0.0 84.5 jit_solution(15064548112767473317)
XLA Ops:
  0.0 1.6 %prepare.1 = (bf16[2,128,128]{2,1,0:T(8,128)(2,1)}, bf16[16,72,128]{2,1,0:T(8,128)(2,1)}) custom-call(s32[2]{0:T(128)} %bitcast.4, bf16[2,4,4096]{2,1,0:T(4,128)(2,1)} %queries_ref.1), custom_call_target="tpu_custom_call" | custom-call | tf_op jit(solution)/shard_map/prepare/pallas_call | solution.py:308
  1.6 10.0 %all-to-all-start = ((bf16[16,72,128]{2,1,0:T(8,128)(2,1)}), bf16[16,72,128]{2,1,0:T(8,128)(2,1)S(1)}, u32[]{:S(2)}, u32[]{:S(2)}) async-start(bf16[16,72,128]{2,1,0:T(8,128)(2,1)} %get-tuple-element.18), calls=%async_computation | async-start | bytes 589824 | tf_op jit(solution)/shard_map/all_to_all | solution.py:318
  11.6 0.0 copy-start
  11.6 1.2 %copy-done = bf16[1,1024,512]{2,1,0:T(8,128)(2,1)S(1)} copy-done((bf16[1,1024,512]{2,1,0:T(8,128)(2,1)S(1)}, bf16[1,1024,512]{2,1,0:T(8,128)(2,1)}, u32[]{:S(2)}) %copy-start) | copy-done | bytes 1048600
  12.8 0.0 copy-start.1
  12.8 1.2 %copy-done.1 = bf16[1,1024,512]{2,1,0:T(8,128)(2,1)S(1)} copy-done((bf16[1,1024,512]{2,1,0:T(8,128)(2,1)S(1)}, bf16[1,1024,512]{2,1,0:T(8,128)(2,1)}, u32[]{:S(2)}) %copy-start.1) | copy-done | bytes 1048600
  14.1 0.0 copy-start.3
  14.1 1.6 %split.1 = (bf16[2,1024,128]{2,1,0:T(8,128)(2,1)S(1)}, bf16[2,1024,128]{2,1,0:T(8,128)(2,1)}, bf16[2,1024,128]{2,1,0:T(8,128)(2,1)}, bf16[2,1024,128]{2,1,0:T(8,128)(2,1)}) custom-call(s32[1]{0:T(128)} %bitcast.2.head_ref, bf16[1,1024,512]{2,1,0:T(8,128)(2,1)S(1)} %copy-done, bf16[1,1024,512]{2,1,0:T(8,128)(2,1)S(1)} %copy-done.1), custom_call_target="tpu_custom_call" | custom-call | tf_op jit(solution)/shard_map/split/pallas_call | solution.py:283
  15.7 0.0 copy-start.2
  15.7 0.2 collective-permute-start
  15.9 1.6 %collective-permute-start.1 = (bf16[2,1024,128]{2,1,0:T(8,128)(2,1)}, bf16[2,1024,128]{2,1,0:T(8,128)(2,1)}, u32[]{:S(2)}, u32[]{:S(2)}) collective-permute-start(bf16[2,1024,128]{2,1,0:T(8,128)(2,1)} %get-tuple-element.27), channel_id=1, source_target_pairs={{0,14},{1,3},{2,0},{3,5},{4,2},{5,7},{6,4},{7,9},{8,6},{9,11},{10,... | collective-permute-start | bytes 1572872 | tf_op jit(solution)/shard_map/ppermute | solution.py:299
  17.5 0.4 collective-permute-start.2
  17.9 6.3 %all-to-all-done.received_ref = bf16[16,72,128]{2,1,0:T(8,128)(2,1)S(1)} async-done(((bf16[16,72,128]{2,1,0:T(8,128)(2,1)}), bf16[16,72,128]{2,1,0:T(8,128)(2,1)S(1)}, u32[]{:S(2)}, u32[]{:S(2)}) %all-to-all-start) | async-done | bytes 294944 | tf_op jit(solution)/shard_map/all_to_all | solution.py:318
  24.2 0.8 %pack.1 = (bf16[16,96,128]{2,1,0:T(8,128)(2,1)S(1)}, s32[32]{0:T(128)S(1)}) custom-call(bf16[16,72,128]{2,1,0:T(8,128)(2,1)S(1)} %all-to-all-done.received_ref), custom_call_target="tpu_custom_call" | custom-call | tf_op jit(solution)/shard_map/pack/pallas_call | solution.py:340
  25.1 0.0 copy-start.4
  25.1 0.8 copy-done.4
  25.8 0.0 copy-start.11
  25.8 6.9 %all-to-all-start.1 = ((bf16[16,96,128]{2,1,0:T(8,128)(2,1)}), bf16[16,96,128]{2,1,0:T(8,128)(2,1)S(1)}, u32[]{:S(2)}, u32[]{:S(2)}) async-start(bf16[16,96,128]{2,1,0:T(8,128)(2,1)} %copy-done.4), calls=%async_computation.1 | async-start | bytes 786432 | tf_op jit(solution)/shard_map/all_to_all | solution.py:352
  32.7 0.0 copy-done.11
  32.8 0.0 copy-start.9
  32.8 0.7 pad.8.fresh_v_ref
  33.5 0.0 copy-start.10
  33.5 0.0 copy-done.3
  33.5 0.0 copy-done.2
  33.5 0.1 copy-done.9
  33.6 0.6 copy-done.10
  34.2 2.7 %suffix.1 = (f32[2,128,128]{2,1,0:T(8,128)S(1)}, f32[2,128,128]{2,1,0:T(8,128)S(1)}) custom-call(s32[2]{0:T(128)S(1)} %copy-done.10, bf16[2,128,128]{2,1,0:T(8,128)(2,1)S(1)} %copy-done.9, bf16[2,16,512]{2,1,0:T(8,128)(2,1)S(1)} %pad.7.fresh_k_ref, bf16[2,16,512]{2,1,0:T(8,128)(2,1)S(1)} %pad.8.fresh_v_ref, bf16[2,512,512]{2,1,0:T(8,128)(2,1)S(1)} %copy-done.2, ...), custom_call_target="tpu_custom_call" | custom-call | tf_op jit(solution)/shard_map/suffix/pallas_call | solution.py:321
  36.9 0.0 copy-start.5
  36.9 0.7 copy-done.5
  37.6 0.0 copy-start.7
  37.6 0.6 copy-done.7
  38.2 5.1 %all-to-all-done.1 = bf16[16,96,128]{2,1,0:T(8,128)(2,1)S(1)} async-done(((bf16[16,96,128]{2,1,0:T(8,128)(2,1)}), bf16[16,96,128]{2,1,0:T(8,128)(2,1)S(1)}, u32[]{:S(2)}, u32[]{:S(2)}) %all-to-all-start.1) | async-done | bytes 393248 | tf_op jit(solution)/shard_map/all_to_all | solution.py:352
  43.4 0.0 collective-permute-done.refs_1_
  43.4 0.0 collective-permute-done.1.refs_2_
  43.4 0.0 collective-permute-done.2.refs_3_
  43.4 10.2 %prefix.1 = s32[16,13,4,128]{3,2,1,0:T(4,128)S(1)} custom-call(bf16[48,32,128]{2,1,0:T(8,128)(2,1)S(1)} %bitcast.3, bf16[2,1024,128]{2,1,0:T(8,128)(2,1)S(1)} %get-tuple-element.25.refs_0_, bf16[2,1024,128]{2,1,0:T(8,128)(2,1)S(1)} %collective-permute-done.refs_1_, bf16[2,1024,128]{2,1,0:T(8,128)(2,1)} %collective-permute-done.1.refs_2_, ...), custom_call_target="tpu_custom_call" | custom-call | tf_op jit(solution)/shard_map/prefix/pallas_call | solution.py:359
  53.6 12.1 %all_to_all.20.reply_ref = s32[16,13,4,128]{3,2,1,0:T(4,128)S(1)} all-to-all(s32[16,13,4,128]{3,2,1,0:T(4,128)S(1)} %prefix.1), channel_id=1, replica_groups=mesh['engine'=16,'seq'=16] {'engine'}, dimensions={0} | all-to-all | bytes 851968 | tf_op jit(solution)/shard_map/all_to_all | solution.py:372
  65.8 0.6 select.5
  66.4 0.0 copy-start.6
  66.4 0.0 copy-start.8
  66.4 16.9 %all_to_all.21.chosen_ref = s32[16,9,4,128]{3,2,1,0:T(4,128)S(1)} all-to-all(s32[16,9,4,128]{3,2,1,0:T(4,128)S(1)} %select.5), channel_id=1, replica_groups=mesh['engine'=16,'seq'=16] {'seq'}, dimensions={0} | all-to-all | bytes 589824 | tf_op jit(solution)/shard_map/all_to_all | solution.py:382
  83.3 0.0 copy-done.6
  83.3 0.0 copy-done.8
  83.3 1.1 %combine.1 = bf16[2,4,4096]{2,1,0:T(4,128)(2,1)} custom-call(s32[16,9,4,128]{3,2,1,0:T(4,128)S(1)} %all_to_all.21.chosen_ref, f32[2,128,128]{2,1,0:T(8,128)S(1)} %copy-done.6, f32[2,128,128]{2,1,0:T(8,128)S(1)} %copy-done.8), custom_call_target="tpu_custom_call" | custom-call | tf_op jit(solution)/shard_map/combine/pallas_call | solution.py:384
  (1 shorter events, 0.0 us)
Async XLA Ops:
  1.6 22.6 %all-to-all-start = ((bf16[16,72,128]{2,1,0:T(8,128)(2,1)}), bf16[16,72,128]{2,1,0:T(8,128)(2,1)S(1)}, u32[]{:S(2)}, u32[]{:S(2)}) async-start(bf16[16,72,128]{2,1,0:T(8,128)(2,1)} %get-tuple-element.18), calls=%async_computation | async-start | bytes 589824 | tf_op jit(solution)/shard_map/all_to_all | solution.py:318
  11.6 1.2 %copy-start = (bf16[1,1024,512]{2,1,0:T(8,128)(2,1)S(1)}, bf16[1,1024,512]{2,1,0:T(8,128)(2,1)}, u32[]{:S(2)}) copy-start(bf16[1,1024,512]{2,1,0:T(8,128)(2,1)} %k_ref.3) | copy-start | bytes 3145732
  12.8 1.2 %copy-start.1 = (bf16[1,1024,512]{2,1,0:T(8,128)(2,1)S(1)}, bf16[1,1024,512]{2,1,0:T(8,128)(2,1)}, u32[]{:S(2)}) copy-start(bf16[1,1024,512]{2,1,0:T(8,128)(2,1)} %v_ref.3) | copy-start | bytes 3145732
  14.1 19.5 %copy-start.3 = (bf16[2,512,512]{2,1,0:T(8,128)(2,1)S(1)}, bf16[2,512,512]{2,1,0:T(8,128)(2,1)}, u32[]{:S(2)}) copy-start(bf16[2,512,512]{2,1,0:T(8,128)(2,1)} %v_ref.2) | copy-start | bytes 3145732
  15.7 17.8 %copy-start.2 = (bf16[2,512,512]{2,1,0:T(8,128)(2,1)S(1)}, bf16[2,512,512]{2,1,0:T(8,128)(2,1)}, u32[]{:S(2)}) copy-start(bf16[2,512,512]{2,1,0:T(8,128)(2,1)} %k_ref.2) | copy-start | bytes 3145732
  15.7 27.7 %collective-permute-start = (bf16[2,1024,128]{2,1,0:T(8,128)(2,1)}, bf16[2,1024,128]{2,1,0:T(8,128)(2,1)S(1)}, u32[]{:S(2)}, u32[]{:S(2)}) collective-permute-start(bf16[2,1024,128]{2,1,0:T(8,128)(2,1)} %get-tuple-element.26), channel_id=1, source_target_pairs={{0,1},{1,0},{2,3},{3,2},{4,5},{5,4},{6,7},{7,6},{8,9},{9,8},{10,11... | collective-permute-start | bytes 1572872 | tf_op jit(solution)/shard_map/ppermute | solution.py:299
  15.9 27.5 %collective-permute-start.1 = (bf16[2,1024,128]{2,1,0:T(8,128)(2,1)}, bf16[2,1024,128]{2,1,0:T(8,128)(2,1)}, u32[]{:S(2)}, u32[]{:S(2)}) collective-permute-start(bf16[2,1024,128]{2,1,0:T(8,128)(2,1)} %get-tuple-element.27), channel_id=1, source_target_pairs={{0,14},{1,3},{2,0},{3,5},{4,2},{5,7},{6,4},{7,9},{8,6},{9,11},{10,... | collective-permute-start | bytes 1572872 | tf_op jit(solution)/shard_map/ppermute | solution.py:299
  17.5 25.9 %collective-permute-start.2 = (bf16[2,1024,128]{2,1,0:T(8,128)(2,1)}, bf16[2,1024,128]{2,1,0:T(8,128)(2,1)}, u32[]{:S(2)}, u32[]{:S(2)}) collective-permute-start(bf16[2,1024,128]{2,1,0:T(8,128)(2,1)} %get-tuple-element.28), channel_id=1, source_target_pairs={{0,15},{1,2},{2,1},{3,4},{4,3},{5,6},{6,5},{7,8},{8,7},{9,10},{10,... | collective-permute-start | bytes 1572872 | tf_op jit(solution)/shard_map/ppermute | solution.py:299
  25.1 0.8 copy-start.4
  25.8 6.9 %copy-start.11 = (bf16[2,4,512]{2,1,0:T(4,128)(2,1)S(1)}, bf16[2,4,512]{2,1,0:T(4,128)(2,1)}, u32[]{:S(2)}) copy-start(bf16[2,4,512]{2,1,0:T(4,128)(2,1)} %param.10) | copy-start | bytes 24580
  25.8 17.5 %all-to-all-start.1 = ((bf16[16,96,128]{2,1,0:T(8,128)(2,1)}), bf16[16,96,128]{2,1,0:T(8,128)(2,1)S(1)}, u32[]{:S(2)}, u32[]{:S(2)}) async-start(bf16[16,96,128]{2,1,0:T(8,128)(2,1)} %copy-done.4), calls=%async_computation.1 | async-start | bytes 786432 | tf_op jit(solution)/shard_map/all_to_all | solution.py:352
  32.8 0.8 copy-start.9
  33.5 0.7 copy-start.10
  36.9 0.7 copy-start.5
  37.6 0.6 copy-start.7
  66.4 16.9 %copy-start.6 = (f32[2,128,128]{2,1,0:T(8,128)S(1)}, f32[2,128,128]{2,1,0:T(8,128)}, u32[]{:S(2)}) copy-start(f32[2,128,128]{2,1,0:T(8,128)} %copy-done.5) | copy-start | bytes 393220
  66.4 16.9 %copy-start.8 = (f32[2,128,128]{2,1,0:T(8,128)S(1)}, f32[2,128,128]{2,1,0:T(8,128)}, u32[]{:S(2)}) copy-start(f32[2,128,128]{2,1,0:T(8,128)} %copy-done.7) | copy-start | bytes 393220

commit v5 on v3

--- a/solution.py
+++ b/solution.py
@@ -89,16 +89,8 @@
             ]
 
 
-def block_scores(rows, keys):
+def scores(rows, keys):
     return lax.dot_general(rows, keys, (((1,), (1,)), ((), ())), preferred_element_type=jnp.float32)
-
-
-def block_attention(raw, values):
-    top = jnp.max(raw, axis=1, keepdims=True)
-    probs = jnp.exp2(raw * (SCALING * LOG2E) - top * (SCALING * LOG2E))
-    total = jnp.sum(probs, axis=1, keepdims=True)
-    acc = jnp.dot(probs.astype(jnp.bfloat16), values, preferred_element_type=jnp.float32)
-    return acc, top, total
 
 
 def encode(out):
@@ -112,54 +104,68 @@
     blocks, reply_ref = refs[:-1], refs[-1]
     slots, per = q_ref.shape[0], q_ref.shape[1]
     rows_of = per // 2
-    body = CAPE * rows_of
-
-    def step(index, _):
-        rows = q_ref[pl.ds(index * chunk, chunk)].reshape(chunk * per, HD)
-        parts, raw = [], block_scores(rows, blocks[0][0])
-        for place, block in enumerate(blocks):
-            ready = raw
-            if place + 1 < len(blocks):
-                raw = block_scores(rows, blocks[place + 1][0])
-            parts.append(block_attention(ready, block[1]))
+    row = lax.broadcasted_iota(jnp.int32, (chunk, per, HD), 1)
+    lane = lax.broadcasted_iota(jnp.int32, (chunk, per, HD), 2)
+
+    def attention(raw, values):
+        top = jnp.max(raw, axis=1, keepdims=True)
+        probs = jnp.exp2((raw - top) * (SCALING * LOG2E))
+        total = jnp.sum(probs, axis=1, keepdims=True)
+        acc = jnp.dot(probs.astype(jnp.bfloat16), values, preferred_element_type=jnp.float32)
+        return acc, top, total
+
+    def finish(first, parts):
         top = functools.reduce(jnp.maximum, [part[1] for part in parts])
         weights = [jnp.exp2((part[1] - top) * (SCALING * LOG2E)) for part in parts]
         total = functools.reduce(jnp.add, [w * part[2] for w, part in zip(weights, parts)])
         share = 1.0 / total
         out = functools.reduce(jnp.add, [(w * share) * part[0] for w, part in zip(weights, parts)])
-        log = top * SCALING + jnp.log(total)
+        log = jnp.round((top * SCALING + jnp.log(total)) * LSE_ONE).astype(jnp.int32)
         code, power = encode(out)
         code = code.reshape(chunk, per, HD)
         packed = jnp.bitwise_or(
             jnp.left_shift(code[:, :rows_of], 16), jnp.bitwise_and(code[:, rows_of:], 0xFFFF)
         )
-        row = lax.broadcasted_iota(jnp.int32, (chunk, per, HD), 1)
-        lane = lax.broadcasted_iota(jnp.int32, (chunk, per, HD), 2)
-        log = jnp.round(log * LSE_ONE).astype(jnp.int32).reshape(chunk, per, 1)
-        note = jnp.where(lane == row, log, 0)
+        note = jnp.where(lane == row, log.reshape(chunk, per, 1), 0)
         note = jnp.where(lane == row + per, power.reshape(chunk, per, 1), note)
         note = jnp.sum(note, axis=1)
-        for part in range(chunk // CAPE):
-            dest = index * (chunk // CAPE) + part
-            here = slice(part * CAPE, (part + 1) * CAPE)
-            reply_ref[dest, 0:body] = packed[here].reshape(body, HD)
-            reply_ref[dest, body : body + CAPE] = note[here]
-        return 0
-
-    lax.fori_loop(0, slots // chunk, step, 0)
+        for slot in range(chunk):
+            dest, rank = (first + slot) // CAPE, (first + slot) % CAPE
+            for part in range(rows_of // 4):
+                reply_ref[dest, rank * (rows_of // 4) + part] = packed[
+                    slot, part * 4 : part * 4 + 4
+                ]
+            reply_ref[dest, CAPE * (rows_of // 4), rank : rank + 1] = note[slot : slot + 1]
+
+    stages = [(first, place) for first in range(0, slots, chunk) for place in range(len(blocks))]
+    rows = {
+        first: q_ref[first : first + chunk].reshape(chunk * per, HD)
+        for first in range(0, slots, chunk)
+    }
+    raw, parts = scores(rows[0], blocks[0][0]), []
+    for number, (first, place) in enumerate(stages):
+        ready = raw
+        if number + 1 < len(stages):
+            later, block = stages[number + 1]
+            raw = scores(rows[later], blocks[block][0])
+        parts.append(attention(ready, blocks[place][1]))
+        if place + 1 == len(blocks):
+            finish(first, parts)
+            parts = []
 
 
 def select_kernel(samples, slots_ref, reply_ref, chosen_ref):
-    body = (chosen_ref.shape[1] - 8) // samples
+    body = (chosen_ref.shape[1] - 1) // samples
     for sample in range(chosen_ref.shape[0] * samples):
         slot = slots_ref[sample]
         prompt, rank = lax.shift_right_logical(slot, 2), lax.bitwise_and(slot, 3)
-        place, start = sample // samples, (sample % samples) * body
-        chosen_ref[place, start : start + body] = reply_ref[
-            prompt, pl.ds(pl.multiple_of(rank * body, body), body)
+        place, which = sample // samples, sample % samples
+        chosen_ref[place, which * body : (which + 1) * body] = reply_ref[
+            prompt, pl.ds(rank * body, body)
         ]
-        note = samples * body + sample % samples
-        chosen_ref[place, note : note + 1] = reply_ref[prompt, pl.ds(CAPE * body + rank, 1)]
+        chosen_ref[place, samples * body, which : which + 1] = reply_ref[
+            prompt, CAPE * body, pl.ds(rank, 1)
+        ]
 
 
 def suffix_kernel(length_ref, rows_ref, fresh_k_ref, fresh_v_ref, k_ref, v_ref, out_ref, log_ref):
@@ -209,8 +215,8 @@
 def combine_kernel(chosen_ref, suffix_out_ref, suffix_log_ref, out_ref):
     places, samples = chosen_ref.shape[0], suffix_out_ref.shape[0]
     steps = out_ref.shape[1]
-    body = (chosen_ref.shape[1] - 8) // samples
-    per = 2 * body
+    body = (chosen_ref.shape[1] - 1) // samples
+    per = 8 * body
     row = lax.broadcasted_iota(jnp.int32, (per, HD), 0)
     lane = lax.broadcasted_iota(jnp.int32, (per, HD), 1)
 
@@ -222,12 +228,13 @@
         for group in range(KVH):
             logs, scales, codes = [], [], []
             for place in range(group, places, KVH):
-                packed = chosen_ref[place, sample * body : (sample + 1) * body]
+                packed = jnp.concatenate(
+                    [chosen_ref[place, sample * body + part] for part in range(body)], axis=0
+                )
                 high = jnp.right_shift(packed, 16)
                 low = jnp.right_shift(jnp.left_shift(packed, 16), 16)
                 codes.append(jnp.concatenate([high, low], axis=0).astype(jnp.float32))
-                at = samples * body + sample
-                note = chosen_ref[place, at : at + 1].astype(jnp.float32)
+                note = chosen_ref[place, samples * body, sample : sample + 1].astype(jnp.float32)
                 logs.append(turn(note, 0) * (1.0 / LSE_ONE))
                 scales.append(jnp.exp2(turn(note, per) - 15.0))
             peak = functools.reduce(jnp.maximum, logs)
@@ -281,7 +288,11 @@
         scratch_shapes=[pltpu.SemaphoreType.DMA((KVH, 2))],
         compiler_params=params(4),
         name="split",
-    )(head_id, prefix_keys, prefix_values)
+    )(
+        head_id,
+        pltpu.with_memory_space_constraint(prefix_keys, pltpu.HBM),
+        pltpu.with_memory_space_constraint(prefix_values, pltpu.HBM),
+    )
 
     def swap(array, near, swapped):
         pairs = []
@@ -333,7 +344,7 @@
     packed, slots = pl.pallas_call(
         functools.partial(pack_kernel, samples),
         out_shape=(
-            shape((engine_count, CAPE * per, HD), jnp.bfloat16),
+            pltpu.HBM((engine_count, CAPE * per, HD), jnp.bfloat16),
             shape((seq_count * samples,), jnp.int32),
         ),
         in_specs=[VMEM],
@@ -348,19 +359,20 @@
         (dispatched, suffix_out, suffix_log)
     )
 
+    chunk = 4 * CAPE
     reply = pl.pallas_call(
-        functools.partial(prefix_kernel, 16 * CAPE),
-        out_shape=shape((engine_count, CAPE * per // 2 + 8, HD), jnp.int32),
+        functools.partial(prefix_kernel, chunk),
+        out_shape=shape((engine_count, CAPE * per // 8 + 1, 4, HD), jnp.int32),
         in_specs=[VMEM] * (1 + KVH),
         out_specs=VMEM,
-        compiler_params=params(32),
+        compiler_params=params(28),
         name="prefix",
     )(dispatched.reshape(engine_count * CAPE, per, HD), *blocks)
     returned = lax.all_to_all(reply, "engine", split_axis=0, concat_axis=0, tiled=True)
 
     chosen = pl.pallas_call(
         functools.partial(select_kernel, samples),
-        out_shape=shape((seq_count, samples * per // 2 + 8, HD), jnp.int32),
+        out_shape=shape((seq_count, samples * per // 8 + 1, 4, HD), jnp.int32),
         in_specs=[SMEM, VMEM],
         out_specs=VMEM,
         compiler_params=params(4),

time: 86.8 us -> 83.6 us (0.963)
  local copies, waits for them, and re-layouts: 5.93 us -> 2.71 us
  waiting for transfers between devices: 11.4 us -> 12.5 us
  blocking collectives: 29.9 us -> 29 us
    unnamed x24 -> x18, local copies, waits for them, and re-layouts: 5.18 us -> 1.97 us
    pallas_call x1, Pallas kernels: 1.61 us -> 2.88 us  [local(): pl.pallas_call(split_kernel, out_shape=[shape((2, positions, HD), jnp.bfl...]
    pallas_call x2, Pallas kernels: 11.9 us -> 10.8 us  [the longest x1 9.8 us: local(): pl.pallas_call(functools.partial(prefix_kernel, chunk), out_shape=shape((...]
    all_to_all x1, waiting for transfers between devices: 6.31 us -> 7.39 us  [local(): lax.all_to_all(payload, 'seq', split_axis=0, concat_axis=0, tiled=True)]
  transfers between devices with their start and end apart: 5 -> 5, of which waited for: 2 -> 2; matrix products, arithmetic and copies ran while one was open for 1% -> 1% of each run, Pallas kernels for 6% -> 8%
where the time goes in v5:
time: 83.6 us; the launch traced here: 83.1 us
  blocking collectives  29 us (35%)
  Pallas kernels  19.8 us (24%)
  starting transfers between devices  19 us (23%)
  waiting for transfers between devices  12.5 us (15%)
  local copies, waits for them, and re-layouts  2.71 us (3%)
    all_to_all x1, blocking collectives, local(): lax.all_to_all(chosen, 'seq', split_axis=0, concat_axis=0, tiled=True)  17 us
    all_to_all x1, blocking collectives, local(): lax.all_to_all(reply, 'engine', split_axis=0, concat_axis=0, tiled=True)  12 us
    all_to_all x1, starting transfers between devices, local(): lax.all_to_all(payload, 'seq', split_axis=0, concat_axis=0, tiled=True)  9.98 us
    pallas_call x1, Pallas kernels, local(): pl.pallas_call(functools.partial(prefix_kernel, chunk), out_shape=shape((...  9.8 us
    all_to_all x1, waiting for transfers between devices, local(): lax.all_to_all(payload, 'seq', split_axis=0, concat_axis=0, tiled=True)  7.39 us
    all_to_all x1, starting transfers between devices, local(): lax.all_to_all(packed, 'engine', split_axis=0, concat_axis=0, tiled=True)  6.77 us
    all_to_all x1, waiting for transfers between devices, local(): lax.all_to_all(packed, 'engine', split_axis=0, concat_axis=0, tiled=True)  5.05 us
    pallas_call x1, Pallas kernels, local(): pl.pallas_call(split_kernel, out_shape=[shape((2, positions, HD), jnp.bfl...  2.88 us
  transfers between devices with their start and end apart: 5, of which 2 were waited for; matrix products, arithmetic and copies ran while one was open for 1% of the time, Pallas kernels for 8%

profile of v5, /device:TPU:1, one launch (start us, length us, event | category | flops | bytes accessed | tf_op | source)
XLA Modules:
  0.0 83.1 jit_solution(9950538394553687697)
XLA Ops:
  0.0 1.6 %prepare.1 = (bf16[2,128,128]{2,1,0:T(8,128)(2,1)}, bf16[16,72,128]{2,1,0:T(8,128)(2,1)}) custom-call(s32[2]{0:T(128)} %bitcast.4, bf16[2,4,4096]{2,1,0:T(4,128)(2,1)} %queries_ref.1), custom_call_target="tpu_custom_call" | custom-call | tf_op jit(solution)/shard_map/prepare/pallas_call | solution.py:312
  1.6 10.0 %all-to-all-start = ((bf16[16,72,128]{2,1,0:T(8,128)(2,1)}), bf16[16,72,128]{2,1,0:T(8,128)(2,1)S(1)}, u32[]{:S(2)}, u32[]{:S(2)}) async-start(bf16[16,72,128]{2,1,0:T(8,128)(2,1)} %get-tuple-element.18), calls=%async_computation | async-start | bytes 589824 | tf_op jit(solution)/shard_map/all_to_all | solution.py:322
  11.6 0.0 copy-start.1
  11.6 2.9 %split.1 = (bf16[2,1024,128]{2,1,0:T(8,128)(2,1)S(1)}, bf16[2,1024,128]{2,1,0:T(8,128)(2,1)}, bf16[2,1024,128]{2,1,0:T(8,128)(2,1)}, bf16[2,1024,128]{2,1,0:T(8,128)(2,1)}) custom-call(s32[1]{0:T(128)} %bitcast.2.head_ref, bf16[1,1024,512]{2,1,0:T(8,128)(2,1)} %k_ref.3, bf16[1,1024,512]{2,1,0:T(8,128)(2,1)} %v_ref.3), custom_call_target="tpu_custom_call" | custom-call | tf_op jit(solution)/shard_map/split/pallas_call | solution.py:283
  14.5 0.0 copy-start
  14.5 0.2 collective-permute-start
  14.7 1.6 %collective-permute-start.1 = (bf16[2,1024,128]{2,1,0:T(8,128)(2,1)}, bf16[2,1024,128]{2,1,0:T(8,128)(2,1)}, u32[]{:S(2)}, u32[]{:S(2)}) collective-permute-start(bf16[2,1024,128]{2,1,0:T(8,128)(2,1)} %get-tuple-element.27), channel_id=1, source_target_pairs={{0,14},{1,3},{2,0},{3,5},{4,2},{5,7},{6,4},{7,9},{8,6},{9,11},{10,... | collective-permute-start | bytes 1572872 | tf_op jit(solution)/shard_map/ppermute | solution.py:303
  16.3 0.4 collective-permute-start.2
  16.7 7.4 %all-to-all-done.received_ref = bf16[16,72,128]{2,1,0:T(8,128)(2,1)S(1)} async-done(((bf16[16,72,128]{2,1,0:T(8,128)(2,1)}), bf16[16,72,128]{2,1,0:T(8,128)(2,1)S(1)}, u32[]{:S(2)}, u32[]{:S(2)}) %all-to-all-start) | async-done | bytes 294944 | tf_op jit(solution)/shard_map/all_to_all | solution.py:322
  24.1 1.0 %pack.1 = (bf16[16,96,128]{2,1,0:T(8,128)(2,1)}, s32[32]{0:T(128)S(1)}) custom-call(bf16[16,72,128]{2,1,0:T(8,128)(2,1)S(1)} %all-to-all-done.received_ref), custom_call_target="tpu_custom_call" | custom-call | tf_op jit(solution)/shard_map/pack/pallas_call | solution.py:344
  25.2 0.0 copy-start.8
  25.2 6.8 %all-to-all-start.1 = ((bf16[16,96,128]{2,1,0:T(8,128)(2,1)}), bf16[16,96,128]{2,1,0:T(8,128)(2,1)S(1)}, u32[]{:S(2)}, u32[]{:S(2)}) async-start(bf16[16,96,128]{2,1,0:T(8,128)(2,1)} %get-tuple-element.20), calls=%async_computation.1 | async-start | bytes 786432 | tf_op jit(solution)/shard_map/all_to_all | solution.py:356
  32.0 0.0 copy-done.8
  32.0 0.0 copy-start.6
  32.0 0.7 pad.8.fresh_v_ref
  32.7 0.0 copy-start.7
  32.7 0.0 copy-done.1
  32.7 0.0 copy-done
  32.7 0.1 copy-done.6
  32.8 0.6 copy-done.7
  33.4 2.7 %suffix.1 = (f32[2,128,128]{2,1,0:T(8,128)S(1)}, f32[2,128,128]{2,1,0:T(8,128)S(1)}) custom-call(s32[2]{0:T(128)S(1)} %copy-done.7, bf16[2,128,128]{2,1,0:T(8,128)(2,1)S(1)} %copy-done.6, bf16[2,16,512]{2,1,0:T(8,128)(2,1)S(1)} %pad.7.fresh_k_ref, bf16[2,16,512]{2,1,0:T(8,128)(2,1)S(1)} %pad.8.fresh_v_ref, bf16[2,512,512]{2,1,0:T(8,128)(2,1)S(1)} %copy-done, ...), custom_call_target="tpu_custom_call" | custom-call | tf_op jit(solution)/shard_map/suffix/pallas_call | solution.py:325
  36.1 0.0 copy-start.2
  36.2 0.6 copy-done.2
  36.8 0.0 copy-start.4
  36.8 0.6 copy-done.4
  37.4 5.1 %all-to-all-done.1 = bf16[16,96,128]{2,1,0:T(8,128)(2,1)S(1)} async-done(((bf16[16,96,128]{2,1,0:T(8,128)(2,1)}), bf16[16,96,128]{2,1,0:T(8,128)(2,1)S(1)}, u32[]{:S(2)}, u32[]{:S(2)}) %all-to-all-start.1) | async-done | bytes 393248 | tf_op jit(solution)/shard_map/all_to_all | solution.py:356
  42.5 0.0 collective-permute-done.refs_1_
  42.5 0.0 collective-permute-done.1.refs_2_
  42.5 0.0 collective-permute-done.2.refs_3_
  42.5 9.8 %prefix.1 = s32[16,13,4,128]{3,2,1,0:T(4,128)S(1)} custom-call(bf16[48,32,128]{2,1,0:T(8,128)(2,1)S(1)} %bitcast.3, bf16[2,1024,128]{2,1,0:T(8,128)(2,1)S(1)} %get-tuple-element.25.refs_0_, bf16[2,1024,128]{2,1,0:T(8,128)(2,1)S(1)} %collective-permute-done.refs_1_, bf16[2,1024,128]{2,1,0:T(8,128)(2,1)} %collective-permute-done.1.refs_2_, ...), custom_call_target="tpu_custom_call" | custom-call | tf_op jit(solution)/shard_map/prefix/pallas_call | solution.py:363
  52.3 12.0 %all_to_all.20.reply_ref = s32[16,13,4,128]{3,2,1,0:T(4,128)S(1)} all-to-all(s32[16,13,4,128]{3,2,1,0:T(4,128)S(1)} %prefix.1), channel_id=1, replica_groups=mesh['engine'=16,'seq'=16] {'engine'}, dimensions={0} | all-to-all | bytes 851968 | tf_op jit(solution)/shard_map/all_to_all | solution.py:371
  64.4 0.6 select.5
  65.0 0.0 copy-start.3
  65.0 0.0 copy-start.5
  65.0 17.0 %all_to_all.21.chosen_ref = s32[16,9,4,128]{3,2,1,0:T(4,128)S(1)} all-to-all(s32[16,9,4,128]{3,2,1,0:T(4,128)S(1)} %select.5), channel_id=1, replica_groups=mesh['engine'=16,'seq'=16] {'seq'}, dimensions={0} | all-to-all | bytes 589824 | tf_op jit(solution)/shard_map/all_to_all | solution.py:381
  82.0 0.0 copy-done.3
  82.0 0.0 copy-done.5
  82.0 1.1 %combine.1 = bf16[2,4,4096]{2,1,0:T(4,128)(2,1)} custom-call(s32[16,9,4,128]{3,2,1,0:T(4,128)S(1)} %all_to_all.21.chosen_ref, f32[2,128,128]{2,1,0:T(8,128)S(1)} %copy-done.3, f32[2,128,128]{2,1,0:T(8,128)S(1)} %copy-done.5), custom_call_target="tpu_custom_call" | custom-call | tf_op jit(solution)/shard_map/combine/pallas_call | solution.py:383
  (1 shorter events, 0.0 us)
Async XLA Ops:
  1.6 22.5 %all-to-all-start = ((bf16[16,72,128]{2,1,0:T(8,128)(2,1)}), bf16[16,72,128]{2,1,0:T(8,128)(2,1)S(1)}, u32[]{:S(2)}, u32[]{:S(2)}) async-start(bf16[16,72,128]{2,1,0:T(8,128)(2,1)} %get-tuple-element.18), calls=%async_computation | async-start | bytes 589824 | tf_op jit(solution)/shard_map/all_to_all | solution.py:322
  11.6 21.1 %copy-start.1 = (bf16[2,512,512]{2,1,0:T(8,128)(2,1)S(1)}, bf16[2,512,512]{2,1,0:T(8,128)(2,1)}, u32[]{:S(2)}) copy-start(bf16[2,512,512]{2,1,0:T(8,128)(2,1)} %v_ref.2) | copy-start | bytes 3145732
  14.5 18.2 %copy-start = (bf16[2,512,512]{2,1,0:T(8,128)(2,1)S(1)}, bf16[2,512,512]{2,1,0:T(8,128)(2,1)}, u32[]{:S(2)}) copy-start(bf16[2,512,512]{2,1,0:T(8,128)(2,1)} %k_ref.2) | copy-start | bytes 3145732
  14.5 28.0 %collective-permute-start = (bf16[2,1024,128]{2,1,0:T(8,128)(2,1)}, bf16[2,1024,128]{2,1,0:T(8,128)(2,1)S(1)}, u32[]{:S(2)}, u32[]{:S(2)}) collective-permute-start(bf16[2,1024,128]{2,1,0:T(8,128)(2,1)} %get-tuple-element.26), channel_id=1, source_target_pairs={{0,1},{1,0},{2,3},{3,2},{4,5},{5,4},{6,7},{7,6},{8,9},{9,8},{10,11... | collective-permute-start | bytes 1572872 | tf_op jit(solution)/shard_map/ppermute | solution.py:303
  14.7 27.8 %collective-permute-start.1 = (bf16[2,1024,128]{2,1,0:T(8,128)(2,1)}, bf16[2,1024,128]{2,1,0:T(8,128)(2,1)}, u32[]{:S(2)}, u32[]{:S(2)}) collective-permute-start(bf16[2,1024,128]{2,1,0:T(8,128)(2,1)} %get-tuple-element.27), channel_id=1, source_target_pairs={{0,14},{1,3},{2,0},{3,5},{4,2},{5,7},{6,4},{7,9},{8,6},{9,11},{10,... | collective-permute-start | bytes 1572872 | tf_op jit(solution)/shard_map/ppermute | solution.py:303
  16.3 26.2 %collective-permute-start.2 = (bf16[2,1024,128]{2,1,0:T(8,128)(2,1)}, bf16[2,1024,128]{2,1,0:T(8,128)(2,1)}, u32[]{:S(2)}, u32[]{:S(2)}) collective-permute-start(bf16[2,1024,128]{2,1,0:T(8,128)(2,1)} %get-tuple-element.28), channel_id=1, source_target_pairs={{0,15},{1,2},{2,1},{3,4},{4,3},{5,6},{6,5},{7,8},{8,7},{9,10},{10,... | collective-permute-start | bytes 1572872 | tf_op jit(solution)/shard_map/ppermute | solution.py:303
  25.2 6.8 %copy-start.8 = (bf16[2,4,512]{2,1,0:T(4,128)(2,1)S(1)}, bf16[2,4,512]{2,1,0:T(4,128)(2,1)}, u32[]{:S(2)}) copy-start(bf16[2,4,512]{2,1,0:T(4,128)(2,1)} %param.10) | copy-start | bytes 24580
  25.2 17.3 %all-to-all-start.1 = ((bf16[16,96,128]{2,1,0:T(8,128)(2,1)}), bf16[16,96,128]{2,1,0:T(8,128)(2,1)S(1)}, u32[]{:S(2)}, u32[]{:S(2)}) async-start(bf16[16,96,128]{2,1,0:T(8,128)(2,1)} %get-tuple-element.20), calls=%async_computation.1 | async-start | bytes 786432 | tf_op jit(solution)/shard_map/all_to_all | solution.py:356
  32.0 0.8 %copy-start.6 = (bf16[2,128,128]{2,1,0:T(8,128)(2,1)S(1)}, bf16[2,128,128]{2,1,0:T(8,128)(2,1)}, u32[]{:S(2)}) copy-start(bf16[2,128,128]{2,1,0:T(8,128)(2,1)} %get-tuple-element.21.rows_ref) | copy-start | bytes 196612
  32.7 0.7 copy-start.7
  36.1 0.7 copy-start.2
  36.8 0.7 copy-start.4
  65.0 17.0 %copy-start.3 = (f32[2,128,128]{2,1,0:T(8,128)S(1)}, f32[2,128,128]{2,1,0:T(8,128)}, u32[]{:S(2)}) copy-start(f32[2,128,128]{2,1,0:T(8,128)} %copy-done.2) | copy-start | bytes 393220
  65.0 17.0 %copy-start.5 = (f32[2,128,128]{2,1,0:T(8,128)S(1)}, f32[2,128,128]{2,1,0:T(8,128)}, u32[]{:S(2)}) copy-start(f32[2,128,128]{2,1,0:T(8,128)} %copy-done.4) | copy-start | bytes 393220

commit v6 on v3

--- a/solution.py
+++ b/solution.py
@@ -95,7 +95,7 @@
 
 def block_attention(raw, values):
     top = jnp.max(raw, axis=1, keepdims=True)
-    probs = jnp.exp2(raw * (SCALING * LOG2E) - top * (SCALING * LOG2E))
+    probs = jnp.exp2((raw - top) * (SCALING * LOG2E))
     total = jnp.sum(probs, axis=1, keepdims=True)
     acc = jnp.dot(probs.astype(jnp.bfloat16), values, preferred_element_type=jnp.float32)
     return acc, top, total
@@ -104,7 +104,7 @@
 def encode(out):
     largest = jnp.max(jnp.abs(out), axis=1, keepdims=True)
     power = jnp.floor(jnp.log2(jnp.maximum(largest, 2.0**-112) * 1.0001)) + 1.0
-    code = jnp.clip(jnp.round(out * jnp.exp2(15.0 - power)), -32767.0, 32767.0)
+    code = jnp.round(out * jnp.exp2(15.0 - power))
     return code.astype(jnp.int32), power.astype(jnp.int32)
 
 
@@ -164,7 +164,12 @@
 
 def suffix_kernel(length_ref, rows_ref, fresh_k_ref, fresh_v_ref, k_ref, v_ref, out_ref, log_ref):
     samples, positions = k_ref.shape[0], k_ref.shape[1]
-    fresh = fresh_k_ref.shape[1]
+    fresh = 16
+
+    def padded(array):
+        rest = jnp.zeros((fresh - array.shape[0], HD), jnp.float32)
+        return jnp.concatenate([array.astype(jnp.float32), rest], axis=0).astype(jnp.bfloat16)
+
     per = rows_ref.shape[1] // KVH
     steps = per // GROUP
     column = lax.broadcasted_iota(jnp.int32, (per, positions), 1)
@@ -180,7 +185,7 @@
                 rows, k_ref[sample, :, cols], dims, preferred_element_type=jnp.float32
             )
             fresh_raw = lax.dot_general(
-                rows, fresh_k_ref[sample, :, cols], dims, preferred_element_type=jnp.float32
+                rows, padded(fresh_k_ref[sample, :, cols]), dims, preferred_element_type=jnp.float32
             )
             cache_raw = jnp.where(live, cache_raw, -jnp.inf)
             fresh_raw = jnp.where(causal, fresh_raw, -jnp.inf)
@@ -198,7 +203,7 @@
                 preferred_element_type=jnp.float32,
             ) + jnp.dot(
                 fresh_probs.astype(jnp.bfloat16),
-                fresh_v_ref[sample, :, cols],
+                padded(fresh_v_ref[sample, :, cols]),
                 preferred_element_type=jnp.float32,
             )
             here = slice(group * per, (group + 1) * per)
@@ -281,7 +286,11 @@
         scratch_shapes=[pltpu.SemaphoreType.DMA((KVH, 2))],
         compiler_params=params(4),
         name="split",
-    )(head_id, prefix_keys, prefix_values)
+    )(
+        head_id,
+        pltpu.with_memory_space_constraint(prefix_keys, pltpu.HBM),
+        pltpu.with_memory_space_constraint(prefix_values, pltpu.HBM),
+    )
 
     def swap(array, near, swapped):
         pairs = []
@@ -310,7 +319,6 @@
     )(sample_prompt.reshape(samples), queries)
     received = lax.all_to_all(payload, "seq", split_axis=0, concat_axis=0, tiled=True)
 
-    fresh_pad = ((0, 0), (0, 16 - steps), (0, 0))
     suffix_out, suffix_log = pl.pallas_call(
         suffix_kernel,
         out_shape=(
@@ -324,8 +332,8 @@
     )(
         suffix_len,
         rows,
-        jnp.pad(new_keys, fresh_pad),
-        jnp.pad(new_values, fresh_pad),
+        new_keys,
+        new_values,
         suffix_keys,
         suffix_values,
     )
@@ -333,7 +341,7 @@
     packed, slots = pl.pallas_call(
         functools.partial(pack_kernel, samples),
         out_shape=(
-            shape((engine_count, CAPE * per, HD), jnp.bfloat16),
+            pltpu.HBM((engine_count, CAPE * per, HD), jnp.bfloat16),
             shape((seq_count * samples,), jnp.int32),
         ),
         in_specs=[VMEM],
@@ -349,11 +357,11 @@
     )
 
     reply = pl.pallas_call(
-        functools.partial(prefix_kernel, 16 * CAPE),
+        functools.partial(prefix_kernel, 8 * CAPE),
         out_shape=shape((engine_count, CAPE * per // 2 + 8, HD), jnp.int32),
         in_specs=[VMEM] * (1 + KVH),
         out_specs=VMEM,
-        compiler_params=params(32),
+        compiler_params=params(28),
         name="prefix",
     )(dispatched.reshape(engine_count * CAPE, per, HD), *blocks)
     returned = lax.all_to_all(reply, "engine", split_axis=0, concat_axis=0, tiled=True)

time: 86.8 us -> 86.4 us (level)
  local copies, waits for them, and re-layouts: 5.93 us -> 4.05 us
  waiting for transfers between devices: 11.4 us -> 12.4 us
    pallas_call x1, Pallas kernels: 1.61 us -> 2.88 us  [local(): pl.pallas_call(split_kernel, out_shape=[shape((2, positions, HD), jnp.bfl...]
    unnamed x24, local copies, waits for them, and re-layouts: 5.18 us -> 4.05 us
    all_to_all x1, waiting for transfers between devices: 6.31 us -> 7.39 us  [local(): lax.all_to_all(payload, 'seq', split_axis=0, concat_axis=0, tiled=True)]
  transfers between devices with their start and end apart: 5 -> 5, of which waited for: 2 -> 2; matrix products, arithmetic and copies ran while one was open for 1% -> 0% of each run, Pallas kernels for 6% -> 8%
where the time goes in v6:
time: 86.4 us; the launch traced here: 85.9 us
  blocking collectives  29.9 us (35%)
  Pallas kernels  20.3 us (23%)
  starting transfers between devices  19.1 us (22%)
  waiting for transfers between devices  12.4 us (14%)
  local copies, waits for them, and re-layouts  4.05 us (5%)
    all_to_all x1, blocking collectives, local(): lax.all_to_all(chosen, 'seq', split_axis=0, concat_axis=0, tiled=True)  17.6 us
    all_to_all x1, blocking collectives, local(): lax.all_to_all(reply, 'engine', split_axis=0, concat_axis=0, tiled=True)  12.4 us
    pallas_call x1, Pallas kernels, local(): pl.pallas_call(functools.partial(prefix_kernel, 8 * CAPE), out_shape=shap...  10.2 us
    all_to_all x1, starting transfers between devices, local(): lax.all_to_all(payload, 'seq', split_axis=0, concat_axis=0, tiled=True)  9.98 us
    all_to_all x1, waiting for transfers between devices, local(): lax.all_to_all(payload, 'seq', split_axis=0, concat_axis=0, tiled=True)  7.39 us
    all_to_all x1, starting transfers between devices, local(): lax.all_to_all(packed, 'engine', split_axis=0, concat_axis=0, tiled=True)  6.89 us
    all_to_all x1, waiting for transfers between devices, local(): lax.all_to_all(packed, 'engine', split_axis=0, concat_axis=0, tiled=True)  4.98 us
    unnamed x24, local copies, waits for them, and re-layouts  4.05 us
  transfers between devices with their start and end apart: 5, of which 2 were waited for; matrix products, arithmetic and copies ran while one was open for 0% of the time, Pallas kernels for 8%

profile of v6, /device:TPU:1, one launch (start us, length us, event | category | flops | bytes accessed | tf_op | source)
XLA Modules:
  0.0 85.9 jit_solution(6987229771675805635)
XLA Ops:
  0.0 1.6 %prepare.1 = (bf16[2,128,128]{2,1,0:T(8,128)(2,1)}, bf16[16,72,128]{2,1,0:T(8,128)(2,1)}) custom-call(s32[2]{0:T(128)} %bitcast.4, bf16[2,4,4096]{2,1,0:T(4,128)(2,1)} %queries_ref.1), custom_call_target="tpu_custom_call" | custom-call | tf_op jit(solution)/shard_map/prepare/pallas_call | solution.py:310
  1.6 10.0 %all-to-all-start = ((bf16[16,72,128]{2,1,0:T(8,128)(2,1)}), bf16[16,72,128]{2,1,0:T(8,128)(2,1)S(1)}, u32[]{:S(2)}, u32[]{:S(2)}) async-start(bf16[16,72,128]{2,1,0:T(8,128)(2,1)} %get-tuple-element.18), calls=%async_computation | async-start | bytes 589824 | tf_op jit(solution)/shard_map/all_to_all | solution.py:320
  11.6 0.0 copy-start.1
  11.6 2.9 %split.1 = (bf16[2,1024,128]{2,1,0:T(8,128)(2,1)S(1)}, bf16[2,1024,128]{2,1,0:T(8,128)(2,1)}, bf16[2,1024,128]{2,1,0:T(8,128)(2,1)}, bf16[2,1024,128]{2,1,0:T(8,128)(2,1)}) custom-call(s32[1]{0:T(128)} %bitcast.2.head_ref, bf16[1,1024,512]{2,1,0:T(8,128)(2,1)} %k_ref.3, bf16[1,1024,512]{2,1,0:T(8,128)(2,1)} %v_ref.3), custom_call_target="tpu_custom_call" | custom-call | tf_op jit(solution)/shard_map/split/pallas_call | solution.py:281
  14.5 0.0 copy-start
  14.5 0.2 collective-permute-start
  14.7 1.6 %collective-permute-start.1 = (bf16[2,1024,128]{2,1,0:T(8,128)(2,1)}, bf16[2,1024,128]{2,1,0:T(8,128)(2,1)}, u32[]{:S(2)}, u32[]{:S(2)}) collective-permute-start(bf16[2,1024,128]{2,1,0:T(8,128)(2,1)} %get-tuple-element.27), channel_id=1, source_target_pairs={{0,14},{1,3},{2,0},{3,5},{4,2},{5,7},{6,4},{7,9},{8,6},{9,11},{10,... | collective-permute-start | bytes 1572872 | tf_op jit(solution)/shard_map/ppermute | solution.py:301
  16.3 0.4 collective-permute-start.2
  16.7 7.4 %all-to-all-done.received_ref = bf16[16,72,128]{2,1,0:T(8,128)(2,1)S(1)} async-done(((bf16[16,72,128]{2,1,0:T(8,128)(2,1)}), bf16[16,72,128]{2,1,0:T(8,128)(2,1)S(1)}, u32[]{:S(2)}, u32[]{:S(2)}) %all-to-all-start) | async-done | bytes 294944 | tf_op jit(solution)/shard_map/all_to_all | solution.py:320
  24.1 1.0 %pack.1 = (bf16[16,96,128]{2,1,0:T(8,128)(2,1)}, s32[32]{0:T(128)S(1)}) custom-call(bf16[16,72,128]{2,1,0:T(8,128)(2,1)S(1)} %all-to-all-done.received_ref), custom_call_target="tpu_custom_call" | custom-call | tf_op jit(solution)/shard_map/pack/pallas_call | solution.py:341
  25.2 0.0 copy-start.10
  25.2 0.6 copy-done.10
  25.8 0.0 copy-start.7
  25.8 0.0 copy-start.8
  25.8 6.9 %all-to-all-start.1 = ((bf16[16,96,128]{2,1,0:T(8,128)(2,1)}), bf16[16,96,128]{2,1,0:T(8,128)(2,1)S(1)}, u32[]{:S(2)}, u32[]{:S(2)}) async-start(bf16[16,96,128]{2,1,0:T(8,128)(2,1)} %get-tuple-element.20), calls=%async_computation.1 | async-start | bytes 786432 | tf_op jit(solution)/shard_map/all_to_all | solution.py:353
  32.7 0.0 copy-start.9
  32.7 0.0 copy-done.1
  32.7 0.0 copy-done
  32.7 0.0 copy-done.7
  32.7 0.0 copy-done.8
  32.7 0.6 copy-done.9
  33.3 0.0 copy-start.6
  33.3 0.8 copy-done.6
  34.2 2.7 %suffix.1 = (f32[2,128,128]{2,1,0:T(8,128)S(1)}, f32[2,128,128]{2,1,0:T(8,128)S(1)}) custom-call(s32[2]{0:T(128)S(1)} %copy-done.9, bf16[2,128,128]{2,1,0:T(8,128)(2,1)S(1)} %copy-done.6, bf16[2,4,512]{2,1,0:T(4,128)(2,1)S(1)} %copy-done.7, bf16[2,4,512]{2,1,0:T(4,128)(2,1)S(1)} %copy-done.8, bf16[2,512,512]{2,1,0:T(8,128)(2,1)S(1)} %copy-done, ...), custom_call_target="tpu_custom_call" | custom-call | tf_op jit(solution)/shard_map/suffix/pallas_call | solution.py:322
  36.9 0.0 copy-start.2
  36.9 0.7 copy-done.2
  37.6 0.0 copy-start.4
  37.6 0.6 copy-done.4
  38.2 5.0 %all-to-all-done.1 = bf16[16,96,128]{2,1,0:T(8,128)(2,1)S(1)} async-done(((bf16[16,96,128]{2,1,0:T(8,128)(2,1)}), bf16[16,96,128]{2,1,0:T(8,128)(2,1)S(1)}, u32[]{:S(2)}, u32[]{:S(2)}) %all-to-all-start.1) | async-done | bytes 393248 | tf_op jit(solution)/shard_map/all_to_all | solution.py:353
  43.2 0.0 collective-permute-done.refs_1_
  43.2 0.0 collective-permute-done.1.refs_2_
  43.2 0.0 collective-permute-done.2.refs_3_
  43.2 10.2 %prefix.1 = s32[16,56,128]{2,1,0:T(8,128)S(1)} custom-call(bf16[48,32,128]{2,1,0:T(8,128)(2,1)S(1)} %bitcast.3, bf16[2,1024,128]{2,1,0:T(8,128)(2,1)S(1)} %get-tuple-element.25.refs_0_, bf16[2,1024,128]{2,1,0:T(8,128)(2,1)S(1)} %collective-permute-done.refs_1_, bf16[2,1024,128]{2,1,0:T(8,128)(2,1)} %collective-permute-done.1.refs_2_, ...), custom_call_target="tpu_custom_call" | custom-call | tf_op jit(solution)/shard_map/prefix/pallas_call | solution.py:359
  53.5 12.4 %all_to_all.20.reply_ref = s32[16,56,128]{2,1,0:T(8,128)S(1)} all-to-all(s32[16,56,128]{2,1,0:T(8,128)S(1)} %prefix.1), channel_id=1, replica_groups=mesh['engine'=16,'seq'=16] {'engine'}, dimensions={0} | all-to-all | bytes 917504 | tf_op jit(solution)/shard_map/all_to_all | solution.py:367
  65.9 0.0 copy-start.11
  65.9 0.7 copy-done.11
  66.5 0.6 select.3
  67.2 0.0 copy-start.3
  67.2 0.0 copy-start.5
  67.2 17.6 %all_to_all.21.chosen_ref = s32[16,40,128]{2,1,0:T(8,128)S(1)} all-to-all(s32[16,40,128]{2,1,0:T(8,128)S(1)} %select.3), channel_id=1, replica_groups=mesh['engine'=16,'seq'=16] {'seq'}, dimensions={0} | all-to-all | bytes 655360 | tf_op jit(solution)/shard_map/all_to_all | solution.py:377
  84.7 0.0 copy-done.3
  84.7 0.0 copy-done.5
  84.7 1.1 %combine.1 = bf16[2,4,4096]{2,1,0:T(4,128)(2,1)} custom-call(s32[16,40,128]{2,1,0:T(8,128)S(1)} %all_to_all.21.chosen_ref, f32[2,128,128]{2,1,0:T(8,128)S(1)} %copy-done.3, f32[2,128,128]{2,1,0:T(8,128)S(1)} %copy-done.5), custom_call_target="tpu_custom_call" | custom-call | tf_op jit(solution)/shard_map/combine/pallas_call | solution.py:379
Async XLA Ops:
  1.6 22.5 %all-to-all-start = ((bf16[16,72,128]{2,1,0:T(8,128)(2,1)}), bf16[16,72,128]{2,1,0:T(8,128)(2,1)S(1)}, u32[]{:S(2)}, u32[]{:S(2)}) async-start(bf16[16,72,128]{2,1,0:T(8,128)(2,1)} %get-tuple-element.18), calls=%async_computation | async-start | bytes 589824 | tf_op jit(solution)/shard_map/all_to_all | solution.py:320
  11.6 21.1 %copy-start.1 = (bf16[2,512,512]{2,1,0:T(8,128)(2,1)S(1)}, bf16[2,512,512]{2,1,0:T(8,128)(2,1)}, u32[]{:S(2)}) copy-start(bf16[2,512,512]{2,1,0:T(8,128)(2,1)} %v_ref.2) | copy-start | bytes 3145732
  14.5 18.2 %copy-start = (bf16[2,512,512]{2,1,0:T(8,128)(2,1)S(1)}, bf16[2,512,512]{2,1,0:T(8,128)(2,1)}, u32[]{:S(2)}) copy-start(bf16[2,512,512]{2,1,0:T(8,128)(2,1)} %k_ref.2) | copy-start | bytes 3145732
  14.5 28.7 %collective-permute-start = (bf16[2,1024,128]{2,1,0:T(8,128)(2,1)}, bf16[2,1024,128]{2,1,0:T(8,128)(2,1)S(1)}, u32[]{:S(2)}, u32[]{:S(2)}) collective-permute-start(bf16[2,1024,128]{2,1,0:T(8,128)(2,1)} %get-tuple-element.26), channel_id=1, source_target_pairs={{0,1},{1,0},{2,3},{3,2},{4,5},{5,4},{6,7},{7,6},{8,9},{9,8},{10,11... | collective-permute-start | bytes 1572872 | tf_op jit(solution)/shard_map/ppermute | solution.py:301
  14.7 28.5 %collective-permute-start.1 = (bf16[2,1024,128]{2,1,0:T(8,128)(2,1)}, bf16[2,1024,128]{2,1,0:T(8,128)(2,1)}, u32[]{:S(2)}, u32[]{:S(2)}) collective-permute-start(bf16[2,1024,128]{2,1,0:T(8,128)(2,1)} %get-tuple-element.27), channel_id=1, source_target_pairs={{0,14},{1,3},{2,0},{3,5},{4,2},{5,7},{6,4},{7,9},{8,6},{9,11},{10,... | collective-permute-start | bytes 1572872 | tf_op jit(solution)/shard_map/ppermute | solution.py:301
  16.3 26.9 %collective-permute-start.2 = (bf16[2,1024,128]{2,1,0:T(8,128)(2,1)}, bf16[2,1024,128]{2,1,0:T(8,128)(2,1)}, u32[]{:S(2)}, u32[]{:S(2)}) collective-permute-start(bf16[2,1024,128]{2,1,0:T(8,128)(2,1)} %get-tuple-element.28), channel_id=1, source_target_pairs={{0,15},{1,2},{2,1},{3,4},{4,3},{5,6},{6,5},{7,8},{8,7},{9,10},{10,... | collective-permute-start | bytes 1572872 | tf_op jit(solution)/shard_map/ppermute | solution.py:301
  25.2 0.6 copy-start.10
  25.8 6.9 %copy-start.7 = (bf16[2,4,512]{2,1,0:T(4,128)(2,1)S(1)}, bf16[2,4,512]{2,1,0:T(4,128)(2,1)}, u32[]{:S(2)}) copy-start(bf16[2,4,512]{2,1,0:T(4,128)(2,1)} %fresh_k_ref.1) | copy-start | bytes 24580
  25.8 6.9 %copy-start.8 = (bf16[2,4,512]{2,1,0:T(4,128)(2,1)S(1)}, bf16[2,4,512]{2,1,0:T(4,128)(2,1)}, u32[]{:S(2)}) copy-start(bf16[2,4,512]{2,1,0:T(4,128)(2,1)} %fresh_v_ref.1) | copy-start | bytes 24580
  25.8 17.4 %all-to-all-start.1 = ((bf16[16,96,128]{2,1,0:T(8,128)(2,1)}), bf16[16,96,128]{2,1,0:T(8,128)(2,1)S(1)}, u32[]{:S(2)}, u32[]{:S(2)}) async-start(bf16[16,96,128]{2,1,0:T(8,128)(2,1)} %get-tuple-element.20), calls=%async_computation.1 | async-start | bytes 786432 | tf_op jit(solution)/shard_map/all_to_all | solution.py:353
  32.7 0.7 copy-start.9
  33.3 0.8 copy-start.6
  36.9 0.7 copy-start.2
  37.6 0.6 copy-start.4
  65.9 0.7 copy-start.11
  67.2 17.6 %copy-start.3 = (f32[2,128,128]{2,1,0:T(8,128)S(1)}, f32[2,128,128]{2,1,0:T(8,128)}, u32[]{:S(2)}) copy-start(f32[2,128,128]{2,1,0:T(8,128)} %copy-done.2) | copy-start | bytes 393220
  67.2 17.6 %copy-start.5 = (f32[2,128,128]{2,1,0:T(8,128)S(1)}, f32[2,128,128]{2,1,0:T(8,128)}, u32[]{:S(2)}) copy-start(f32[2,128,128]{2,1,0:T(8,128)} %copy-done.4) | copy-start | bytes 393220

commit v7 on v6

--- a/solution.py
+++ b/solution.py
@@ -14,7 +14,6 @@
 CAPE = 3
 SCALING = HD ** (-0.5)
 LOG2E = math.log2(math.e)
-LN2 = math.log(2.0)
 LSE_ONE = float(2**20)
 VMEM = pl.BlockSpec(memory_space=pltpu.VMEM)
 SMEM = pl.BlockSpec(memory_space=pltpu.SMEM)
@@ -72,7 +71,7 @@
         copy.wait()
 
 
-def pack_kernel(samples, received_ref, packed_ref, slots_ref, counts_ref):
+def pack_kernel(samples, _, received_ref, packed_ref, slots_ref, counts_ref):
     prompts, part = packed_ref.shape[0], packed_ref.shape[1] // CAPE
     packed_ref[...] = jnp.zeros(packed_ref.shape, packed_ref.dtype)
     for prompt in range(prompts):
@@ -98,13 +97,13 @@
     probs = jnp.exp2((raw - top) * (SCALING * LOG2E))
     total = jnp.sum(probs, axis=1, keepdims=True)
     acc = jnp.dot(probs.astype(jnp.bfloat16), values, preferred_element_type=jnp.float32)
-    return acc, top, total
+    return acc, top * (SCALING * LOG2E), total
 
 
 def encode(out):
     largest = jnp.max(jnp.abs(out), axis=1, keepdims=True)
     power = jnp.floor(jnp.log2(jnp.maximum(largest, 2.0**-112) * 1.0001)) + 1.0
-    code = jnp.round(out * jnp.exp2(15.0 - power))
+    code = jnp.clip(jnp.round(out * jnp.exp2(15.0 - power)), -32767.0, 32767.0)
     return code.astype(jnp.int32), power.astype(jnp.int32)
 
 
@@ -112,7 +111,6 @@
     blocks, reply_ref = refs[:-1], refs[-1]
     slots, per = q_ref.shape[0], q_ref.shape[1]
     rows_of = per // 2
-    body = CAPE * rows_of
 
     def step(index, _):
         rows = q_ref[pl.ds(index * chunk, chunk)].reshape(chunk * per, HD)
@@ -123,11 +121,11 @@
                 raw = block_scores(rows, blocks[place + 1][0])
             parts.append(block_attention(ready, block[1]))
         top = functools.reduce(jnp.maximum, [part[1] for part in parts])
-        weights = [jnp.exp2((part[1] - top) * (SCALING * LOG2E)) for part in parts]
+        weights = [jnp.exp2(part[1] - top) for part in parts]
         total = functools.reduce(jnp.add, [w * part[2] for w, part in zip(weights, parts)])
         share = 1.0 / total
         out = functools.reduce(jnp.add, [(w * share) * part[0] for w, part in zip(weights, parts)])
-        log = top * SCALING + jnp.log(total)
+        log = top + jnp.log2(total)
         code, power = encode(out)
         code = code.reshape(chunk, per, HD)
         packed = jnp.bitwise_or(
@@ -139,27 +137,30 @@
         note = jnp.where(lane == row, log, 0)
         note = jnp.where(lane == row + per, power.reshape(chunk, per, 1), note)
         note = jnp.sum(note, axis=1)
-        for part in range(chunk // CAPE):
-            dest = index * (chunk // CAPE) + part
-            here = slice(part * CAPE, (part + 1) * CAPE)
-            reply_ref[dest, 0:body] = packed[here].reshape(body, HD)
-            reply_ref[dest, body : body + CAPE] = note[here]
+        for slot in range(chunk):
+            dest, rank = index * (chunk // CAPE) + slot // CAPE, slot % CAPE
+            for part in range(rows_of // 4):
+                reply_ref[dest, rank * (rows_of // 4) + part] = packed[
+                    slot, part * 4 : part * 4 + 4
+                ]
+            reply_ref[dest, CAPE * (rows_of // 4), rank : rank + 1] = note[slot : slot + 1]
         return 0
 
     lax.fori_loop(0, slots // chunk, step, 0)
 
 
 def select_kernel(samples, slots_ref, reply_ref, chosen_ref):
-    body = (chosen_ref.shape[1] - 8) // samples
+    body = (chosen_ref.shape[1] - 1) // samples
     for sample in range(chosen_ref.shape[0] * samples):
         slot = slots_ref[sample]
         prompt, rank = lax.shift_right_logical(slot, 2), lax.bitwise_and(slot, 3)
-        place, start = sample // samples, (sample % samples) * body
-        chosen_ref[place, start : start + body] = reply_ref[
-            prompt, pl.ds(pl.multiple_of(rank * body, body), body)
+        place, which = sample // samples, sample % samples
+        chosen_ref[place, which * body : (which + 1) * body] = reply_ref[
+            prompt, pl.ds(rank * body, body)
         ]
-        note = samples * body + sample % samples
-        chosen_ref[place, note : note + 1] = reply_ref[prompt, pl.ds(CAPE * body + rank, 1)]
+        chosen_ref[place, samples * body, which : which + 1] = reply_ref[
+            prompt, CAPE * body, pl.ds(rank, 1)
+        ]
 
 
 def suffix_kernel(length_ref, rows_ref, fresh_k_ref, fresh_v_ref, k_ref, v_ref, out_ref, log_ref):
@@ -208,14 +209,16 @@
             )
             here = slice(group * per, (group + 1) * per)
             out_ref[sample, here] = acc / total
-            log_ref[sample, here] = jnp.broadcast_to(top * SCALING + jnp.log(total), (per, HD))
+            log_ref[sample, here] = jnp.broadcast_to(
+                top * (SCALING * LOG2E) + jnp.log2(total), (per, HD)
+            )
 
 
 def combine_kernel(chosen_ref, suffix_out_ref, suffix_log_ref, out_ref):
     places, samples = chosen_ref.shape[0], suffix_out_ref.shape[0]
     steps = out_ref.shape[1]
-    body = (chosen_ref.shape[1] - 8) // samples
-    per = 2 * body
+    body = (chosen_ref.shape[1] - 1) // samples
+    per = 8 * body
     row = lax.broadcasted_iota(jnp.int32, (per, HD), 0)
     lane = lax.broadcasted_iota(jnp.int32, (per, HD), 1)
 
@@ -227,27 +230,28 @@
         for group in range(KVH):
             logs, scales, codes = [], [], []
             for place in range(group, places, KVH):
-                packed = chosen_ref[place, sample * body : (sample + 1) * body]
+                packed = jnp.concatenate(
+                    [chosen_ref[place, sample * body + part] for part in range(body)], axis=0
+                )
                 high = jnp.right_shift(packed, 16)
                 low = jnp.right_shift(jnp.left_shift(packed, 16), 16)
                 codes.append(jnp.concatenate([high, low], axis=0).astype(jnp.float32))
-                at = samples * body + sample
-                note = chosen_ref[place, at : at + 1].astype(jnp.float32)
+                note = chosen_ref[place, samples * body, sample : sample + 1].astype(jnp.float32)
                 logs.append(turn(note, 0) * (1.0 / LSE_ONE))
                 scales.append(jnp.exp2(turn(note, per) - 15.0))
             peak = functools.reduce(jnp.maximum, logs)
-            weights = [jnp.exp(log - peak) for log in logs]
+            weights = [jnp.exp2(log - peak) for log in logs]
             weight_sum = functools.reduce(jnp.add, weights)
             prefix = functools.reduce(
                 jnp.add, [(w * s) * c for w, s, c in zip(weights, scales, codes)]
             )
-            prefix_log = peak + jnp.log(weight_sum)
+            prefix_log = peak + jnp.log2(weight_sum)
             first = group * per
             suffix_log = suffix_log_ref[sample, first : first + per][:, 0:1]
             suffix = suffix_out_ref[sample, first : first + per]
             top = jnp.maximum(prefix_log, suffix_log)
-            prefix_weight = jnp.exp(prefix_log - top)
-            suffix_weight = jnp.exp(suffix_log - top)
+            prefix_weight = jnp.exp2(prefix_log - top)
+            suffix_weight = jnp.exp2(suffix_log - top)
             whole = prefix_weight + suffix_weight
             result = (prefix_weight / (weight_sum * whole)) * prefix + (
                 suffix_weight / whole
@@ -284,7 +288,7 @@
         in_specs=[SMEM] + [pl.BlockSpec(memory_space=pltpu.HBM)] * 2,
         out_specs=[VMEM] * KVH,
         scratch_shapes=[pltpu.SemaphoreType.DMA((KVH, 2))],
-        compiler_params=params(4),
+        compiler_params=params(16),
         name="split",
     )(
         head_id,
@@ -327,7 +331,7 @@
         ),
         in_specs=[SMEM] + [VMEM] * 5,
         out_specs=(VMEM, VMEM),
-        compiler_params=params(12),
+        compiler_params=params(16),
         name="suffix",
     )(
         suffix_len,
@@ -338,40 +342,58 @@
         suffix_values,
     )
 
+    suffix_out, suffix_log = pl.pallas_call(
+        suffix_kernel,
+        out_shape=(
+            shape((samples, heads * steps, HD), jnp.float32),
+            shape((samples, heads * steps, HD), jnp.float32),
+        ),
+        in_specs=[SMEM] + [VMEM] * 5,
+        out_specs=(VMEM, VMEM),
+        compiler_params=params(16),
+        name="suffix",
+    )(
+        suffix_len,
+        rows,
+        new_keys,
+        new_values,
+        suffix_keys,
+        suffix_values,
+    )
+
     packed, slots = pl.pallas_call(
         functools.partial(pack_kernel, samples),
         out_shape=(
             pltpu.HBM((engine_count, CAPE * per, HD), jnp.bfloat16),
             shape((seq_count * samples,), jnp.int32),
         ),
-        in_specs=[VMEM],
+        in_specs=[pl.BlockSpec(memory_space=pl.ANY), VMEM],
         out_specs=(VMEM, SMEM),
         scratch_shapes=[pltpu.SMEM((engine_count,), jnp.int32)],
-        compiler_params=params(4),
+        compiler_params=params(16),
         name="pack",
-    )(received)
+    )(suffix_log, received)
     dispatched = lax.all_to_all(packed, "engine", split_axis=0, concat_axis=0, tiled=True)
-
-    dispatched, suffix_out, suffix_log = lax.optimization_barrier(
-        (dispatched, suffix_out, suffix_log)
-    )
 
     reply = pl.pallas_call(
         functools.partial(prefix_kernel, 8 * CAPE),
-        out_shape=shape((engine_count, CAPE * per // 2 + 8, HD), jnp.int32),
+        out_shape=shape((engine_count, CAPE * per // 8 + 1, 4, HD), jnp.int32),
         in_specs=[VMEM] * (1 + KVH),
         out_specs=VMEM,
-        compiler_params=params(28),
+        compiler_params=params(16),
         name="prefix",
-    )(dispatched.reshape(engine_count * CAPE, per, HD), *blocks)
+    )(
+        dispatched.reshape(engine_count * CAPE, per, HD),
+        *[pltpu.with_memory_space_constraint(block, pltpu.VMEM) for block in blocks],
+    )
     returned = lax.all_to_all(reply, "engine", split_axis=0, concat_axis=0, tiled=True)
 
     chosen = pl.pallas_call(
         functools.partial(select_kernel, samples),
-        out_shape=shape((seq_count, samples * per // 2 + 8, HD), jnp.int32),
+        out_shape=shape((seq_count, samples * per // 8 + 1, 4, HD), jnp.int32),
         in_specs=[SMEM, VMEM],
         out_specs=VMEM,
-        compiler_params=params(4),
+        compiler_params=params(16),
         name="select",
     )(slots, returned)
     gathered = lax.all_to_all(chosen, "seq", split_axis=0, concat_axis=0, tiled=True)
@@ -381,7 +403,7 @@
         out_shape=shape((samples, steps, features), jnp.bfloat16),
         in_specs=[VMEM] * 3,
         out_specs=VMEM,
-        compiler_params=params(6),
+        compiler_params=params(16),
         name="combine",
     )(gathered, suffix_out, suffix_log)
 

time: 86.4 us -> 83.2 us (0.963)
  local copies, waits for them, and re-layouts: 4.05 us -> 0.03 us
  waiting for transfers between devices: 12.4 us -> 15.2 us
  blocking collectives: 29.9 us -> 28.9 us
  Pallas kernels: 20.3 us -> 19.4 us
    all_to_all x1, waiting for transfers between devices: 4.98 us -> 10.5 us  [local(): lax.all_to_all(packed, 'engine', split_axis=0, concat_axis=0, tiled=True)]
    unnamed x24 -> x12, local copies, waits for them, and re-layouts: 4.05 us -> 0.03 us
    all_to_all x1, waiting for transfers between devices: 7.39 us -> 4.72 us  [local(): lax.all_to_all(payload, 'seq', split_axis=0, concat_axis=0, tiled=True)]
where the time goes in v7:
time: 83.2 us; the launch traced here: 82.7 us
  blocking collectives  28.9 us (35%)
  Pallas kernels  19.4 us (23%)
  starting transfers between devices  19.1 us (23%)
  waiting for transfers between devices  15.2 us (18%)
    all_to_all x1, blocking collectives, local(): lax.all_to_all(chosen, 'seq', split_axis=0, concat_axis=0, tiled=True)  16.8 us
    all_to_all x1, blocking collectives, local(): lax.all_to_all(reply, 'engine', split_axis=0, concat_axis=0, tiled=True)  12 us
    all_to_all x1, waiting for transfers between devices, local(): lax.all_to_all(packed, 'engine', split_axis=0, concat_axis=0, tiled=True)  10.5 us
    all_to_all x1, starting transfers between devices, local(): lax.all_to_all(payload, 'seq', split_axis=0, concat_axis=0, tiled=True)  10.1 us
    pallas_call x1, Pallas kernels, local(): pl.pallas_call(functools.partial(prefix_kernel, 8 * CAPE), out_shape=shap...  9.46 us
    all_to_all x1, starting transfers between devices, local(): lax.all_to_all(packed, 'engine', split_axis=0, concat_axis=0, tiled=True)  6.77 us
    all_to_all x1, waiting for transfers between devices, local(): lax.all_to_all(payload, 'seq', split_axis=0, concat_axis=0, tiled=True)  4.72 us
    pallas_call x1, Pallas kernels, local(): pl.pallas_call(suffix_kernel, out_shape=(shape((samples, heads * steps, H...  2.75 us
  transfers between devices with their start and end apart: 5, of which 2 were waited for; matrix products, arithmetic and copies ran while one was open for 0% of the time, Pallas kernels for 8%

profile of v7, /device:TPU:1, one launch (start us, length us, event | category | flops | bytes accessed | tf_op | source)
XLA Modules:
  0.0 82.7 jit_solution(5935220163556331756)
XLA Ops:
  0.0 1.6 %prepare.1 = (bf16[2,128,128]{2,1,0:T(8,128)(2,1)}, bf16[16,72,128]{2,1,0:T(8,128)(2,1)}) custom-call(s32[2]{0:T(128)} %bitcast.4, bf16[2,4,4096]{2,1,0:T(4,128)(2,1)} %queries_ref.1), custom_call_target="tpu_custom_call" | custom-call | tf_op jit(solution)/shard_map/prepare/pallas_call | solution.py:314
  1.6 0.0 copy-start.2
  1.6 0.0 copy-start.4
  1.6 0.0 copy-start.5
  1.6 10.1 %all-to-all-start = ((bf16[16,72,128]{2,1,0:T(8,128)(2,1)}), bf16[16,72,128]{2,1,0:T(8,128)(2,1)S(1)}, u32[]{:S(2)}, u32[]{:S(2)}) async-start(bf16[16,72,128]{2,1,0:T(8,128)(2,1)} %get-tuple-element.17), calls=%async_computation | async-start | bytes 589824 | tf_op jit(solution)/shard_map/all_to_all | solution.py:324
  11.8 0.0 copy-start
  11.8 0.0 copy-start.1
  11.8 0.0 copy-start.3
  11.8 2.8 %split.1 = (bf16[2,1024,128]{2,1,0:T(8,128)(2,1)S(1)}, bf16[2,1024,128]{2,1,0:T(8,128)(2,1)}, bf16[2,1024,128]{2,1,0:T(8,128)(2,1)}, bf16[2,1024,128]{2,1,0:T(8,128)(2,1)S(1)}) custom-call(s32[1]{0:T(128)} %bitcast.2.head_ref, bf16[1,1024,512]{2,1,0:T(8,128)(2,1)} %k_ref.3, bf16[1,1024,512]{2,1,0:T(8,128)(2,1)} %v_ref.3), custom_call_target="tpu_custom_call" | custom-call | tf_op jit(solution)/shard_map/split/pallas_call | solution.py:285
  14.5 0.2 collective-permute-start
  14.7 1.6 %collective-permute-start.1 = (bf16[2,1024,128]{2,1,0:T(8,128)(2,1)}, bf16[2,1024,128]{2,1,0:T(8,128)(2,1)S(1)}, u32[]{:S(2)}, u32[]{:S(2)}) collective-permute-start(bf16[2,1024,128]{2,1,0:T(8,128)(2,1)} %get-tuple-element.22), channel_id=1, source_target_pairs={{0,14},{1,3},{2,0},{3,5},{4,2},{5,7},{6,4},{7,9},{8,6},{9,11},{10,... | collective-permute-start | bytes 1572872 | tf_op jit(solution)/shard_map/ppermute | solution.py:305
  16.4 0.4 collective-permute-start.2
  16.8 0.0 copy-done.2
  16.8 0.0 copy-done.4
  16.8 0.0 copy-done.5
  16.8 0.0 copy-done
  16.8 0.0 copy-done.1
  16.8 0.0 copy-done.3
  16.8 2.8 %suffix.1 = (f32[2,128,128]{2,1,0:T(8,128)S(1)}, f32[2,128,128]{2,1,0:T(8,128)S(1)}) custom-call(s32[2]{0:T(128)S(1)} %copy-done.5, bf16[2,128,128]{2,1,0:T(8,128)(2,1)S(1)} %copy-done.2, bf16[2,4,512]{2,1,0:T(4,128)(2,1)S(1)} %copy-done.3, bf16[2,4,512]{2,1,0:T(4,128)(2,1)S(1)} %copy-done.4, bf16[2,512,512]{2,1,0:T(8,128)(2,1)S(1)} %copy-done, ...), custom_call_target="tpu_custom_call" | custom-call | tf_op jit(solution)/shard_map/suffix/pallas_call | solution.py:345
  19.6 4.7 %all-to-all-done.received_ref = bf16[16,72,128]{2,1,0:T(8,128)(2,1)S(1)} async-done(((bf16[16,72,128]{2,1,0:T(8,128)(2,1)}), bf16[16,72,128]{2,1,0:T(8,128)(2,1)S(1)}, u32[]{:S(2)}, u32[]{:S(2)}) %all-to-all-start) | async-done | bytes 294944 | tf_op jit(solution)/shard_map/all_to_all | solution.py:324
  24.3 1.0 %pack.1 = (bf16[16,96,128]{2,1,0:T(8,128)(2,1)}, s32[32]{0:T(128)S(1)}) custom-call(f32[2,128,128]{2,1,0:T(8,128)S(1)} %get-tuple-element.16._.suffix_log_ref, bf16[16,72,128]{2,1,0:T(8,128)(2,1)S(1)} %all-to-all-done.received_ref), custom_call_target="tpu_custom_call" | custom-call | tf_op jit(solution)/shard_map/pack/pallas_call | solution.py:364
  25.3 6.8 %all-to-all-start.1 = ((bf16[16,96,128]{2,1,0:T(8,128)(2,1)}), bf16[16,96,128]{2,1,0:T(8,128)(2,1)S(1)}, u32[]{:S(2)}, u32[]{:S(2)}) async-start(bf16[16,96,128]{2,1,0:T(8,128)(2,1)} %get-tuple-element.19), calls=%async_computation.1 | async-start | bytes 786432 | tf_op jit(solution)/shard_map/all_to_all | solution.py:376
  32.1 0.0 collective-permute-done.refs_1_
  32.1 0.0 collective-permute-done.1.refs_2_
  32.1 0.0 collective-permute-done.2.refs_3_
  32.1 10.5 %all-to-all-done.1 = bf16[16,96,128]{2,1,0:T(8,128)(2,1)S(1)} async-done(((bf16[16,96,128]{2,1,0:T(8,128)(2,1)}), bf16[16,96,128]{2,1,0:T(8,128)(2,1)S(1)}, u32[]{:S(2)}, u32[]{:S(2)}) %all-to-all-start.1) | async-done | bytes 393248 | tf_op jit(solution)/shard_map/all_to_all | solution.py:376
  42.6 9.5 %prefix.1 = s32[16,13,4,128]{3,2,1,0:T(4,128)S(1)} custom-call(bf16[48,32,128]{2,1,0:T(8,128)(2,1)S(1)} %bitcast.3, bf16[2,1024,128]{2,1,0:T(8,128)(2,1)S(1)} %get-tuple-element.20.refs_0_, bf16[2,1024,128]{2,1,0:T(8,128)(2,1)S(1)} %collective-permute-done.refs_1_, bf16[2,1024,128]{2,1,0:T(8,128)(2,1)S(1)} %collective-permute-done.1.refs_2_, ...), custom_call_target="tpu_custom_call" | custom-call | tf_op jit(solution)/shard_map/prefix/pallas_call | solution.py:378
  52.1 12.0 %all_to_all.20.reply_ref = s32[16,13,4,128]{3,2,1,0:T(4,128)S(1)} all-to-all(s32[16,13,4,128]{3,2,1,0:T(4,128)S(1)} %prefix.1), channel_id=1, replica_groups=mesh['engine'=16,'seq'=16] {'engine'}, dimensions={0} | all-to-all | bytes 851968 | tf_op jit(solution)/shard_map/all_to_all | solution.py:389
  64.1 0.6 select.3
  64.8 16.8 %all_to_all.21.chosen_ref = s32[16,9,4,128]{3,2,1,0:T(4,128)S(1)} all-to-all(s32[16,9,4,128]{3,2,1,0:T(4,128)S(1)} %select.3), channel_id=1, replica_groups=mesh['engine'=16,'seq'=16] {'seq'}, dimensions={0} | all-to-all | bytes 589824 | tf_op jit(solution)/shard_map/all_to_all | solution.py:399
  81.6 1.1 %combine.1 = bf16[2,4,4096]{2,1,0:T(4,128)(2,1)} custom-call(s32[16,9,4,128]{3,2,1,0:T(4,128)S(1)} %all_to_all.21.chosen_ref, f32[2,128,128]{2,1,0:T(8,128)S(1)} %get-tuple-element.24.suffix_out_ref, f32[2,128,128]{2,1,0:T(8,128)S(1)} %get-tuple-element.16._.suffix_log_ref), custom_call_target="tpu_custom_call" | custom-call | tf_op jit(solution)/shard_map/combine/pallas_call | solution.py:401
Async XLA Ops:
  1.6 15.1 %copy-start.2 = (bf16[2,128,128]{2,1,0:T(8,128)(2,1)S(1)}, bf16[2,128,128]{2,1,0:T(8,128)(2,1)}, u32[]{:S(2)}) copy-start(bf16[2,128,128]{2,1,0:T(8,128)(2,1)} %get-tuple-element.15.rows_ref) | copy-start | bytes 196612
  1.6 15.1 %copy-start.4 = (bf16[2,4,512]{2,1,0:T(4,128)(2,1)S(1)}, bf16[2,4,512]{2,1,0:T(4,128)(2,1)}, u32[]{:S(2)}) copy-start(bf16[2,4,512]{2,1,0:T(4,128)(2,1)} %fresh_v_ref.1) | copy-start | bytes 24580
  1.6 15.2 %copy-start.5 = (s32[2]{0:T(128)S(1)}, s32[2]{0:T(128)}, u32[]{:S(2)}) copy-start(s32[2]{0:T(128)} %length_ref.1) | copy-start | bytes 28
  1.6 22.6 %all-to-all-start = ((bf16[16,72,128]{2,1,0:T(8,128)(2,1)}), bf16[16,72,128]{2,1,0:T(8,128)(2,1)S(1)}, u32[]{:S(2)}, u32[]{:S(2)}) async-start(bf16[16,72,128]{2,1,0:T(8,128)(2,1)} %get-tuple-element.17), calls=%async_computation | async-start | bytes 589824 | tf_op jit(solution)/shard_map/all_to_all | solution.py:324
  11.8 5.0 %copy-start = (bf16[2,512,512]{2,1,0:T(8,128)(2,1)S(1)}, bf16[2,512,512]{2,1,0:T(8,128)(2,1)}, u32[]{:S(2)}) copy-start(bf16[2,512,512]{2,1,0:T(8,128)(2,1)} %k_ref.2) | copy-start | bytes 3145732
  11.8 5.0 %copy-start.1 = (bf16[2,512,512]{2,1,0:T(8,128)(2,1)S(1)}, bf16[2,512,512]{2,1,0:T(8,128)(2,1)}, u32[]{:S(2)}) copy-start(bf16[2,512,512]{2,1,0:T(8,128)(2,1)} %v_ref.2) | copy-start | bytes 3145732
  11.8 5.0 %copy-start.3 = (bf16[2,4,512]{2,1,0:T(4,128)(2,1)S(1)}, bf16[2,4,512]{2,1,0:T(4,128)(2,1)}, u32[]{:S(2)}) copy-start(bf16[2,4,512]{2,1,0:T(4,128)(2,1)} %fresh_k_ref.1) | copy-start | bytes 24580
  14.5 17.5 %collective-permute-start = (bf16[2,1024,128]{2,1,0:T(8,128)(2,1)}, bf16[2,1024,128]{2,1,0:T(8,128)(2,1)S(1)}, u32[]{:S(2)}, u32[]{:S(2)}) collective-permute-start(bf16[2,1024,128]{2,1,0:T(8,128)(2,1)} %get-tuple-element.21), channel_id=1, source_target_pairs={{0,1},{1,0},{2,3},{3,2},{4,5},{5,4},{6,7},{7,6},{8,9},{9,8},{10,11... | collective-permute-start | bytes 1572872 | tf_op jit(solution)/shard_map/ppermute | solution.py:305
  14.7 17.4 %collective-permute-start.1 = (bf16[2,1024,128]{2,1,0:T(8,128)(2,1)}, bf16[2,1024,128]{2,1,0:T(8,128)(2,1)S(1)}, u32[]{:S(2)}, u32[]{:S(2)}) collective-permute-start(bf16[2,1024,128]{2,1,0:T(8,128)(2,1)} %get-tuple-element.22), channel_id=1, source_target_pairs={{0,14},{1,3},{2,0},{3,5},{4,2},{5,7},{6,4},{7,9},{8,6},{9,11},{10,... | collective-permute-start | bytes 1572872 | tf_op jit(solution)/shard_map/ppermute | solution.py:305
  16.4 15.8 %collective-permute-start.2 = (bf16[2,1024,128]{2,1,0:T(8,128)(2,1)S(1)}, bf16[2,1024,128]{2,1,0:T(8,128)(2,1)S(1)}, u32[]{:S(2)}, u32[]{:S(2)}) collective-permute-start(bf16[2,1024,128]{2,1,0:T(8,128)(2,1)S(1)} %get-tuple-element.23), channel_id=1, source_target_pairs={{0,15},{1,2},{2,1},{3,4},{4,3},{5,6},{6,5},{7,8},{8,7},{9,10},{10,... | collective-permute-start | bytes 1572872 | tf_op jit(solution)/shard_map/ppermute | solution.py:305
  25.3 17.3 %all-to-all-start.1 = ((bf16[16,96,128]{2,1,0:T(8,128)(2,1)}), bf16[16,96,128]{2,1,0:T(8,128)(2,1)S(1)}, u32[]{:S(2)}, u32[]{:S(2)}) async-start(bf16[16,96,128]{2,1,0:T(8,128)(2,1)} %get-tuple-element.19), calls=%async_computation.1 | async-start | bytes 786432 | tf_op jit(solution)/shard_map/all_to_all | solution.py:376

commit v8 on v7

--- a/solution.py
+++ b/solution.py
@@ -56,19 +56,24 @@
 
 
 def split_kernel(head_ref, k_ref, v_ref, *refs):
-    outs, sems = refs[:-1], refs[-1]
+    outs, held, sems = refs[:KVH], refs[KVH], refs[KVH + 1]
     copies = []
     for place, out in enumerate(outs):
         head = jnp.bitwise_xor(head_ref[0], place)
         cols = pl.ds(pl.multiple_of(head * HD, HD), HD)
-        for which, array in enumerate((k_ref, v_ref)):
-            copies.append(
-                pltpu.make_async_copy(array.at[0, :, cols], out.at[which], sems.at[place, which])
-            )
-    for copy in copies:
-        copy.start()
-    for copy in copies:
-        copy.wait()
+        keys = pltpu.make_async_copy(k_ref.at[0, :, cols], out.at[0], sems.at[place, 0])
+        values = pltpu.make_async_copy(v_ref.at[0, :, cols], held.at[place], sems.at[place, 1])
+        copies.append((keys, values))
+    for keys, values in copies:
+        values.start()
+    for keys, values in copies:
+        keys.start()
+    for place, out in enumerate(outs):
+        copies[place][1].wait()
+        for first in range(0, held.shape[1], HD):
+            out[1, first : first + HD] = held[place, first : first + HD].T
+    for keys, values in copies:
+        keys.wait()
 
 
 def pack_kernel(samples, _, received_ref, packed_ref, slots_ref, counts_ref):
@@ -89,19 +94,22 @@
 
 
 def block_scores(rows, keys):
-    return lax.dot_general(rows, keys, (((1,), (1,)), ((), ())), preferred_element_type=jnp.float32)
+    return lax.dot_general(keys, rows, (((1,), (1,)), ((), ())), preferred_element_type=jnp.float32)
 
 
 def block_attention(raw, values):
-    top = jnp.max(raw, axis=1, keepdims=True)
+    values = jnp.concatenate(
+        [values[first : first + HD] for first in range(0, values.shape[0], HD)], axis=1
+    )
+    top = jnp.max(raw, axis=0, keepdims=True)
     probs = jnp.exp2((raw - top) * (SCALING * LOG2E))
-    total = jnp.sum(probs, axis=1, keepdims=True)
-    acc = jnp.dot(probs.astype(jnp.bfloat16), values, preferred_element_type=jnp.float32)
+    total = jnp.sum(probs, axis=0, keepdims=True)
+    acc = jnp.dot(values, probs.astype(jnp.bfloat16), preferred_element_type=jnp.float32)
     return acc, top * (SCALING * LOG2E), total
 
 
 def encode(out):
-    largest = jnp.max(jnp.abs(out), axis=1, keepdims=True)
+    largest = jnp.max(jnp.abs(out), axis=0, keepdims=True)
     power = jnp.floor(jnp.log2(jnp.maximum(largest, 2.0**-112) * 1.0001)) + 1.0
     code = jnp.clip(jnp.round(out * jnp.exp2(15.0 - power)), -32767.0, 32767.0)
     return code.astype(jnp.int32), power.astype(jnp.int32)
@@ -111,9 +119,17 @@
     blocks, reply_ref = refs[:-1], refs[-1]
     slots, per = q_ref.shape[0], q_ref.shape[1]
     rows_of = per // 2
+    wide = chunk * rows_of
 
     def step(index, _):
-        rows = q_ref[pl.ds(index * chunk, chunk)].reshape(chunk * per, HD)
+        here = pl.ds(index * chunk, chunk)
+        rows = jnp.concatenate(
+            [
+                q_ref[here, 0:rows_of].reshape(wide, HD),
+                q_ref[here, rows_of:per].reshape(wide, HD),
+            ],
+            axis=0,
+        )
         parts, raw = [], block_scores(rows, blocks[0][0])
         for place, block in enumerate(blocks):
             ready = raw
@@ -125,25 +141,27 @@
         total = functools.reduce(jnp.add, [w * part[2] for w, part in zip(weights, parts)])
         share = 1.0 / total
         out = functools.reduce(jnp.add, [(w * share) * part[0] for w, part in zip(weights, parts)])
-        log = top + jnp.log2(total)
+        log = jnp.round((top + jnp.log2(total)) * LSE_ONE).astype(jnp.int32)
         code, power = encode(out)
-        code = code.reshape(chunk, per, HD)
         packed = jnp.bitwise_or(
-            jnp.left_shift(code[:, :rows_of], 16), jnp.bitwise_and(code[:, rows_of:], 0xFFFF)
-        )
-        row = lax.broadcasted_iota(jnp.int32, (chunk, per, HD), 1)
-        lane = lax.broadcasted_iota(jnp.int32, (chunk, per, HD), 2)
-        log = jnp.round(log * LSE_ONE).astype(jnp.int32).reshape(chunk, per, 1)
-        note = jnp.where(lane == row, log, 0)
-        note = jnp.where(lane == row + per, power.reshape(chunk, per, 1), note)
-        note = jnp.sum(note, axis=1)
+            jnp.left_shift(code[:, :wide], 16), jnp.bitwise_and(code[:, wide:], 0xFFFF)
+        ).T
+        rest = jnp.zeros((1, HD - 2 * per), jnp.int32)
         for slot in range(chunk):
             dest, rank = index * (chunk // CAPE) + slot // CAPE, slot % CAPE
+            first = slot * rows_of
             for part in range(rows_of // 4):
                 reply_ref[dest, rank * (rows_of // 4) + part] = packed[
-                    slot, part * 4 : part * 4 + 4
+                    first + part * 4 : first + part * 4 + 4
                 ]
-            reply_ref[dest, CAPE * (rows_of // 4), rank : rank + 1] = note[slot : slot + 1]
+            pieces = [
+                array[:, start : start + rows_of]
+                for array in (log, power)
+                for start in (first, wide + first)
+            ]
+            reply_ref[dest, CAPE * (rows_of // 4), rank : rank + 1] = jnp.concatenate(
+                pieces + [rest], axis=1
+            )
         return 0
 
     lax.fori_loop(0, slots // chunk, step, 0)
@@ -287,7 +305,10 @@
         out_shape=[shape((2, positions, HD), jnp.bfloat16)] * KVH,
         in_specs=[SMEM] + [pl.BlockSpec(memory_space=pltpu.HBM)] * 2,
         out_specs=[VMEM] * KVH,
-        scratch_shapes=[pltpu.SemaphoreType.DMA((KVH, 2))],
+        scratch_shapes=[
+            pltpu.VMEM((KVH, positions, HD), jnp.bfloat16),
+            pltpu.SemaphoreType.DMA((KVH, 2)),
+        ],
         compiler_params=params(16),
         name="split",
     )(

time: 83.2 us -> 82.5 us (level)
  no operation moved by 1% of the time
where the time goes in v8:
time: 82.5 us; the launch traced here: 82 us
  blocking collectives  28.9 us (35%)
  starting transfers between devices  19.1 us (23%)
  Pallas kernels  18.7 us (23%)
  waiting for transfers between devices  15.2 us (18%)
    all_to_all x1, blocking collectives, local(): lax.all_to_all(chosen, 'seq', split_axis=0, concat_axis=0, tiled=True)  16.9 us
    all_to_all x1, blocking collectives, local(): lax.all_to_all(reply, 'engine', split_axis=0, concat_axis=0, tiled=True)  12 us
    all_to_all x1, waiting for transfers between devices, local(): lax.all_to_all(packed, 'engine', split_axis=0, concat_axis=0, tiled=True)  10.5 us
    all_to_all x1, starting transfers between devices, local(): lax.all_to_all(payload, 'seq', split_axis=0, concat_axis=0, tiled=True)  10.1 us
    pallas_call x1, Pallas kernels, local(): pl.pallas_call(functools.partial(prefix_kernel, 8 * CAPE), out_shape=shap...  8.76 us
    all_to_all x1, starting transfers between devices, local(): lax.all_to_all(packed, 'engine', split_axis=0, concat_axis=0, tiled=True)  6.77 us
    all_to_all x1, waiting for transfers between devices, local(): lax.all_to_all(payload, 'seq', split_axis=0, concat_axis=0, tiled=True)  4.72 us
    pallas_call x1, Pallas kernels, local(): pl.pallas_call(suffix_kernel, out_shape=(shape((samples, heads * steps, H...  2.75 us
  transfers between devices with their start and end apart: 5, of which 2 were waited for; matrix products, arithmetic and copies ran while one was open for 0% of the time, Pallas kernels for 8%

profile of v8, /device:TPU:1, one launch (start us, length us, event | category | flops | bytes accessed | tf_op | source)
XLA Modules:
  0.0 82.0 jit_solution(12039301498972974158)
XLA Ops:
  0.0 1.6 %prepare.1 = (bf16[2,128,128]{2,1,0:T(8,128)(2,1)}, bf16[16,72,128]{2,1,0:T(8,128)(2,1)}) custom-call(s32[2]{0:T(128)} %bitcast.4, bf16[2,4,4096]{2,1,0:T(4,128)(2,1)} %queries_ref.1), custom_call_target="tpu_custom_call" | custom-call | tf_op jit(solution)/shard_map/prepare/pallas_call | solution.py:335
  1.6 0.0 copy-start.2
  1.6 0.0 copy-start.4
  1.6 0.0 copy-start.5
  1.6 10.1 %all-to-all-start = ((bf16[16,72,128]{2,1,0:T(8,128)(2,1)}), bf16[16,72,128]{2,1,0:T(8,128)(2,1)S(1)}, u32[]{:S(2)}, u32[]{:S(2)}) async-start(bf16[16,72,128]{2,1,0:T(8,128)(2,1)} %get-tuple-element.17), calls=%async_computation | async-start | bytes 589824 | tf_op jit(solution)/shard_map/all_to_all | solution.py:345
  11.8 0.0 copy-start
  11.8 0.0 copy-start.1
  11.8 0.0 copy-start.3
  11.8 2.8 %split.1 = (bf16[2,1024,128]{2,1,0:T(8,128)(2,1)S(1)}, bf16[2,1024,128]{2,1,0:T(8,128)(2,1)}, bf16[2,1024,128]{2,1,0:T(8,128)(2,1)}, bf16[2,1024,128]{2,1,0:T(8,128)(2,1)S(1)}) custom-call(s32[1]{0:T(128)} %bitcast.2.head_ref, bf16[1,1024,512]{2,1,0:T(8,128)(2,1)} %k_ref.3, bf16[1,1024,512]{2,1,0:T(8,128)(2,1)} %v_ref.3), custom_call_target="tpu_custom_call" | custom-call | tf_op jit(solution)/shard_map/split/pallas_call | solution.py:303
  14.5 0.2 collective-permute-start
  14.7 1.6 %collective-permute-start.1 = (bf16[2,1024,128]{2,1,0:T(8,128)(2,1)}, bf16[2,1024,128]{2,1,0:T(8,128)(2,1)S(1)}, u32[]{:S(2)}, u32[]{:S(2)}) collective-permute-start(bf16[2,1024,128]{2,1,0:T(8,128)(2,1)} %get-tuple-element.22), channel_id=1, source_target_pairs={{0,14},{1,3},{2,0},{3,5},{4,2},{5,7},{6,4},{7,9},{8,6},{9,11},{10,... | collective-permute-start | bytes 1572872 | tf_op jit(solution)/shard_map/ppermute | solution.py:326
  16.4 0.4 collective-permute-start.2
  16.8 0.0 copy-done.2
  16.8 0.0 copy-done.4
  16.8 0.0 copy-done.5
  16.8 0.0 copy-done
  16.8 0.0 copy-done.1
  16.8 0.0 copy-done.3
  16.8 2.8 %suffix.1 = (f32[2,128,128]{2,1,0:T(8,128)S(1)}, f32[2,128,128]{2,1,0:T(8,128)S(1)}) custom-call(s32[2]{0:T(128)S(1)} %copy-done.5, bf16[2,128,128]{2,1,0:T(8,128)(2,1)S(1)} %copy-done.2, bf16[2,4,512]{2,1,0:T(4,128)(2,1)S(1)} %copy-done.3, bf16[2,4,512]{2,1,0:T(4,128)(2,1)S(1)} %copy-done.4, bf16[2,512,512]{2,1,0:T(8,128)(2,1)S(1)} %copy-done, ...), custom_call_target="tpu_custom_call" | custom-call | tf_op jit(solution)/shard_map/suffix/pallas_call | solution.py:366
  19.6 4.7 %all-to-all-done.received_ref = bf16[16,72,128]{2,1,0:T(8,128)(2,1)S(1)} async-done(((bf16[16,72,128]{2,1,0:T(8,128)(2,1)}), bf16[16,72,128]{2,1,0:T(8,128)(2,1)S(1)}, u32[]{:S(2)}, u32[]{:S(2)}) %all-to-all-start) | async-done | bytes 294944 | tf_op jit(solution)/shard_map/all_to_all | solution.py:345
  24.3 1.0 %pack.1 = (bf16[16,96,128]{2,1,0:T(8,128)(2,1)}, s32[32]{0:T(128)S(1)}) custom-call(f32[2,128,128]{2,1,0:T(8,128)S(1)} %get-tuple-element.16._.suffix_log_ref, bf16[16,72,128]{2,1,0:T(8,128)(2,1)S(1)} %all-to-all-done.received_ref), custom_call_target="tpu_custom_call" | custom-call | tf_op jit(solution)/shard_map/pack/pallas_call | solution.py:385
  25.3 6.8 %all-to-all-start.1 = ((bf16[16,96,128]{2,1,0:T(8,128)(2,1)}), bf16[16,96,128]{2,1,0:T(8,128)(2,1)S(1)}, u32[]{:S(2)}, u32[]{:S(2)}) async-start(bf16[16,96,128]{2,1,0:T(8,128)(2,1)} %get-tuple-element.19), calls=%async_computation.1 | async-start | bytes 786432 | tf_op jit(solution)/shard_map/all_to_all | solution.py:397
  32.1 0.0 collective-permute-done.refs_1_
  32.1 0.0 collective-permute-done.1.refs_2_
  32.1 0.0 collective-permute-done.2.refs_3_
  32.1 10.5 %all-to-all-done.1 = bf16[16,96,128]{2,1,0:T(8,128)(2,1)S(1)} async-done(((bf16[16,96,128]{2,1,0:T(8,128)(2,1)}), bf16[16,96,128]{2,1,0:T(8,128)(2,1)S(1)}, u32[]{:S(2)}, u32[]{:S(2)}) %all-to-all-start.1) | async-done | bytes 393248 | tf_op jit(solution)/shard_map/all_to_all | solution.py:397
  42.6 8.8 %prefix.1 = s32[16,13,4,128]{3,2,1,0:T(4,128)S(1)} custom-call(bf16[48,32,128]{2,1,0:T(8,128)(2,1)S(1)} %bitcast.3, bf16[2,1024,128]{2,1,0:T(8,128)(2,1)S(1)} %get-tuple-element.20.refs_0_, bf16[2,1024,128]{2,1,0:T(8,128)(2,1)S(1)} %collective-permute-done.refs_1_, bf16[2,1024,128]{2,1,0:T(8,128)(2,1)S(1)} %collective-permute-done.1.refs_2_, ...), custom_call_target="tpu_custom_call" | custom-call | tf_op jit(solution)/shard_map/prefix/pallas_call | solution.py:399
  51.4 12.0 %all_to_all.20.reply_ref = s32[16,13,4,128]{3,2,1,0:T(4,128)S(1)} all-to-all(s32[16,13,4,128]{3,2,1,0:T(4,128)S(1)} %prefix.1), channel_id=1, replica_groups=mesh['engine'=16,'seq'=16] {'engine'}, dimensions={0} | all-to-all | bytes 851968 | tf_op jit(solution)/shard_map/all_to_all | solution.py:410
  63.4 0.6 select.3
  64.0 16.9 %all_to_all.21.chosen_ref = s32[16,9,4,128]{3,2,1,0:T(4,128)S(1)} all-to-all(s32[16,9,4,128]{3,2,1,0:T(4,128)S(1)} %select.3), channel_id=1, replica_groups=mesh['engine'=16,'seq'=16] {'seq'}, dimensions={0} | all-to-all | bytes 589824 | tf_op jit(solution)/shard_map/all_to_all | solution.py:420
  80.9 1.1 %combine.1 = bf16[2,4,4096]{2,1,0:T(4,128)(2,1)} custom-call(s32[16,9,4,128]{3,2,1,0:T(4,128)S(1)} %all_to_all.21.chosen_ref, f32[2,128,128]{2,1,0:T(8,128)S(1)} %get-tuple-element.24.suffix_out_ref, f32[2,128,128]{2,1,0:T(8,128)S(1)} %get-tuple-element.16._.suffix_log_ref), custom_call_target="tpu_custom_call" | custom-call | tf_op jit(solution)/shard_map/combine/pallas_call | solution.py:422
Async XLA Ops:
  1.6 15.1 %copy-start.2 = (bf16[2,128,128]{2,1,0:T(8,128)(2,1)S(1)}, bf16[2,128,128]{2,1,0:T(8,128)(2,1)}, u32[]{:S(2)}) copy-start(bf16[2,128,128]{2,1,0:T(8,128)(2,1)} %get-tuple-element.15.rows_ref) | copy-start | bytes 196612
  1.6 15.1 %copy-start.4 = (bf16[2,4,512]{2,1,0:T(4,128)(2,1)S(1)}, bf16[2,4,512]{2,1,0:T(4,128)(2,1)}, u32[]{:S(2)}) copy-start(bf16[2,4,512]{2,1,0:T(4,128)(2,1)} %fresh_v_ref.1) | copy-start | bytes 24580
  1.6 15.1 %copy-start.5 = (s32[2]{0:T(128)S(1)}, s32[2]{0:T(128)}, u32[]{:S(2)}) copy-start(s32[2]{0:T(128)} %length_ref.1) | copy-start | bytes 28
  1.6 22.6 %all-to-all-start = ((bf16[16,72,128]{2,1,0:T(8,128)(2,1)}), bf16[16,72,128]{2,1,0:T(8,128)(2,1)S(1)}, u32[]{:S(2)}, u32[]{:S(2)}) async-start(bf16[16,72,128]{2,1,0:T(8,128)(2,1)} %get-tuple-element.17), calls=%async_computation | async-start | bytes 589824 | tf_op jit(solution)/shard_map/all_to_all | solution.py:345
  11.8 5.0 %copy-start = (bf16[2,512,512]{2,1,0:T(8,128)(2,1)S(1)}, bf16[2,512,512]{2,1,0:T(8,128)(2,1)}, u32[]{:S(2)}) copy-start(bf16[2,512,512]{2,1,0:T(8,128)(2,1)} %k_ref.2) | copy-start | bytes 3145732
  11.8 5.0 %copy-start.1 = (bf16[2,512,512]{2,1,0:T(8,128)(2,1)S(1)}, bf16[2,512,512]{2,1,0:T(8,128)(2,1)}, u32[]{:S(2)}) copy-start(bf16[2,512,512]{2,1,0:T(8,128)(2,1)} %v_ref.2) | copy-start | bytes 3145732
  11.8 5.0 %copy-start.3 = (bf16[2,4,512]{2,1,0:T(4,128)(2,1)S(1)}, bf16[2,4,512]{2,1,0:T(4,128)(2,1)}, u32[]{:S(2)}) copy-start(bf16[2,4,512]{2,1,0:T(4,128)(2,1)} %fresh_k_ref.1) | copy-start | bytes 24580
  14.5 17.5 %collective-permute-start = (bf16[2,1024,128]{2,1,0:T(8,128)(2,1)}, bf16[2,1024,128]{2,1,0:T(8,128)(2,1)S(1)}, u32[]{:S(2)}, u32[]{:S(2)}) collective-permute-start(bf16[2,1024,128]{2,1,0:T(8,128)(2,1)} %get-tuple-element.21), channel_id=1, source_target_pairs={{0,1},{1,0},{2,3},{3,2},{4,5},{5,4},{6,7},{7,6},{8,9},{9,8},{10,11... | collective-permute-start | bytes 1572872 | tf_op jit(solution)/shard_map/ppermute | solution.py:326
  14.7 17.4 %collective-permute-start.1 = (bf16[2,1024,128]{2,1,0:T(8,128)(2,1)}, bf16[2,1024,128]{2,1,0:T(8,128)(2,1)S(1)}, u32[]{:S(2)}, u32[]{:S(2)}) collective-permute-start(bf16[2,1024,128]{2,1,0:T(8,128)(2,1)} %get-tuple-element.22), channel_id=1, source_target_pairs={{0,14},{1,3},{2,0},{3,5},{4,2},{5,7},{6,4},{7,9},{8,6},{9,11},{10,... | collective-permute-start | bytes 1572872 | tf_op jit(solution)/shard_map/ppermute | solution.py:326
  16.4 15.8 %collective-permute-start.2 = (bf16[2,1024,128]{2,1,0:T(8,128)(2,1)S(1)}, bf16[2,1024,128]{2,1,0:T(8,128)(2,1)S(1)}, u32[]{:S(2)}, u32[]{:S(2)}) collective-permute-start(bf16[2,1024,128]{2,1,0:T(8,128)(2,1)S(1)} %get-tuple-element.23), channel_id=1, source_target_pairs={{0,15},{1,2},{2,1},{3,4},{4,3},{5,6},{6,5},{7,8},{8,7},{9,10},{10,... | collective-permute-start | bytes 1572872 | tf_op jit(solution)/shard_map/ppermute | solution.py:326
  25.3 17.3 %all-to-all-start.1 = ((bf16[16,96,128]{2,1,0:T(8,128)(2,1)}), bf16[16,96,128]{2,1,0:T(8,128)(2,1)S(1)}, u32[]{:S(2)}, u32[]{:S(2)}) async-start(bf16[16,96,128]{2,1,0:T(8,128)(2,1)} %get-tuple-element.19), calls=%async_computation.1 | async-start | bytes 786432 | tf_op jit(solution)/shard_map/all_to_all | solution.py:397

commit v9 on v8

--- a/solution.py
+++ b/solution.py
@@ -121,21 +121,16 @@
     rows_of = per // 2
     wide = chunk * rows_of
 
-    def step(index, _):
-        here = pl.ds(index * chunk, chunk)
-        rows = jnp.concatenate(
+    def rows_from(start):
+        return jnp.concatenate(
             [
-                q_ref[here, 0:rows_of].reshape(wide, HD),
-                q_ref[here, rows_of:per].reshape(wide, HD),
+                q_ref[start : start + chunk, 0:rows_of].reshape(wide, HD),
+                q_ref[start : start + chunk, rows_of:per].reshape(wide, HD),
             ],
             axis=0,
         )
-        parts, raw = [], block_scores(rows, blocks[0][0])
-        for place, block in enumerate(blocks):
-            ready = raw
-            if place + 1 < len(blocks):
-                raw = block_scores(rows, blocks[place + 1][0])
-            parts.append(block_attention(ready, block[1]))
+
+    def finish(start, parts):
         top = functools.reduce(jnp.maximum, [part[1] for part in parts])
         weights = [jnp.exp2(part[1] - top) for part in parts]
         total = functools.reduce(jnp.add, [w * part[2] for w, part in zip(weights, parts)])
@@ -148,23 +143,34 @@
         ).T
         rest = jnp.zeros((1, HD - 2 * per), jnp.int32)
         for slot in range(chunk):
-            dest, rank = index * (chunk // CAPE) + slot // CAPE, slot % CAPE
+            dest, rank = (start + slot) // CAPE, (start + slot) % CAPE
             first = slot * rows_of
             for part in range(rows_of // 4):
                 reply_ref[dest, rank * (rows_of // 4) + part] = packed[
                     first + part * 4 : first + part * 4 + 4
                 ]
             pieces = [
-                array[:, start : start + rows_of]
+                array[:, begin : begin + rows_of]
                 for array in (log, power)
-                for start in (first, wide + first)
+                for begin in (first, wide + first)
             ]
             reply_ref[dest, CAPE * (rows_of // 4), rank : rank + 1] = jnp.concatenate(
                 pieces + [rest], axis=1
             )
-        return 0
-
-    lax.fori_loop(0, slots // chunk, step, 0)
+
+    starts = range(0, slots, chunk)
+    stages = [(start, place) for start in starts for place in range(len(blocks))]
+    rows = {start: rows_from(start) for start in starts}
+    raw, parts = block_scores(rows[0], blocks[0][0]), []
+    for number, (start, place) in enumerate(stages):
+        ready = raw
+        if number + 1 < len(stages):
+            later, block = stages[number + 1]
+            raw = block_scores(rows[later], blocks[block][0])
+        parts.append(block_attention(ready, blocks[place][1]))
+        if place + 1 == len(blocks):
+            finish(start, parts)
+            parts = []
 
 
 def select_kernel(samples, slots_ref, reply_ref, chosen_ref):

time: 82.5 us -> 81.9 us (level)
  no operation moved by 1% of the time
where the time goes in v9:
time: 81.9 us; the launch traced here: 81.5 us
  blocking collectives  28.9 us (35%)
  starting transfers between devices  19.1 us (23%)
  Pallas kernels  18.1 us (22%)
  waiting for transfers between devices  15.2 us (19%)
    all_to_all x1, blocking collectives, local(): lax.all_to_all(chosen, 'seq', split_axis=0, concat_axis=0, tiled=True)  16.8 us
    all_to_all x1, blocking collectives, local(): lax.all_to_all(reply, 'engine', split_axis=0, concat_axis=0, tiled=True)  12 us
    all_to_all x1, waiting for transfers between devices, local(): lax.all_to_all(packed, 'engine', split_axis=0, concat_axis=0, tiled=True)  10.5 us
    all_to_all x1, starting transfers between devices, local(): lax.all_to_all(payload, 'seq', split_axis=0, concat_axis=0, tiled=True)  10.1 us
    pallas_call x1, Pallas kernels, local(): pl.pallas_call(functools.partial(prefix_kernel, 8 * CAPE), out_shape=shap...  8.18 us
    all_to_all x1, starting transfers between devices, local(): lax.all_to_all(packed, 'engine', split_axis=0, concat_axis=0, tiled=True)  6.77 us
    all_to_all x1, waiting for transfers between devices, local(): lax.all_to_all(payload, 'seq', split_axis=0, concat_axis=0, tiled=True)  4.72 us
    pallas_call x1, Pallas kernels, local(): pl.pallas_call(suffix_kernel, out_shape=(shape((samples, heads * steps, H...  2.75 us
  transfers between devices with their start and end apart: 5, of which 2 were waited for; matrix products, arithmetic and copies ran while one was open for 0% of the time, Pallas kernels for 8%

profile of v9, /device:TPU:1, one launch (start us, length us, event | category | flops | bytes accessed | tf_op | source)
XLA Modules:
  0.0 81.5 jit_solution(15448337868298905303)
XLA Ops:
  0.0 1.6 %prepare.1 = (bf16[2,128,128]{2,1,0:T(8,128)(2,1)}, bf16[16,72,128]{2,1,0:T(8,128)(2,1)}) custom-call(s32[2]{0:T(128)} %bitcast.4, bf16[2,4,4096]{2,1,0:T(4,128)(2,1)} %queries_ref.1), custom_call_target="tpu_custom_call" | custom-call | tf_op jit(solution)/shard_map/prepare/pallas_call | solution.py:341
  1.6 0.0 copy-start.2
  1.6 0.0 copy-start.4
  1.6 0.0 copy-start.5
  1.6 10.1 %all-to-all-start = ((bf16[16,72,128]{2,1,0:T(8,128)(2,1)}), bf16[16,72,128]{2,1,0:T(8,128)(2,1)S(1)}, u32[]{:S(2)}, u32[]{:S(2)}) async-start(bf16[16,72,128]{2,1,0:T(8,128)(2,1)} %get-tuple-element.17), calls=%async_computation | async-start | bytes 589824 | tf_op jit(solution)/shard_map/all_to_all | solution.py:351
  11.8 0.0 copy-start
  11.8 0.0 copy-start.1
  11.8 0.0 copy-start.3
  11.8 2.8 %split.1 = (bf16[2,1024,128]{2,1,0:T(8,128)(2,1)S(1)}, bf16[2,1024,128]{2,1,0:T(8,128)(2,1)}, bf16[2,1024,128]{2,1,0:T(8,128)(2,1)}, bf16[2,1024,128]{2,1,0:T(8,128)(2,1)S(1)}) custom-call(s32[1]{0:T(128)} %bitcast.2.head_ref, bf16[1,1024,512]{2,1,0:T(8,128)(2,1)} %k_ref.3, bf16[1,1024,512]{2,1,0:T(8,128)(2,1)} %v_ref.3), custom_call_target="tpu_custom_call" | custom-call | tf_op jit(solution)/shard_map/split/pallas_call | solution.py:309
  14.5 0.2 collective-permute-start
  14.7 1.6 %collective-permute-start.1 = (bf16[2,1024,128]{2,1,0:T(8,128)(2,1)}, bf16[2,1024,128]{2,1,0:T(8,128)(2,1)S(1)}, u32[]{:S(2)}, u32[]{:S(2)}) collective-permute-start(bf16[2,1024,128]{2,1,0:T(8,128)(2,1)} %get-tuple-element.22), channel_id=1, source_target_pairs={{0,14},{1,3},{2,0},{3,5},{4,2},{5,7},{6,4},{7,9},{8,6},{9,11},{10,... | collective-permute-start | bytes 1572872 | tf_op jit(solution)/shard_map/ppermute | solution.py:332
  16.4 0.4 collective-permute-start.2
  16.8 0.0 copy-done.2
  16.8 0.0 copy-done.4
  16.8 0.0 copy-done.5
  16.8 0.0 copy-done
  16.8 0.0 copy-done.1
  16.8 0.0 copy-done.3
  16.8 2.8 %suffix.1 = (f32[2,128,128]{2,1,0:T(8,128)S(1)}, f32[2,128,128]{2,1,0:T(8,128)S(1)}) custom-call(s32[2]{0:T(128)S(1)} %copy-done.5, bf16[2,128,128]{2,1,0:T(8,128)(2,1)S(1)} %copy-done.2, bf16[2,4,512]{2,1,0:T(4,128)(2,1)S(1)} %copy-done.3, bf16[2,4,512]{2,1,0:T(4,128)(2,1)S(1)} %copy-done.4, bf16[2,512,512]{2,1,0:T(8,128)(2,1)S(1)} %copy-done, ...), custom_call_target="tpu_custom_call" | custom-call | tf_op jit(solution)/shard_map/suffix/pallas_call | solution.py:372
  19.6 4.7 %all-to-all-done.received_ref = bf16[16,72,128]{2,1,0:T(8,128)(2,1)S(1)} async-done(((bf16[16,72,128]{2,1,0:T(8,128)(2,1)}), bf16[16,72,128]{2,1,0:T(8,128)(2,1)S(1)}, u32[]{:S(2)}, u32[]{:S(2)}) %all-to-all-start) | async-done | bytes 294944 | tf_op jit(solution)/shard_map/all_to_all | solution.py:351
  24.3 1.0 %pack.1 = (bf16[16,96,128]{2,1,0:T(8,128)(2,1)}, s32[32]{0:T(128)S(1)}) custom-call(f32[2,128,128]{2,1,0:T(8,128)S(1)} %get-tuple-element.16._.suffix_log_ref, bf16[16,72,128]{2,1,0:T(8,128)(2,1)S(1)} %all-to-all-done.received_ref), custom_call_target="tpu_custom_call" | custom-call | tf_op jit(solution)/shard_map/pack/pallas_call | solution.py:391
  25.3 6.8 %all-to-all-start.1 = ((bf16[16,96,128]{2,1,0:T(8,128)(2,1)}), bf16[16,96,128]{2,1,0:T(8,128)(2,1)S(1)}, u32[]{:S(2)}, u32[]{:S(2)}) async-start(bf16[16,96,128]{2,1,0:T(8,128)(2,1)} %get-tuple-element.19), calls=%async_computation.1 | async-start | bytes 786432 | tf_op jit(solution)/shard_map/all_to_all | solution.py:403
  32.1 0.0 collective-permute-done.refs_1_
  32.1 0.0 collective-permute-done.1.refs_2_
  32.1 0.0 collective-permute-done.2.refs_3_
  32.1 10.5 %all-to-all-done.1 = bf16[16,96,128]{2,1,0:T(8,128)(2,1)S(1)} async-done(((bf16[16,96,128]{2,1,0:T(8,128)(2,1)}), bf16[16,96,128]{2,1,0:T(8,128)(2,1)S(1)}, u32[]{:S(2)}, u32[]{:S(2)}) %all-to-all-start.1) | async-done | bytes 393248 | tf_op jit(solution)/shard_map/all_to_all | solution.py:403
  42.6 8.2 %prefix.1 = s32[16,13,4,128]{3,2,1,0:T(4,128)S(1)} custom-call(bf16[48,32,128]{2,1,0:T(8,128)(2,1)S(1)} %bitcast.3, bf16[2,1024,128]{2,1,0:T(8,128)(2,1)S(1)} %get-tuple-element.20.refs_0_, bf16[2,1024,128]{2,1,0:T(8,128)(2,1)S(1)} %collective-permute-done.refs_1_, bf16[2,1024,128]{2,1,0:T(8,128)(2,1)S(1)} %collective-permute-done.1.refs_2_, ...), custom_call_target="tpu_custom_call" | custom-call | tf_op jit(solution)/shard_map/prefix/pallas_call | solution.py:405
  50.8 12.0 %all_to_all.20.reply_ref = s32[16,13,4,128]{3,2,1,0:T(4,128)S(1)} all-to-all(s32[16,13,4,128]{3,2,1,0:T(4,128)S(1)} %prefix.1), channel_id=1, replica_groups=mesh['engine'=16,'seq'=16] {'engine'}, dimensions={0} | all-to-all | bytes 851968 | tf_op jit(solution)/shard_map/all_to_all | solution.py:416
  62.9 0.6 select.3
  63.5 16.8 %all_to_all.21.chosen_ref = s32[16,9,4,128]{3,2,1,0:T(4,128)S(1)} all-to-all(s32[16,9,4,128]{3,2,1,0:T(4,128)S(1)} %select.3), channel_id=1, replica_groups=mesh['engine'=16,'seq'=16] {'seq'}, dimensions={0} | all-to-all | bytes 589824 | tf_op jit(solution)/shard_map/all_to_all | solution.py:426
  80.3 1.1 %combine.1 = bf16[2,4,4096]{2,1,0:T(4,128)(2,1)} custom-call(s32[16,9,4,128]{3,2,1,0:T(4,128)S(1)} %all_to_all.21.chosen_ref, f32[2,128,128]{2,1,0:T(8,128)S(1)} %get-tuple-element.24.suffix_out_ref, f32[2,128,128]{2,1,0:T(8,128)S(1)} %get-tuple-element.16._.suffix_log_ref), custom_call_target="tpu_custom_call" | custom-call | tf_op jit(solution)/shard_map/combine/pallas_call | solution.py:428
Async XLA Ops:
  1.6 15.1 %copy-start.2 = (bf16[2,128,128]{2,1,0:T(8,128)(2,1)S(1)}, bf16[2,128,128]{2,1,0:T(8,128)(2,1)}, u32[]{:S(2)}) copy-start(bf16[2,128,128]{2,1,0:T(8,128)(2,1)} %get-tuple-element.15.rows_ref) | copy-start | bytes 196612
  1.6 15.1 %copy-start.4 = (bf16[2,4,512]{2,1,0:T(4,128)(2,1)S(1)}, bf16[2,4,512]{2,1,0:T(4,128)(2,1)}, u32[]{:S(2)}) copy-start(bf16[2,4,512]{2,1,0:T(4,128)(2,1)} %fresh_v_ref.1) | copy-start | bytes 24580
  1.6 15.1 %copy-start.5 = (s32[2]{0:T(128)S(1)}, s32[2]{0:T(128)}, u32[]{:S(2)}) copy-start(s32[2]{0:T(128)} %length_ref.1) | copy-start | bytes 28
  1.6 22.6 %all-to-all-start = ((bf16[16,72,128]{2,1,0:T(8,128)(2,1)}), bf16[16,72,128]{2,1,0:T(8,128)(2,1)S(1)}, u32[]{:S(2)}, u32[]{:S(2)}) async-start(bf16[16,72,128]{2,1,0:T(8,128)(2,1)} %get-tuple-element.17), calls=%async_computation | async-start | bytes 589824 | tf_op jit(solution)/shard_map/all_to_all | solution.py:351
  11.8 5.0 %copy-start = (bf16[2,512,512]{2,1,0:T(8,128)(2,1)S(1)}, bf16[2,512,512]{2,1,0:T(8,128)(2,1)}, u32[]{:S(2)}) copy-start(bf16[2,512,512]{2,1,0:T(8,128)(2,1)} %k_ref.2) | copy-start | bytes 3145732
  11.8 5.0 %copy-start.1 = (bf16[2,512,512]{2,1,0:T(8,128)(2,1)S(1)}, bf16[2,512,512]{2,1,0:T(8,128)(2,1)}, u32[]{:S(2)}) copy-start(bf16[2,512,512]{2,1,0:T(8,128)(2,1)} %v_ref.2) | copy-start | bytes 3145732
  11.8 5.0 %copy-start.3 = (bf16[2,4,512]{2,1,0:T(4,128)(2,1)S(1)}, bf16[2,4,512]{2,1,0:T(4,128)(2,1)}, u32[]{:S(2)}) copy-start(bf16[2,4,512]{2,1,0:T(4,128)(2,1)} %fresh_k_ref.1) | copy-start | bytes 24580
  14.5 17.5 %collective-permute-start = (bf16[2,1024,128]{2,1,0:T(8,128)(2,1)}, bf16[2,1024,128]{2,1,0:T(8,128)(2,1)S(1)}, u32[]{:S(2)}, u32[]{:S(2)}) collective-permute-start(bf16[2,1024,128]{2,1,0:T(8,128)(2,1)} %get-tuple-element.21), channel_id=1, source_target_pairs={{0,1},{1,0},{2,3},{3,2},{4,5},{5,4},{6,7},{7,6},{8,9},{9,8},{10,11... | collective-permute-start | bytes 1572872 | tf_op jit(solution)/shard_map/ppermute | solution.py:332
  14.7 17.4 %collective-permute-start.1 = (bf16[2,1024,128]{2,1,0:T(8,128)(2,1)}, bf16[2,1024,128]{2,1,0:T(8,128)(2,1)S(1)}, u32[]{:S(2)}, u32[]{:S(2)}) collective-permute-start(bf16[2,1024,128]{2,1,0:T(8,128)(2,1)} %get-tuple-element.22), channel_id=1, source_target_pairs={{0,14},{1,3},{2,0},{3,5},{4,2},{5,7},{6,4},{7,9},{8,6},{9,11},{10,... | collective-permute-start | bytes 1572872 | tf_op jit(solution)/shard_map/ppermute | solution.py:332
  16.4 15.8 %collective-permute-start.2 = (bf16[2,1024,128]{2,1,0:T(8,128)(2,1)S(1)}, bf16[2,1024,128]{2,1,0:T(8,128)(2,1)S(1)}, u32[]{:S(2)}, u32[]{:S(2)}) collective-permute-start(bf16[2,1024,128]{2,1,0:T(8,128)(2,1)S(1)} %get-tuple-element.23), channel_id=1, source_target_pairs={{0,15},{1,2},{2,1},{3,4},{4,3},{5,6},{6,5},{7,8},{8,7},{9,10},{10,... | collective-permute-start | bytes 1572872 | tf_op jit(solution)/shard_map/ppermute | solution.py:332
  25.3 17.3 %all-to-all-start.1 = ((bf16[16,96,128]{2,1,0:T(8,128)(2,1)}), bf16[16,96,128]{2,1,0:T(8,128)(2,1)S(1)}, u32[]{:S(2)}, u32[]{:S(2)}) async-start(bf16[16,96,128]{2,1,0:T(8,128)(2,1)} %get-tuple-element.19), calls=%async_computation.1 | async-start | bytes 786432 | tf_op jit(solution)/shard_map/all_to_all | solution.py:403

commit v10 on v9

--- a/solution.py
+++ b/solution.py
@@ -403,7 +403,7 @@
     dispatched = lax.all_to_all(packed, "engine", split_axis=0, concat_axis=0, tiled=True)
 
     reply = pl.pallas_call(
-        functools.partial(prefix_kernel, 8 * CAPE),
+        functools.partial(prefix_kernel, 16),
         out_shape=shape((engine_count, CAPE * per // 8 + 1, 4, HD), jnp.int32),
         in_specs=[VMEM] * (1 + KVH),
         out_specs=VMEM,

time: 81.9 us -> 81.8 us (level)
  no operation moved by 1% of the time
where the time goes in v10:
time: 81.8 us; the launch traced here: 81.4 us
  blocking collectives  28.9 us (35%)
  starting transfers between devices  19.1 us (23%)
  Pallas kernels  18 us (22%)
  waiting for transfers between devices  15.2 us (19%)
    all_to_all x1, blocking collectives, local(): lax.all_to_all(chosen, 'seq', split_axis=0, concat_axis=0, tiled=True)  16.8 us
    all_to_all x1, blocking collectives, local(): lax.all_to_all(reply, 'engine', split_axis=0, concat_axis=0, tiled=True)  12 us
    all_to_all x1, waiting for transfers between devices, local(): lax.all_to_all(packed, 'engine', split_axis=0, concat_axis=0, tiled=True)  10.5 us
    all_to_all x1, starting transfers between devices, local(): lax.all_to_all(payload, 'seq', split_axis=0, concat_axis=0, tiled=True)  10.1 us
    pallas_call x1, Pallas kernels, local(): pl.pallas_call(functools.partial(prefix_kernel, 16), out_shape=shape((eng...  8.13 us
    all_to_all x1, starting transfers between devices, local(): lax.all_to_all(packed, 'engine', split_axis=0, concat_axis=0, tiled=True)  6.77 us
    all_to_all x1, waiting for transfers between devices, local(): lax.all_to_all(payload, 'seq', split_axis=0, concat_axis=0, tiled=True)  4.72 us
    pallas_call x1, Pallas kernels, local(): pl.pallas_call(suffix_kernel, out_shape=(shape((samples, heads * steps, H...  2.75 us
  transfers between devices with their start and end apart: 5, of which 2 were waited for; matrix products, arithmetic and copies ran while one was open for 0% of the time, Pallas kernels for 8%

profile of v10, /device:TPU:1, one launch (start us, length us, event | category | flops | bytes accessed | tf_op | source)
XLA Modules:
  0.0 81.4 jit_solution(16790949283098445351)
XLA Ops:
  0.0 1.6 %prepare.1 = (bf16[2,128,128]{2,1,0:T(8,128)(2,1)}, bf16[16,72,128]{2,1,0:T(8,128)(2,1)}) custom-call(s32[2]{0:T(128)} %bitcast.4, bf16[2,4,4096]{2,1,0:T(4,128)(2,1)} %queries_ref.1), custom_call_target="tpu_custom_call" | custom-call | tf_op jit(solution)/shard_map/prepare/pallas_call | solution.py:341
  1.6 0.0 copy-start.2
  1.6 0.0 copy-start.4
  1.6 0.0 copy-start.5
  1.6 10.1 %all-to-all-start = ((bf16[16,72,128]{2,1,0:T(8,128)(2,1)}), bf16[16,72,128]{2,1,0:T(8,128)(2,1)S(1)}, u32[]{:S(2)}, u32[]{:S(2)}) async-start(bf16[16,72,128]{2,1,0:T(8,128)(2,1)} %get-tuple-element.17), calls=%async_computation | async-start | bytes 589824 | tf_op jit(solution)/shard_map/all_to_all | solution.py:351
  11.8 0.0 copy-start
  11.8 0.0 copy-start.1
  11.8 0.0 copy-start.3
  11.8 2.8 %split.1 = (bf16[2,1024,128]{2,1,0:T(8,128)(2,1)S(1)}, bf16[2,1024,128]{2,1,0:T(8,128)(2,1)}, bf16[2,1024,128]{2,1,0:T(8,128)(2,1)}, bf16[2,1024,128]{2,1,0:T(8,128)(2,1)S(1)}) custom-call(s32[1]{0:T(128)} %bitcast.2.head_ref, bf16[1,1024,512]{2,1,0:T(8,128)(2,1)} %k_ref.3, bf16[1,1024,512]{2,1,0:T(8,128)(2,1)} %v_ref.3), custom_call_target="tpu_custom_call" | custom-call | tf_op jit(solution)/shard_map/split/pallas_call | solution.py:309
  14.5 0.2 collective-permute-start
  14.7 1.6 %collective-permute-start.1 = (bf16[2,1024,128]{2,1,0:T(8,128)(2,1)}, bf16[2,1024,128]{2,1,0:T(8,128)(2,1)S(1)}, u32[]{:S(2)}, u32[]{:S(2)}) collective-permute-start(bf16[2,1024,128]{2,1,0:T(8,128)(2,1)} %get-tuple-element.22), channel_id=1, source_target_pairs={{0,14},{1,3},{2,0},{3,5},{4,2},{5,7},{6,4},{7,9},{8,6},{9,11},{10,... | collective-permute-start | bytes 1572872 | tf_op jit(solution)/shard_map/ppermute | solution.py:332
  16.4 0.4 collective-permute-start.2
  16.8 0.0 copy-done.2
  16.8 0.0 copy-done.4
  16.8 0.0 copy-done.5
  16.8 0.0 copy-done
  16.8 0.0 copy-done.1
  16.8 0.0 copy-done.3
  16.8 2.8 %suffix.1 = (f32[2,128,128]{2,1,0:T(8,128)S(1)}, f32[2,128,128]{2,1,0:T(8,128)S(1)}) custom-call(s32[2]{0:T(128)S(1)} %copy-done.5, bf16[2,128,128]{2,1,0:T(8,128)(2,1)S(1)} %copy-done.2, bf16[2,4,512]{2,1,0:T(4,128)(2,1)S(1)} %copy-done.3, bf16[2,4,512]{2,1,0:T(4,128)(2,1)S(1)} %copy-done.4, bf16[2,512,512]{2,1,0:T(8,128)(2,1)S(1)} %copy-done, ...), custom_call_target="tpu_custom_call" | custom-call | tf_op jit(solution)/shard_map/suffix/pallas_call | solution.py:372
  19.6 4.7 %all-to-all-done.received_ref = bf16[16,72,128]{2,1,0:T(8,128)(2,1)S(1)} async-done(((bf16[16,72,128]{2,1,0:T(8,128)(2,1)}), bf16[16,72,128]{2,1,0:T(8,128)(2,1)S(1)}, u32[]{:S(2)}, u32[]{:S(2)}) %all-to-all-start) | async-done | bytes 294944 | tf_op jit(solution)/shard_map/all_to_all | solution.py:351
  24.3 1.0 %pack.1 = (bf16[16,96,128]{2,1,0:T(8,128)(2,1)}, s32[32]{0:T(128)S(1)}) custom-call(f32[2,128,128]{2,1,0:T(8,128)S(1)} %get-tuple-element.16._.suffix_log_ref, bf16[16,72,128]{2,1,0:T(8,128)(2,1)S(1)} %all-to-all-done.received_ref), custom_call_target="tpu_custom_call" | custom-call | tf_op jit(solution)/shard_map/pack/pallas_call | solution.py:391
  25.3 6.8 %all-to-all-start.1 = ((bf16[16,96,128]{2,1,0:T(8,128)(2,1)}), bf16[16,96,128]{2,1,0:T(8,128)(2,1)S(1)}, u32[]{:S(2)}, u32[]{:S(2)}) async-start(bf16[16,96,128]{2,1,0:T(8,128)(2,1)} %get-tuple-element.19), calls=%async_computation.1 | async-start | bytes 786432 | tf_op jit(solution)/shard_map/all_to_all | solution.py:403
  32.1 0.0 collective-permute-done.refs_1_
  32.1 0.0 collective-permute-done.1.refs_2_
  32.1 0.0 collective-permute-done.2.refs_3_
  32.1 10.5 %all-to-all-done.1 = bf16[16,96,128]{2,1,0:T(8,128)(2,1)S(1)} async-done(((bf16[16,96,128]{2,1,0:T(8,128)(2,1)}), bf16[16,96,128]{2,1,0:T(8,128)(2,1)S(1)}, u32[]{:S(2)}, u32[]{:S(2)}) %all-to-all-start.1) | async-done | bytes 393248 | tf_op jit(solution)/shard_map/all_to_all | solution.py:403
  42.6 8.1 %prefix.1 = s32[16,13,4,128]{3,2,1,0:T(4,128)S(1)} custom-call(bf16[48,32,128]{2,1,0:T(8,128)(2,1)S(1)} %bitcast.3, bf16[2,1024,128]{2,1,0:T(8,128)(2,1)S(1)} %get-tuple-element.20.refs_0_, bf16[2,1024,128]{2,1,0:T(8,128)(2,1)S(1)} %collective-permute-done.refs_1_, bf16[2,1024,128]{2,1,0:T(8,128)(2,1)S(1)} %collective-permute-done.1.refs_2_, ...), custom_call_target="tpu_custom_call" | custom-call | tf_op jit(solution)/shard_map/prefix/pallas_call | solution.py:405
  50.8 12.0 %all_to_all.20.reply_ref = s32[16,13,4,128]{3,2,1,0:T(4,128)S(1)} all-to-all(s32[16,13,4,128]{3,2,1,0:T(4,128)S(1)} %prefix.1), channel_id=1, replica_groups=mesh['engine'=16,'seq'=16] {'engine'}, dimensions={0} | all-to-all | bytes 851968 | tf_op jit(solution)/shard_map/all_to_all | solution.py:416
  62.8 0.6 select.3
  63.4 16.8 %all_to_all.21.chosen_ref = s32[16,9,4,128]{3,2,1,0:T(4,128)S(1)} all-to-all(s32[16,9,4,128]{3,2,1,0:T(4,128)S(1)} %select.3), channel_id=1, replica_groups=mesh['engine'=16,'seq'=16] {'seq'}, dimensions={0} | all-to-all | bytes 589824 | tf_op jit(solution)/shard_map/all_to_all | solution.py:426
  80.3 1.1 %combine.1 = bf16[2,4,4096]{2,1,0:T(4,128)(2,1)} custom-call(s32[16,9,4,128]{3,2,1,0:T(4,128)S(1)} %all_to_all.21.chosen_ref, f32[2,128,128]{2,1,0:T(8,128)S(1)} %get-tuple-element.24.suffix_out_ref, f32[2,128,128]{2,1,0:T(8,128)S(1)} %get-tuple-element.16._.suffix_log_ref), custom_call_target="tpu_custom_call" | custom-call | tf_op jit(solution)/shard_map/combine/pallas_call | solution.py:428
Async XLA Ops:
  1.6 15.1 %copy-start.2 = (bf16[2,128,128]{2,1,0:T(8,128)(2,1)S(1)}, bf16[2,128,128]{2,1,0:T(8,128)(2,1)}, u32[]{:S(2)}) copy-start(bf16[2,128,128]{2,1,0:T(8,128)(2,1)} %get-tuple-element.15.rows_ref) | copy-start | bytes 196612
  1.6 15.1 %copy-start.4 = (bf16[2,4,512]{2,1,0:T(4,128)(2,1)S(1)}, bf16[2,4,512]{2,1,0:T(4,128)(2,1)}, u32[]{:S(2)}) copy-start(bf16[2,4,512]{2,1,0:T(4,128)(2,1)} %fresh_v_ref.1) | copy-start | bytes 24580
  1.6 15.1 %copy-start.5 = (s32[2]{0:T(128)S(1)}, s32[2]{0:T(128)}, u32[]{:S(2)}) copy-start(s32[2]{0:T(128)} %length_ref.1) | copy-start | bytes 28
  1.6 22.6 %all-to-all-start = ((bf16[16,72,128]{2,1,0:T(8,128)(2,1)}), bf16[16,72,128]{2,1,0:T(8,128)(2,1)S(1)}, u32[]{:S(2)}, u32[]{:S(2)}) async-start(bf16[16,72,128]{2,1,0:T(8,128)(2,1)} %get-tuple-element.17), calls=%async_computation | async-start | bytes 589824 | tf_op jit(solution)/shard_map/all_to_all | solution.py:351
  11.8 5.0 %copy-start = (bf16[2,512,512]{2,1,0:T(8,128)(2,1)S(1)}, bf16[2,512,512]{2,1,0:T(8,128)(2,1)}, u32[]{:S(2)}) copy-start(bf16[2,512,512]{2,1,0:T(8,128)(2,1)} %k_ref.2) | copy-start | bytes 3145732
  11.8 5.0 %copy-start.1 = (bf16[2,512,512]{2,1,0:T(8,128)(2,1)S(1)}, bf16[2,512,512]{2,1,0:T(8,128)(2,1)}, u32[]{:S(2)}) copy-start(bf16[2,512,512]{2,1,0:T(8,128)(2,1)} %v_ref.2) | copy-start | bytes 3145732
  11.8 5.0 %copy-start.3 = (bf16[2,4,512]{2,1,0:T(4,128)(2,1)S(1)}, bf16[2,4,512]{2,1,0:T(4,128)(2,1)}, u32[]{:S(2)}) copy-start(bf16[2,4,512]{2,1,0:T(4,128)(2,1)} %fresh_k_ref.1) | copy-start | bytes 24580
  14.5 17.5 %collective-permute-start = (bf16[2,1024,128]{2,1,0:T(8,128)(2,1)}, bf16[2,1024,128]{2,1,0:T(8,128)(2,1)S(1)}, u32[]{:S(2)}, u32[]{:S(2)}) collective-permute-start(bf16[2,1024,128]{2,1,0:T(8,128)(2,1)} %get-tuple-element.21), channel_id=1, source_target_pairs={{0,1},{1,0},{2,3},{3,2},{4,5},{5,4},{6,7},{7,6},{8,9},{9,8},{10,11... | collective-permute-start | bytes 1572872 | tf_op jit(solution)/shard_map/ppermute | solution.py:332
  14.7 17.4 %collective-permute-start.1 = (bf16[2,1024,128]{2,1,0:T(8,128)(2,1)}, bf16[2,1024,128]{2,1,0:T(8,128)(2,1)S(1)}, u32[]{:S(2)}, u32[]{:S(2)}) collective-permute-start(bf16[2,1024,128]{2,1,0:T(8,128)(2,1)} %get-tuple-element.22), channel_id=1, source_target_pairs={{0,14},{1,3},{2,0},{3,5},{4,2},{5,7},{6,4},{7,9},{8,6},{9,11},{10,... | collective-permute-start | bytes 1572872 | tf_op jit(solution)/shard_map/ppermute | solution.py:332
  16.4 15.8 %collective-permute-start.2 = (bf16[2,1024,128]{2,1,0:T(8,128)(2,1)S(1)}, bf16[2,1024,128]{2,1,0:T(8,128)(2,1)S(1)}, u32[]{:S(2)}, u32[]{:S(2)}) collective-permute-start(bf16[2,1024,128]{2,1,0:T(8,128)(2,1)S(1)} %get-tuple-element.23), channel_id=1, source_target_pairs={{0,15},{1,2},{2,1},{3,4},{4,3},{5,6},{6,5},{7,8},{8,7},{9,10},{10,... | collective-permute-start | bytes 1572872 | tf_op jit(solution)/shard_map/ppermute | solution.py:332
  25.3 17.3 %all-to-all-start.1 = ((bf16[16,96,128]{2,1,0:T(8,128)(2,1)}), bf16[16,96,128]{2,1,0:T(8,128)(2,1)S(1)}, u32[]{:S(2)}, u32[]{:S(2)}) async-start(bf16[16,96,128]{2,1,0:T(8,128)(2,1)} %get-tuple-element.19), calls=%async_computation.1 | async-start | bytes 786432 | tf_op jit(solution)/shard_map/all_to_all | solution.py:403

commit v11 on v10

--- a/solution.py
+++ b/solution.py
@@ -97,15 +97,18 @@
     return lax.dot_general(keys, rows, (((1,), (1,)), ((), ())), preferred_element_type=jnp.float32)
 
 
-def block_attention(raw, values):
-    values = jnp.concatenate(
-        [values[first : first + HD] for first in range(0, values.shape[0], HD)], axis=1
-    )
+def block_softmax(raw):
     top = jnp.max(raw, axis=0, keepdims=True)
     probs = jnp.exp2((raw - top) * (SCALING * LOG2E))
     total = jnp.sum(probs, axis=0, keepdims=True)
-    acc = jnp.dot(values, probs.astype(jnp.bfloat16), preferred_element_type=jnp.float32)
-    return acc, top * (SCALING * LOG2E), total
+    return probs.astype(jnp.bfloat16), top * (SCALING * LOG2E), total
+
+
+def block_product(probs, values):
+    values = jnp.concatenate(
+        [values[first : first + HD] for first in range(0, values.shape[0], HD)], axis=1
+    )
+    return jnp.dot(values, probs, preferred_element_type=jnp.float32)
 
 
 def encode(out):
@@ -161,16 +164,24 @@
     starts = range(0, slots, chunk)
     stages = [(start, place) for start in starts for place in range(len(blocks))]
     rows = {start: rows_from(start) for start in starts}
-    raw, parts = block_scores(rows[0], blocks[0][0]), []
-    for number, (start, place) in enumerate(stages):
+    raw, waiting, parts = block_scores(rows[0], blocks[0][0]), None, []
+
+    def product():
+        (start, place), (probs, top, total) = waiting
+        parts.append((block_product(probs, blocks[place][1]), top, total))
+        if place + 1 == len(blocks):
+            finish(start, parts)
+            parts.clear()
+
+    for number, stage in enumerate(stages):
         ready = raw
         if number + 1 < len(stages):
             later, block = stages[number + 1]
             raw = block_scores(rows[later], blocks[block][0])
-        parts.append(block_attention(ready, blocks[place][1]))
-        if place + 1 == len(blocks):
-            finish(start, parts)
-            parts = []
+        if waiting is not None:
+            product()
+        waiting = (stage, block_softmax(ready))
+    product()
 
 
 def select_kernel(samples, slots_ref, reply_ref, chosen_ref):

time: 81.8 us -> 81.8 us (level)
  no operation moved by 1% of the time
where the time goes in v11:
time: 81.8 us; the launch traced here: 81.4 us
  blocking collectives  28.9 us (35%)
  starting transfers between devices  19.1 us (23%)
  Pallas kernels  18 us (22%)
  waiting for transfers between devices  15.2 us (19%)
    all_to_all x1, blocking collectives, local(): lax.all_to_all(chosen, 'seq', split_axis=0, concat_axis=0, tiled=True)  16.8 us
    all_to_all x1, blocking collectives, local(): lax.all_to_all(reply, 'engine', split_axis=0, concat_axis=0, tiled=True)  12.1 us
    all_to_all x1, waiting for transfers between devices, local(): lax.all_to_all(packed, 'engine', split_axis=0, concat_axis=0, tiled=True)  10.5 us
    all_to_all x1, starting transfers between devices, local(): lax.all_to_all(payload, 'seq', split_axis=0, concat_axis=0, tiled=True)  10.1 us
    pallas_call x1, Pallas kernels, local(): pl.pallas_call(functools.partial(prefix_kernel, 16), out_shape=shape((eng...  8.13 us
    all_to_all x1, starting transfers between devices, local(): lax.all_to_all(packed, 'engine', split_axis=0, concat_axis=0, tiled=True)  6.77 us
    all_to_all x1, waiting for transfers between devices, local(): lax.all_to_all(payload, 'seq', split_axis=0, concat_axis=0, tiled=True)  4.72 us
    pallas_call x1, Pallas kernels, local(): pl.pallas_call(suffix_kernel, out_shape=(shape((samples, heads * steps, H...  2.75 us
  transfers between devices with their start and end apart: 5, of which 2 were waited for; matrix products, arithmetic and copies ran while one was open for 0% of the time, Pallas kernels for 8%

profile of v11, /device:TPU:1, one launch (start us, length us, event | category | flops | bytes accessed | tf_op | source)
XLA Modules:
  0.0 81.4 jit_solution(9176681454657638899)
XLA Ops:
  0.0 1.6 %prepare.1 = (bf16[2,128,128]{2,1,0:T(8,128)(2,1)}, bf16[16,72,128]{2,1,0:T(8,128)(2,1)}) custom-call(s32[2]{0:T(128)} %bitcast.4, bf16[2,4,4096]{2,1,0:T(4,128)(2,1)} %queries_ref.1), custom_call_target="tpu_custom_call" | custom-call | tf_op jit(solution)/shard_map/prepare/pallas_call | solution.py:352
  1.6 0.0 copy-start.2
  1.6 0.0 copy-start.4
  1.6 0.0 copy-start.5
  1.6 10.1 %all-to-all-start = ((bf16[16,72,128]{2,1,0:T(8,128)(2,1)}), bf16[16,72,128]{2,1,0:T(8,128)(2,1)S(1)}, u32[]{:S(2)}, u32[]{:S(2)}) async-start(bf16[16,72,128]{2,1,0:T(8,128)(2,1)} %get-tuple-element.17), calls=%async_computation | async-start | bytes 589824 | tf_op jit(solution)/shard_map/all_to_all | solution.py:362
  11.8 0.0 copy-start
  11.8 0.0 copy-start.1
  11.8 0.0 copy-start.3
  11.8 2.8 %split.1 = (bf16[2,1024,128]{2,1,0:T(8,128)(2,1)S(1)}, bf16[2,1024,128]{2,1,0:T(8,128)(2,1)}, bf16[2,1024,128]{2,1,0:T(8,128)(2,1)}, bf16[2,1024,128]{2,1,0:T(8,128)(2,1)S(1)}) custom-call(s32[1]{0:T(128)} %bitcast.2.head_ref, bf16[1,1024,512]{2,1,0:T(8,128)(2,1)} %k_ref.3, bf16[1,1024,512]{2,1,0:T(8,128)(2,1)} %v_ref.3), custom_call_target="tpu_custom_call" | custom-call | tf_op jit(solution)/shard_map/split/pallas_call | solution.py:320
  14.5 0.2 collective-permute-start
  14.7 1.6 %collective-permute-start.1 = (bf16[2,1024,128]{2,1,0:T(8,128)(2,1)}, bf16[2,1024,128]{2,1,0:T(8,128)(2,1)S(1)}, u32[]{:S(2)}, u32[]{:S(2)}) collective-permute-start(bf16[2,1024,128]{2,1,0:T(8,128)(2,1)} %get-tuple-element.22), channel_id=1, source_target_pairs={{0,14},{1,3},{2,0},{3,5},{4,2},{5,7},{6,4},{7,9},{8,6},{9,11},{10,... | collective-permute-start | bytes 1572872 | tf_op jit(solution)/shard_map/ppermute | solution.py:343
  16.4 0.4 collective-permute-start.2
  16.8 0.0 copy-done.2
  16.8 0.0 copy-done.4
  16.8 0.0 copy-done.5
  16.8 0.0 copy-done
  16.8 0.0 copy-done.1
  16.8 0.0 copy-done.3
  16.8 2.8 %suffix.1 = (f32[2,128,128]{2,1,0:T(8,128)S(1)}, f32[2,128,128]{2,1,0:T(8,128)S(1)}) custom-call(s32[2]{0:T(128)S(1)} %copy-done.5, bf16[2,128,128]{2,1,0:T(8,128)(2,1)S(1)} %copy-done.2, bf16[2,4,512]{2,1,0:T(4,128)(2,1)S(1)} %copy-done.3, bf16[2,4,512]{2,1,0:T(4,128)(2,1)S(1)} %copy-done.4, bf16[2,512,512]{2,1,0:T(8,128)(2,1)S(1)} %copy-done, ...), custom_call_target="tpu_custom_call" | custom-call | tf_op jit(solution)/shard_map/suffix/pallas_call | solution.py:383
  19.6 4.7 %all-to-all-done.received_ref = bf16[16,72,128]{2,1,0:T(8,128)(2,1)S(1)} async-done(((bf16[16,72,128]{2,1,0:T(8,128)(2,1)}), bf16[16,72,128]{2,1,0:T(8,128)(2,1)S(1)}, u32[]{:S(2)}, u32[]{:S(2)}) %all-to-all-start) | async-done | bytes 294944 | tf_op jit(solution)/shard_map/all_to_all | solution.py:362
  24.3 1.0 %pack.1 = (bf16[16,96,128]{2,1,0:T(8,128)(2,1)}, s32[32]{0:T(128)S(1)}) custom-call(f32[2,128,128]{2,1,0:T(8,128)S(1)} %get-tuple-element.16._.suffix_log_ref, bf16[16,72,128]{2,1,0:T(8,128)(2,1)S(1)} %all-to-all-done.received_ref), custom_call_target="tpu_custom_call" | custom-call | tf_op jit(solution)/shard_map/pack/pallas_call | solution.py:402
  25.3 6.8 %all-to-all-start.1 = ((bf16[16,96,128]{2,1,0:T(8,128)(2,1)}), bf16[16,96,128]{2,1,0:T(8,128)(2,1)S(1)}, u32[]{:S(2)}, u32[]{:S(2)}) async-start(bf16[16,96,128]{2,1,0:T(8,128)(2,1)} %get-tuple-element.19), calls=%async_computation.1 | async-start | bytes 786432 | tf_op jit(solution)/shard_map/all_to_all | solution.py:414
  32.1 0.0 collective-permute-done.refs_1_
  32.1 0.0 collective-permute-done.1.refs_2_
  32.1 0.0 collective-permute-done.2.refs_3_
  32.1 10.5 %all-to-all-done.1 = bf16[16,96,128]{2,1,0:T(8,128)(2,1)S(1)} async-done(((bf16[16,96,128]{2,1,0:T(8,128)(2,1)}), bf16[16,96,128]{2,1,0:T(8,128)(2,1)S(1)}, u32[]{:S(2)}, u32[]{:S(2)}) %all-to-all-start.1) | async-done | bytes 393248 | tf_op jit(solution)/shard_map/all_to_all | solution.py:414
  42.6 8.1 %prefix.1 = s32[16,13,4,128]{3,2,1,0:T(4,128)S(1)} custom-call(bf16[48,32,128]{2,1,0:T(8,128)(2,1)S(1)} %bitcast.3, bf16[2,1024,128]{2,1,0:T(8,128)(2,1)S(1)} %get-tuple-element.20.refs_0_, bf16[2,1024,128]{2,1,0:T(8,128)(2,1)S(1)} %collective-permute-done.refs_1_, bf16[2,1024,128]{2,1,0:T(8,128)(2,1)S(1)} %collective-permute-done.1.refs_2_, ...), custom_call_target="tpu_custom_call" | custom-call | tf_op jit(solution)/shard_map/prefix/pallas_call | solution.py:416
  50.8 12.1 %all_to_all.20.reply_ref = s32[16,13,4,128]{3,2,1,0:T(4,128)S(1)} all-to-all(s32[16,13,4,128]{3,2,1,0:T(4,128)S(1)} %prefix.1), channel_id=1, replica_groups=mesh['engine'=16,'seq'=16] {'engine'}, dimensions={0} | all-to-all | bytes 851968 | tf_op jit(solution)/shard_map/all_to_all | solution.py:427
  62.8 0.6 select.3
  63.5 16.8 %all_to_all.21.chosen_ref = s32[16,9,4,128]{3,2,1,0:T(4,128)S(1)} all-to-all(s32[16,9,4,128]{3,2,1,0:T(4,128)S(1)} %select.3), channel_id=1, replica_groups=mesh['engine'=16,'seq'=16] {'seq'}, dimensions={0} | all-to-all | bytes 589824 | tf_op jit(solution)/shard_map/all_to_all | solution.py:437
  80.3 1.1 %combine.1 = bf16[2,4,4096]{2,1,0:T(4,128)(2,1)} custom-call(s32[16,9,4,128]{3,2,1,0:T(4,128)S(1)} %all_to_all.21.chosen_ref, f32[2,128,128]{2,1,0:T(8,128)S(1)} %get-tuple-element.24.suffix_out_ref, f32[2,128,128]{2,1,0:T(8,128)S(1)} %get-tuple-element.16._.suffix_log_ref), custom_call_target="tpu_custom_call" | custom-call | tf_op jit(solution)/shard_map/combine/pallas_call | solution.py:439
Async XLA Ops:
  1.6 15.1 %copy-start.2 = (bf16[2,128,128]{2,1,0:T(8,128)(2,1)S(1)}, bf16[2,128,128]{2,1,0:T(8,128)(2,1)}, u32[]{:S(2)}) copy-start(bf16[2,128,128]{2,1,0:T(8,128)(2,1)} %get-tuple-element.15.rows_ref) | copy-start | bytes 196612
  1.6 15.1 %copy-start.4 = (bf16[2,4,512]{2,1,0:T(4,128)(2,1)S(1)}, bf16[2,4,512]{2,1,0:T(4,128)(2,1)}, u32[]{:S(2)}) copy-start(bf16[2,4,512]{2,1,0:T(4,128)(2,1)} %fresh_v_ref.1) | copy-start | bytes 24580
  1.6 15.1 %copy-start.5 = (s32[2]{0:T(128)S(1)}, s32[2]{0:T(128)}, u32[]{:S(2)}) copy-start(s32[2]{0:T(128)} %length_ref.1) | copy-start | bytes 28
  1.6 22.6 %all-to-all-start = ((bf16[16,72,128]{2,1,0:T(8,128)(2,1)}), bf16[16,72,128]{2,1,0:T(8,128)(2,1)S(1)}, u32[]{:S(2)}, u32[]{:S(2)}) async-start(bf16[16,72,128]{2,1,0:T(8,128)(2,1)} %get-tuple-element.17), calls=%async_computation | async-start | bytes 589824 | tf_op jit(solution)/shard_map/all_to_all | solution.py:362
  11.8 5.0 %copy-start = (bf16[2,512,512]{2,1,0:T(8,128)(2,1)S(1)}, bf16[2,512,512]{2,1,0:T(8,128)(2,1)}, u32[]{:S(2)}) copy-start(bf16[2,512,512]{2,1,0:T(8,128)(2,1)} %k_ref.2) | copy-start | bytes 3145732
  11.8 5.0 %copy-start.1 = (bf16[2,512,512]{2,1,0:T(8,128)(2,1)S(1)}, bf16[2,512,512]{2,1,0:T(8,128)(2,1)}, u32[]{:S(2)}) copy-start(bf16[2,512,512]{2,1,0:T(8,128)(2,1)} %v_ref.2) | copy-start | bytes 3145732
  11.8 5.0 %copy-start.3 = (bf16[2,4,512]{2,1,0:T(4,128)(2,1)S(1)}, bf16[2,4,512]{2,1,0:T(4,128)(2,1)}, u32[]{:S(2)}) copy-start(bf16[2,4,512]{2,1,0:T(4,128)(2,1)} %fresh_k_ref.1) | copy-start | bytes 24580
  14.5 17.5 %collective-permute-start = (bf16[2,1024,128]{2,1,0:T(8,128)(2,1)}, bf16[2,1024,128]{2,1,0:T(8,128)(2,1)S(1)}, u32[]{:S(2)}, u32[]{:S(2)}) collective-permute-start(bf16[2,1024,128]{2,1,0:T(8,128)(2,1)} %get-tuple-element.21), channel_id=1, source_target_pairs={{0,1},{1,0},{2,3},{3,2},{4,5},{5,4},{6,7},{7,6},{8,9},{9,8},{10,11... | collective-permute-start | bytes 1572872 | tf_op jit(solution)/shard_map/ppermute | solution.py:343
  14.7 17.4 %collective-permute-start.1 = (bf16[2,1024,128]{2,1,0:T(8,128)(2,1)}, bf16[2,1024,128]{2,1,0:T(8,128)(2,1)S(1)}, u32[]{:S(2)}, u32[]{:S(2)}) collective-permute-start(bf16[2,1024,128]{2,1,0:T(8,128)(2,1)} %get-tuple-element.22), channel_id=1, source_target_pairs={{0,14},{1,3},{2,0},{3,5},{4,2},{5,7},{6,4},{7,9},{8,6},{9,11},{10,... | collective-permute-start | bytes 1572872 | tf_op jit(solution)/shard_map/ppermute | solution.py:343
  16.4 15.8 %collective-permute-start.2 = (bf16[2,1024,128]{2,1,0:T(8,128)(2,1)S(1)}, bf16[2,1024,128]{2,1,0:T(8,128)(2,1)S(1)}, u32[]{:S(2)}, u32[]{:S(2)}) collective-permute-start(bf16[2,1024,128]{2,1,0:T(8,128)(2,1)S(1)} %get-tuple-element.23), channel_id=1, source_target_pairs={{0,15},{1,2},{2,1},{3,4},{4,3},{5,6},{6,5},{7,8},{8,7},{9,10},{10,... | collective-permute-start | bytes 1572872 | tf_op jit(solution)/shard_map/ppermute | solution.py:343
  25.3 17.3 %all-to-all-start.1 = ((bf16[16,96,128]{2,1,0:T(8,128)(2,1)}), bf16[16,96,128]{2,1,0:T(8,128)(2,1)S(1)}, u32[]{:S(2)}, u32[]{:S(2)}) async-start(bf16[16,96,128]{2,1,0:T(8,128)(2,1)} %get-tuple-element.19), calls=%async_computation.1 | async-start | bytes 786432 | tf_op jit(solution)/shard_map/all_to_all | solution.py:414

commit v12 on v11

--- a/solution.py
+++ b/solution.py
@@ -98,10 +98,10 @@
 
 
 def block_softmax(raw):
-    top = jnp.max(raw, axis=0, keepdims=True)
-    probs = jnp.exp2((raw - top) * (SCALING * LOG2E))
+    top = jnp.max(raw, axis=0, keepdims=True) * (SCALING * LOG2E)
+    probs = jnp.exp2(raw * (SCALING * LOG2E) - top)
     total = jnp.sum(probs, axis=0, keepdims=True)
-    return probs.astype(jnp.bfloat16), top * (SCALING * LOG2E), total
+    return probs.astype(jnp.bfloat16), top, total
 
 
 def block_product(probs, values):

time: 81.8 us -> 82.5 us (level)
  no operation moved by 1% of the time
where the time goes in v12:
time: 82.5 us; the launch traced here: 82 us
  blocking collectives  28.9 us (35%)
  starting transfers between devices  19.1 us (23%)
  Pallas kernels  18.7 us (23%)
  waiting for transfers between devices  15.2 us (18%)
    all_to_all x1, blocking collectives, local(): lax.all_to_all(chosen, 'seq', split_axis=0, concat_axis=0, tiled=True)  16.9 us
    all_to_all x1, blocking collectives, local(): lax.all_to_all(reply, 'engine', split_axis=0, concat_axis=0, tiled=True)  12 us
    all_to_all x1, waiting for transfers between devices, local(): lax.all_to_all(packed, 'engine', split_axis=0, concat_axis=0, tiled=True)  10.5 us
    all_to_all x1, starting transfers between devices, local(): lax.all_to_all(payload, 'seq', split_axis=0, concat_axis=0, tiled=True)  10.1 us
    pallas_call x1, Pallas kernels, local(): pl.pallas_call(functools.partial(prefix_kernel, 16), out_shape=shape((eng...  8.75 us
    all_to_all x1, starting transfers between devices, local(): lax.all_to_all(packed, 'engine', split_axis=0, concat_axis=0, tiled=True)  6.77 us
    all_to_all x1, waiting for transfers between devices, local(): lax.all_to_all(payload, 'seq', split_axis=0, concat_axis=0, tiled=True)  4.72 us
    pallas_call x1, Pallas kernels, local(): pl.pallas_call(suffix_kernel, out_shape=(shape((samples, heads * steps, H...  2.75 us
  transfers between devices with their start and end apart: 5, of which 2 were waited for; matrix products, arithmetic and copies ran while one was open for 0% of the time, Pallas kernels for 8%

profile of v12, /device:TPU:1, one launch (start us, length us, event | category | flops | bytes accessed | tf_op | source)
XLA Modules:
  0.0 82.0 jit_solution(8326231235752463896)
XLA Ops:
  0.0 1.6 %prepare.1 = (bf16[2,128,128]{2,1,0:T(8,128)(2,1)}, bf16[16,72,128]{2,1,0:T(8,128)(2,1)}) custom-call(s32[2]{0:T(128)} %bitcast.4, bf16[2,4,4096]{2,1,0:T(4,128)(2,1)} %queries_ref.1), custom_call_target="tpu_custom_call" | custom-call | tf_op jit(solution)/shard_map/prepare/pallas_call | solution.py:352
  1.6 0.0 copy-start.2
  1.6 0.0 copy-start.4
  1.6 0.0 copy-start.5
  1.6 10.1 %all-to-all-start = ((bf16[16,72,128]{2,1,0:T(8,128)(2,1)}), bf16[16,72,128]{2,1,0:T(8,128)(2,1)S(1)}, u32[]{:S(2)}, u32[]{:S(2)}) async-start(bf16[16,72,128]{2,1,0:T(8,128)(2,1)} %get-tuple-element.17), calls=%async_computation | async-start | bytes 589824 | tf_op jit(solution)/shard_map/all_to_all | solution.py:362
  11.8 0.0 copy-start
  11.8 0.0 copy-start.1
  11.8 0.0 copy-start.3
  11.8 2.8 %split.1 = (bf16[2,1024,128]{2,1,0:T(8,128)(2,1)S(1)}, bf16[2,1024,128]{2,1,0:T(8,128)(2,1)}, bf16[2,1024,128]{2,1,0:T(8,128)(2,1)}, bf16[2,1024,128]{2,1,0:T(8,128)(2,1)S(1)}) custom-call(s32[1]{0:T(128)} %bitcast.2.head_ref, bf16[1,1024,512]{2,1,0:T(8,128)(2,1)} %k_ref.3, bf16[1,1024,512]{2,1,0:T(8,128)(2,1)} %v_ref.3), custom_call_target="tpu_custom_call" | custom-call | tf_op jit(solution)/shard_map/split/pallas_call | solution.py:320
  14.5 0.2 collective-permute-start
  14.7 1.6 %collective-permute-start.1 = (bf16[2,1024,128]{2,1,0:T(8,128)(2,1)}, bf16[2,1024,128]{2,1,0:T(8,128)(2,1)S(1)}, u32[]{:S(2)}, u32[]{:S(2)}) collective-permute-start(bf16[2,1024,128]{2,1,0:T(8,128)(2,1)} %get-tuple-element.22), channel_id=1, source_target_pairs={{0,14},{1,3},{2,0},{3,5},{4,2},{5,7},{6,4},{7,9},{8,6},{9,11},{10,... | collective-permute-start | bytes 1572872 | tf_op jit(solution)/shard_map/ppermute | solution.py:343
  16.4 0.4 collective-permute-start.2
  16.8 0.0 copy-done.2
  16.8 0.0 copy-done.4
  16.8 0.0 copy-done.5
  16.8 0.0 copy-done
  16.8 0.0 copy-done.1
  16.8 0.0 copy-done.3
  16.8 2.8 %suffix.1 = (f32[2,128,128]{2,1,0:T(8,128)S(1)}, f32[2,128,128]{2,1,0:T(8,128)S(1)}) custom-call(s32[2]{0:T(128)S(1)} %copy-done.5, bf16[2,128,128]{2,1,0:T(8,128)(2,1)S(1)} %copy-done.2, bf16[2,4,512]{2,1,0:T(4,128)(2,1)S(1)} %copy-done.3, bf16[2,4,512]{2,1,0:T(4,128)(2,1)S(1)} %copy-done.4, bf16[2,512,512]{2,1,0:T(8,128)(2,1)S(1)} %copy-done, ...), custom_call_target="tpu_custom_call" | custom-call | tf_op jit(solution)/shard_map/suffix/pallas_call | solution.py:383
  19.6 4.7 %all-to-all-done.received_ref = bf16[16,72,128]{2,1,0:T(8,128)(2,1)S(1)} async-done(((bf16[16,72,128]{2,1,0:T(8,128)(2,1)}), bf16[16,72,128]{2,1,0:T(8,128)(2,1)S(1)}, u32[]{:S(2)}, u32[]{:S(2)}) %all-to-all-start) | async-done | bytes 294944 | tf_op jit(solution)/shard_map/all_to_all | solution.py:362
  24.3 1.0 %pack.1 = (bf16[16,96,128]{2,1,0:T(8,128)(2,1)}, s32[32]{0:T(128)S(1)}) custom-call(f32[2,128,128]{2,1,0:T(8,128)S(1)} %get-tuple-element.16._.suffix_log_ref, bf16[16,72,128]{2,1,0:T(8,128)(2,1)S(1)} %all-to-all-done.received_ref), custom_call_target="tpu_custom_call" | custom-call | tf_op jit(solution)/shard_map/pack/pallas_call | solution.py:402
  25.3 6.8 %all-to-all-start.1 = ((bf16[16,96,128]{2,1,0:T(8,128)(2,1)}), bf16[16,96,128]{2,1,0:T(8,128)(2,1)S(1)}, u32[]{:S(2)}, u32[]{:S(2)}) async-start(bf16[16,96,128]{2,1,0:T(8,128)(2,1)} %get-tuple-element.19), calls=%async_computation.1 | async-start | bytes 786432 | tf_op jit(solution)/shard_map/all_to_all | solution.py:414
  32.1 0.0 collective-permute-done.refs_1_
  32.1 0.0 collective-permute-done.1.refs_2_
  32.1 0.0 collective-permute-done.2.refs_3_
  32.1 10.5 %all-to-all-done.1 = bf16[16,96,128]{2,1,0:T(8,128)(2,1)S(1)} async-done(((bf16[16,96,128]{2,1,0:T(8,128)(2,1)}), bf16[16,96,128]{2,1,0:T(8,128)(2,1)S(1)}, u32[]{:S(2)}, u32[]{:S(2)}) %all-to-all-start.1) | async-done | bytes 393248 | tf_op jit(solution)/shard_map/all_to_all | solution.py:414
  42.6 8.8 %prefix.1 = s32[16,13,4,128]{3,2,1,0:T(4,128)S(1)} custom-call(bf16[48,32,128]{2,1,0:T(8,128)(2,1)S(1)} %bitcast.3, bf16[2,1024,128]{2,1,0:T(8,128)(2,1)S(1)} %get-tuple-element.20.refs_0_, bf16[2,1024,128]{2,1,0:T(8,128)(2,1)S(1)} %collective-permute-done.refs_1_, bf16[2,1024,128]{2,1,0:T(8,128)(2,1)S(1)} %collective-permute-done.1.refs_2_, ...), custom_call_target="tpu_custom_call" | custom-call | tf_op jit(solution)/shard_map/prefix/pallas_call | solution.py:416
  51.4 12.0 %all_to_all.20.reply_ref = s32[16,13,4,128]{3,2,1,0:T(4,128)S(1)} all-to-all(s32[16,13,4,128]{3,2,1,0:T(4,128)S(1)} %prefix.1), channel_id=1, replica_groups=mesh['engine'=16,'seq'=16] {'engine'}, dimensions={0} | all-to-all | bytes 851968 | tf_op jit(solution)/shard_map/all_to_all | solution.py:427
  63.4 0.6 select.3
  64.0 16.9 %all_to_all.21.chosen_ref = s32[16,9,4,128]{3,2,1,0:T(4,128)S(1)} all-to-all(s32[16,9,4,128]{3,2,1,0:T(4,128)S(1)} %select.3), channel_id=1, replica_groups=mesh['engine'=16,'seq'=16] {'seq'}, dimensions={0} | all-to-all | bytes 589824 | tf_op jit(solution)/shard_map/all_to_all | solution.py:437
  80.9 1.1 %combine.1 = bf16[2,4,4096]{2,1,0:T(4,128)(2,1)} custom-call(s32[16,9,4,128]{3,2,1,0:T(4,128)S(1)} %all_to_all.21.chosen_ref, f32[2,128,128]{2,1,0:T(8,128)S(1)} %get-tuple-element.24.suffix_out_ref, f32[2,128,128]{2,1,0:T(8,128)S(1)} %get-tuple-element.16._.suffix_log_ref), custom_call_target="tpu_custom_call" | custom-call | tf_op jit(solution)/shard_map/combine/pallas_call | solution.py:439
Async XLA Ops:
  1.6 15.1 %copy-start.2 = (bf16[2,128,128]{2,1,0:T(8,128)(2,1)S(1)}, bf16[2,128,128]{2,1,0:T(8,128)(2,1)}, u32[]{:S(2)}) copy-start(bf16[2,128,128]{2,1,0:T(8,128)(2,1)} %get-tuple-element.15.rows_ref) | copy-start | bytes 196612
  1.6 15.1 %copy-start.4 = (bf16[2,4,512]{2,1,0:T(4,128)(2,1)S(1)}, bf16[2,4,512]{2,1,0:T(4,128)(2,1)}, u32[]{:S(2)}) copy-start(bf16[2,4,512]{2,1,0:T(4,128)(2,1)} %fresh_v_ref.1) | copy-start | bytes 24580
  1.6 15.1 %copy-start.5 = (s32[2]{0:T(128)S(1)}, s32[2]{0:T(128)}, u32[]{:S(2)}) copy-start(s32[2]{0:T(128)} %length_ref.1) | copy-start | bytes 28
  1.6 22.6 %all-to-all-start = ((bf16[16,72,128]{2,1,0:T(8,128)(2,1)}), bf16[16,72,128]{2,1,0:T(8,128)(2,1)S(1)}, u32[]{:S(2)}, u32[]{:S(2)}) async-start(bf16[16,72,128]{2,1,0:T(8,128)(2,1)} %get-tuple-element.17), calls=%async_computation | async-start | bytes 589824 | tf_op jit(solution)/shard_map/all_to_all | solution.py:362
  11.8 5.0 %copy-start = (bf16[2,512,512]{2,1,0:T(8,128)(2,1)S(1)}, bf16[2,512,512]{2,1,0:T(8,128)(2,1)}, u32[]{:S(2)}) copy-start(bf16[2,512,512]{2,1,0:T(8,128)(2,1)} %k_ref.2) | copy-start | bytes 3145732
  11.8 5.0 %copy-start.1 = (bf16[2,512,512]{2,1,0:T(8,128)(2,1)S(1)}, bf16[2,512,512]{2,1,0:T(8,128)(2,1)}, u32[]{:S(2)}) copy-start(bf16[2,512,512]{2,1,0:T(8,128)(2,1)} %v_ref.2) | copy-start | bytes 3145732
  11.8 5.0 %copy-start.3 = (bf16[2,4,512]{2,1,0:T(4,128)(2,1)S(1)}, bf16[2,4,512]{2,1,0:T(4,128)(2,1)}, u32[]{:S(2)}) copy-start(bf16[2,4,512]{2,1,0:T(4,128)(2,1)} %fresh_k_ref.1) | copy-start | bytes 24580
  14.5 17.6 %collective-permute-start = (bf16[2,1024,128]{2,1,0:T(8,128)(2,1)}, bf16[2,1024,128]{2,1,0:T(8,128)(2,1)S(1)}, u32[]{:S(2)}, u32[]{:S(2)}) collective-permute-start(bf16[2,1024,128]{2,1,0:T(8,128)(2,1)} %get-tuple-element.21), channel_id=1, source_target_pairs={{0,1},{1,0},{2,3},{3,2},{4,5},{5,4},{6,7},{7,6},{8,9},{9,8},{10,11... | collective-permute-start | bytes 1572872 | tf_op jit(solution)/shard_map/ppermute | solution.py:343
  14.7 17.4 %collective-permute-start.1 = (bf16[2,1024,128]{2,1,0:T(8,128)(2,1)}, bf16[2,1024,128]{2,1,0:T(8,128)(2,1)S(1)}, u32[]{:S(2)}, u32[]{:S(2)}) collective-permute-start(bf16[2,1024,128]{2,1,0:T(8,128)(2,1)} %get-tuple-element.22), channel_id=1, source_target_pairs={{0,14},{1,3},{2,0},{3,5},{4,2},{5,7},{6,4},{7,9},{8,6},{9,11},{10,... | collective-permute-start | bytes 1572872 | tf_op jit(solution)/shard_map/ppermute | solution.py:343
  16.4 15.8 %collective-permute-start.2 = (bf16[2,1024,128]{2,1,0:T(8,128)(2,1)S(1)}, bf16[2,1024,128]{2,1,0:T(8,128)(2,1)S(1)}, u32[]{:S(2)}, u32[]{:S(2)}) collective-permute-start(bf16[2,1024,128]{2,1,0:T(8,128)(2,1)S(1)} %get-tuple-element.23), channel_id=1, source_target_pairs={{0,15},{1,2},{2,1},{3,4},{4,3},{5,6},{6,5},{7,8},{8,7},{9,10},{10,... | collective-permute-start | bytes 1572872 | tf_op jit(solution)/shard_map/ppermute | solution.py:343
  25.3 17.3 %all-to-all-start.1 = ((bf16[16,96,128]{2,1,0:T(8,128)(2,1)}), bf16[16,96,128]{2,1,0:T(8,128)(2,1)S(1)}, u32[]{:S(2)}, u32[]{:S(2)}) async-start(bf16[16,96,128]{2,1,0:T(8,128)(2,1)} %get-tuple-element.19), calls=%async_computation.1 | async-start | bytes 786432 | tf_op jit(solution)/shard_map/all_to_all | solution.py:414

commit v13 on v11

--- a/solution.py
+++ b/solution.py
@@ -55,7 +55,7 @@
         payload_ref[place, samples * part :] = note
 
 
-def split_kernel(head_ref, k_ref, v_ref, *refs):
+def split_kernel(_, head_ref, k_ref, v_ref, *refs):
     outs, held, sems = refs[:KVH], refs[KVH], refs[KVH + 1]
     copies = []
     for place, out in enumerate(outs):
@@ -316,39 +316,6 @@
     engine_count = lax.axis_size("engine")
     positions = prefix_keys.shape[1]
 
-    head_id = lax.rem(lax.axis_index("seq"), KVH).reshape(1)
-    heads_of_block = pl.pallas_call(
-        split_kernel,
-        out_shape=[shape((2, positions, HD), jnp.bfloat16)] * KVH,
-        in_specs=[SMEM] + [pl.BlockSpec(memory_space=pltpu.HBM)] * 2,
-        out_specs=[VMEM] * KVH,
-        scratch_shapes=[
-            pltpu.VMEM((KVH, positions, HD), jnp.bfloat16),
-            pltpu.SemaphoreType.DMA((KVH, 2)),
-        ],
-        compiler_params=params(16),
-        name="split",
-    )(
-        head_id,
-        pltpu.with_memory_space_constraint(prefix_keys, pltpu.HBM),
-        pltpu.with_memory_space_constraint(prefix_values, pltpu.HBM),
-    )
-
-    def swap(array, near, swapped):
-        pairs = []
-        for place in range(seq_count):
-            chip, core = place // 2, place % 2
-            chip = (chip + near * (2 * core - 1)) % (seq_count // 2)
-            pairs.append((place, 2 * chip + (1 - core if swapped else core)))
-        return lax.ppermute(array, "seq", pairs)
-
-    blocks = [
-        heads_of_block[0],
-        swap(heads_of_block[1], 0, True),
-        swap(heads_of_block[2], 1, False),
-        swap(heads_of_block[3], 1, True),
-    ]
-
     rows, payload = pl.pallas_call(
         prepare_kernel,
         out_shape=(
@@ -399,6 +366,41 @@
         suffix_values,
     )
 
+    head_id = lax.rem(lax.axis_index("seq"), KVH).reshape(1)
+    heads_of_block = pl.pallas_call(
+        split_kernel,
+        out_shape=[shape((2, positions, HD), jnp.bfloat16)] * KVH,
+        in_specs=[pl.BlockSpec(memory_space=pl.ANY), SMEM]
+        + [pl.BlockSpec(memory_space=pltpu.HBM)] * 2,
+        out_specs=[VMEM] * KVH,
+        scratch_shapes=[
+            pltpu.VMEM((KVH, positions, HD), jnp.bfloat16),
+            pltpu.SemaphoreType.DMA((KVH, 2)),
+        ],
+        compiler_params=params(16),
+        name="split",
+    )(
+        suffix_log,
+        head_id,
+        pltpu.with_memory_space_constraint(prefix_keys, pltpu.HBM),
+        pltpu.with_memory_space_constraint(prefix_values, pltpu.HBM),
+    )
+
+    def swap(array, near, swapped):
+        pairs = []
+        for place in range(seq_count):
+            chip, core = place // 2, place % 2
+            chip = (chip + near * (2 * core - 1)) % (seq_count // 2)
+            pairs.append((place, 2 * chip + (1 - core if swapped else core)))
+        return lax.ppermute(array, "seq", pairs)
+
+    blocks = [
+        heads_of_block[0],
+        swap(heads_of_block[1], 0, True),
+        swap(heads_of_block[2], 1, False),
+        swap(heads_of_block[3], 1, True),
+    ]
+
     packed, slots = pl.pallas_call(
         functools.partial(pack_kernel, samples),
         out_shape=(
@@ -410,7 +412,7 @@
         scratch_shapes=[pltpu.SMEM((engine_count,), jnp.int32)],
         compiler_params=params(16),
         name="pack",
-    )(suffix_log, received)
+    )(heads_of_block[0], received)
     dispatched = lax.all_to_all(packed, "engine", split_axis=0, concat_axis=0, tiled=True)
 
     reply = pl.pallas_call(

time: 81.8 us -> 83.3 us (1.018)
  waiting for transfers between devices: 15.2 us -> 11.6 us
  local copies, waits for them, and re-layouts: 0.03 us -> 3.13 us
  blocking collectives: 28.9 us -> 30.9 us
    all_to_all x1, waiting for transfers between devices: 10.5 us -> 6.47 us  [local(): lax.all_to_all(packed, 'engine', split_axis=0, concat_axis=0, tiled=True)]
    ppermute x3, waiting for transfers between devices: 0.04 us -> 3.57 us  [swap(): return lax.ppermute(array, 'seq', pairs)]
    all_to_all x1, waiting for transfers between devices: 4.72 us -> 1.59 us  [local(): lax.all_to_all(payload, 'seq', split_axis=0, concat_axis=0, tiled=True)]
    unnamed x12, local copies, waits for them, and re-layouts: 0.03 us -> 3.13 us
    all_to_all x1, blocking collectives: 16.8 us -> 18.6 us  [local(): lax.all_to_all(chosen, 'seq', split_axis=0, concat_axis=0, tiled=True)]
  transfers between devices with their start and end apart: 5 -> 5, of which waited for: 2 -> 3; matrix products, arithmetic and copies ran while one was open for 0% -> 0% of each run, Pallas kernels for 8% -> 8%
where the time goes in v13:
time: 83.3 us; the launch traced here: 82.7 us
  blocking collectives  30.9 us (37%)
  starting transfers between devices  19.1 us (23%)
  Pallas kernels  17.9 us (21%)
  waiting for transfers between devices  11.6 us (14%)
  local copies, waits for them, and re-layouts  3.13 us (4%)
    all_to_all x1, blocking collectives, local(): lax.all_to_all(chosen, 'seq', split_axis=0, concat_axis=0, tiled=True)  18.6 us
    all_to_all x1, blocking collectives, local(): lax.all_to_all(reply, 'engine', split_axis=0, concat_axis=0, tiled=True)  12.3 us
    all_to_all x1, starting transfers between devices, local(): lax.all_to_all(payload, 'seq', split_axis=0, concat_axis=0, tiled=True)  10.1 us
    pallas_call x1, Pallas kernels, local(): pl.pallas_call(functools.partial(prefix_kernel, 16), out_shape=shape((eng...  8.09 us
    all_to_all x1, starting transfers between devices, local(): lax.all_to_all(packed, 'engine', split_axis=0, concat_axis=0, tiled=True)  6.77 us
    all_to_all x1, waiting for transfers between devices, local(): lax.all_to_all(packed, 'engine', split_axis=0, concat_axis=0, tiled=True)  6.47 us
    ppermute x3, waiting for transfers between devices, swap(): return lax.ppermute(array, 'seq', pairs)  3.57 us
    unnamed x12, local copies, waits for them, and re-layouts  3.13 us
  transfers between devices with their start and end apart: 5, of which 3 were waited for; matrix products, arithmetic and copies ran while one was open for 0% of the time, Pallas kernels for 8%

profile of v13, /device:TPU:1, one launch (start us, length us, event | category | flops | bytes accessed | tf_op | source)
XLA Modules:
  0.0 82.7 jit_solution(6657410004251904410)
XLA Ops:
  0.0 1.6 %prepare.1 = (bf16[2,128,128]{2,1,0:T(8,128)(2,1)}, bf16[16,72,128]{2,1,0:T(8,128)(2,1)}) custom-call(s32[2]{0:T(128)} %bitcast.4, bf16[2,4,4096]{2,1,0:T(4,128)(2,1)} %queries_ref.1), custom_call_target="tpu_custom_call" | custom-call | tf_op jit(solution)/shard_map/prepare/pallas_call | solution.py:319
  1.6 0.0 copy-start.2
  1.6 10.1 %all-to-all-start = ((bf16[16,72,128]{2,1,0:T(8,128)(2,1)}), bf16[16,72,128]{2,1,0:T(8,128)(2,1)S(1)}, u32[]{:S(2)}, u32[]{:S(2)}) async-start(bf16[16,72,128]{2,1,0:T(8,128)(2,1)} %get-tuple-element.18), calls=%async_computation | async-start | bytes 589824 | tf_op jit(solution)/shard_map/all_to_all | solution.py:329
  11.7 0.0 copy-start.4
  11.8 0.0 copy-start.3
  11.8 0.0 copy-start.5
  11.8 0.0 copy-done.2
  11.8 0.7 copy-done.4
  12.4 0.0 copy-done.3
  12.5 0.0 copy-done.5
  12.5 0.0 copy-start
  12.5 1.2 %copy-done = bf16[2,512,512]{2,1,0:T(8,128)(2,1)S(1)} copy-done((bf16[2,512,512]{2,1,0:T(8,128)(2,1)S(1)}, bf16[2,512,512]{2,1,0:T(8,128)(2,1)}, u32[]{:S(2)}) %copy-start) | copy-done | bytes 1048600
  13.7 0.0 copy-start.1
  13.7 1.2 %copy-done.1 = bf16[2,512,512]{2,1,0:T(8,128)(2,1)S(1)} copy-done((bf16[2,512,512]{2,1,0:T(8,128)(2,1)S(1)}, bf16[2,512,512]{2,1,0:T(8,128)(2,1)}, u32[]{:S(2)}) %copy-start.1) | copy-done | bytes 1048600
  14.9 2.8 %suffix.1 = (f32[2,128,128]{2,1,0:T(8,128)S(1)}, f32[2,128,128]{2,1,0:T(8,128)S(1)}) custom-call(s32[2]{0:T(128)S(1)} %copy-done.5, bf16[2,128,128]{2,1,0:T(8,128)(2,1)S(1)} %copy-done.2, bf16[2,4,512]{2,1,0:T(4,128)(2,1)S(1)} %copy-done.3, bf16[2,4,512]{2,1,0:T(4,128)(2,1)S(1)} %copy-done.4, bf16[2,512,512]{2,1,0:T(8,128)(2,1)S(1)} %copy-done, ...), custom_call_target="tpu_custom_call" | custom-call | tf_op jit(solution)/shard_map/suffix/pallas_call | solution.py:350
  17.7 2.6 %split.1 = (bf16[2,1024,128]{2,1,0:T(8,128)(2,1)S(1)}, bf16[2,1024,128]{2,1,0:T(8,128)(2,1)}, bf16[2,1024,128]{2,1,0:T(8,128)(2,1)}, bf16[2,1024,128]{2,1,0:T(8,128)(2,1)S(1)}) custom-call(f32[2,128,128]{2,1,0:T(8,128)S(1)} %get-tuple-element.16._.suffix_log_ref, s32[1]{0:T(128)} %bitcast.1.head_ref, bf16[1,1024,512]{2,1,0:T(8,128)(2,1)} %k_ref.3, ...), custom_call_target="tpu_custom_call" | custom-call | tf_op jit(solution)/shard_map/split/pallas_call | solution.py:370
  20.3 0.2 collective-permute-start
  20.5 1.6 %collective-permute-start.1 = (bf16[2,1024,128]{2,1,0:T(8,128)(2,1)}, bf16[2,1024,128]{2,1,0:T(8,128)(2,1)S(1)}, u32[]{:S(2)}, u32[]{:S(2)}) collective-permute-start(bf16[2,1024,128]{2,1,0:T(8,128)(2,1)} %get-tuple-element.22), channel_id=1, source_target_pairs={{0,14},{1,3},{2,0},{3,5},{4,2},{5,7},{6,4},{7,9},{8,6},{9,11},{10,... | collective-permute-start | bytes 1572872 | tf_op jit(solution)/shard_map/ppermute | solution.py:395
  22.1 0.4 collective-permute-start.2
  22.5 1.6 %all-to-all-done.received_ref = bf16[16,72,128]{2,1,0:T(8,128)(2,1)S(1)} async-done(((bf16[16,72,128]{2,1,0:T(8,128)(2,1)}), bf16[16,72,128]{2,1,0:T(8,128)(2,1)S(1)}, u32[]{:S(2)}, u32[]{:S(2)}) %all-to-all-start) | async-done | bytes 294944 | tf_op jit(solution)/shard_map/all_to_all | solution.py:329
  24.1 1.0 %pack.1 = (bf16[16,96,128]{2,1,0:T(8,128)(2,1)}, s32[32]{0:T(128)S(1)}) custom-call(bf16[2,1024,128]{2,1,0:T(8,128)(2,1)S(1)} %get-tuple-element.17._.refs_0_, bf16[16,72,128]{2,1,0:T(8,128)(2,1)S(1)} %all-to-all-done.received_ref), custom_call_target="tpu_custom_call" | custom-call | tf_op jit(solution)/shard_map/pack/pallas_call | solution.py:404
  25.1 6.8 %all-to-all-start.1 = ((bf16[16,96,128]{2,1,0:T(8,128)(2,1)}), bf16[16,96,128]{2,1,0:T(8,128)(2,1)S(1)}, u32[]{:S(2)}, u32[]{:S(2)}) async-start(bf16[16,96,128]{2,1,0:T(8,128)(2,1)} %get-tuple-element.20), calls=%async_computation.1 | async-start | bytes 786432 | tf_op jit(solution)/shard_map/all_to_all | solution.py:416
  31.9 0.0 collective-permute-done.refs_1_
  31.9 0.0 collective-permute-done.1.refs_2_
  31.9 3.6 %collective-permute-done.2.refs_3_ = bf16[2,1024,128]{2,1,0:T(8,128)(2,1)S(1)} collective-permute-done((bf16[2,1024,128]{2,1,0:T(8,128)(2,1)S(1)}, bf16[2,1024,128]{2,1,0:T(8,128)(2,1)S(1)}, u32[]{:S(2)}, u32[]{:S(2)}) %collective-permute-start.2) | collective-permute-done | bytes 524320 | tf_op jit(solution)/shard_map/ppermute | solution.py:395
  35.5 6.5 %all-to-all-done.1 = bf16[16,96,128]{2,1,0:T(8,128)(2,1)S(1)} async-done(((bf16[16,96,128]{2,1,0:T(8,128)(2,1)}), bf16[16,96,128]{2,1,0:T(8,128)(2,1)S(1)}, u32[]{:S(2)}, u32[]{:S(2)}) %all-to-all-start.1) | async-done | bytes 393248 | tf_op jit(solution)/shard_map/all_to_all | solution.py:416
  42.0 8.1 %prefix.1 = s32[16,13,4,128]{3,2,1,0:T(4,128)S(1)} custom-call(bf16[48,32,128]{2,1,0:T(8,128)(2,1)S(1)} %bitcast.3, bf16[2,1024,128]{2,1,0:T(8,128)(2,1)S(1)} %get-tuple-element.17._.refs_0_, bf16[2,1024,128]{2,1,0:T(8,128)(2,1)S(1)} %collective-permute-done.refs_1_, bf16[2,1024,128]{2,1,0:T(8,128)(2,1)S(1)} %collective-permute-done.1.refs_2_, ...), custom_call_target="tpu_custom_call" | custom-call | tf_op jit(solution)/shard_map/prefix/pallas_call | solution.py:418
  50.1 12.3 %all_to_all.20.reply_ref = s32[16,13,4,128]{3,2,1,0:T(4,128)S(1)} all-to-all(s32[16,13,4,128]{3,2,1,0:T(4,128)S(1)} %prefix.1), channel_id=1, replica_groups=mesh['engine'=16,'seq'=16] {'engine'}, dimensions={0} | all-to-all | bytes 851968 | tf_op jit(solution)/shard_map/all_to_all | solution.py:429
  62.4 0.6 select.3
  63.0 18.6 %all_to_all.21.chosen_ref = s32[16,9,4,128]{3,2,1,0:T(4,128)S(1)} all-to-all(s32[16,9,4,128]{3,2,1,0:T(4,128)S(1)} %select.3), channel_id=1, replica_groups=mesh['engine'=16,'seq'=16] {'seq'}, dimensions={0} | all-to-all | bytes 589824 | tf_op jit(solution)/shard_map/all_to_all | solution.py:439
  81.6 1.1 %combine.1 = bf16[2,4,4096]{2,1,0:T(4,128)(2,1)} custom-call(s32[16,9,4,128]{3,2,1,0:T(4,128)S(1)} %all_to_all.21.chosen_ref, f32[2,128,128]{2,1,0:T(8,128)S(1)} %get-tuple-element.24.suffix_out_ref, f32[2,128,128]{2,1,0:T(8,128)S(1)} %get-tuple-element.16._.suffix_log_ref), custom_call_target="tpu_custom_call" | custom-call | tf_op jit(solution)/shard_map/combine/pallas_call | solution.py:441
Async XLA Ops:
  1.6 10.2 %copy-start.2 = (bf16[2,128,128]{2,1,0:T(8,128)(2,1)S(1)}, bf16[2,128,128]{2,1,0:T(8,128)(2,1)}, u32[]{:S(2)}) copy-start(bf16[2,128,128]{2,1,0:T(8,128)(2,1)} %get-tuple-element.15.rows_ref) | copy-start | bytes 196612
  1.6 22.5 %all-to-all-start = ((bf16[16,72,128]{2,1,0:T(8,128)(2,1)}), bf16[16,72,128]{2,1,0:T(8,128)(2,1)S(1)}, u32[]{:S(2)}, u32[]{:S(2)}) async-start(bf16[16,72,128]{2,1,0:T(8,128)(2,1)} %get-tuple-element.18), calls=%async_computation | async-start | bytes 589824 | tf_op jit(solution)/shard_map/all_to_all | solution.py:329
  11.7 0.7 copy-start.4
  11.8 0.7 copy-start.3
  11.8 0.7 copy-start.5
  12.5 1.2 %copy-start = (bf16[2,512,512]{2,1,0:T(8,128)(2,1)S(1)}, bf16[2,512,512]{2,1,0:T(8,128)(2,1)}, u32[]{:S(2)}) copy-start(bf16[2,512,512]{2,1,0:T(8,128)(2,1)} %k_ref.2) | copy-start | bytes 3145732
  13.7 1.2 %copy-start.1 = (bf16[2,512,512]{2,1,0:T(8,128)(2,1)S(1)}, bf16[2,512,512]{2,1,0:T(8,128)(2,1)}, u32[]{:S(2)}) copy-start(bf16[2,512,512]{2,1,0:T(8,128)(2,1)} %v_ref.2) | copy-start | bytes 3145732
  20.3 11.6 %collective-permute-start = (bf16[2,1024,128]{2,1,0:T(8,128)(2,1)}, bf16[2,1024,128]{2,1,0:T(8,128)(2,1)S(1)}, u32[]{:S(2)}, u32[]{:S(2)}) collective-permute-start(bf16[2,1024,128]{2,1,0:T(8,128)(2,1)} %get-tuple-element.21), channel_id=1, source_target_pairs={{0,1},{1,0},{2,3},{3,2},{4,5},{5,4},{6,7},{7,6},{8,9},{9,8},{10,11... | collective-permute-start | bytes 1572872 | tf_op jit(solution)/shard_map/ppermute | solution.py:395
  20.5 11.4 %collective-permute-start.1 = (bf16[2,1024,128]{2,1,0:T(8,128)(2,1)}, bf16[2,1024,128]{2,1,0:T(8,128)(2,1)S(1)}, u32[]{:S(2)}, u32[]{:S(2)}) collective-permute-start(bf16[2,1024,128]{2,1,0:T(8,128)(2,1)} %get-tuple-element.22), channel_id=1, source_target_pairs={{0,14},{1,3},{2,0},{3,5},{4,2},{5,7},{6,4},{7,9},{8,6},{9,11},{10,... | collective-permute-start | bytes 1572872 | tf_op jit(solution)/shard_map/ppermute | solution.py:395
  22.1 13.4 %collective-permute-start.2 = (bf16[2,1024,128]{2,1,0:T(8,128)(2,1)S(1)}, bf16[2,1024,128]{2,1,0:T(8,128)(2,1)S(1)}, u32[]{:S(2)}, u32[]{:S(2)}) collective-permute-start(bf16[2,1024,128]{2,1,0:T(8,128)(2,1)S(1)} %get-tuple-element.23), channel_id=1, source_target_pairs={{0,15},{1,2},{2,1},{3,4},{4,3},{5,6},{6,5},{7,8},{8,7},{9,10},{10,... | collective-permute-start | bytes 1572872 | tf_op jit(solution)/shard_map/ppermute | solution.py:395
  25.1 16.8 %all-to-all-start.1 = ((bf16[16,96,128]{2,1,0:T(8,128)(2,1)}), bf16[16,96,128]{2,1,0:T(8,128)(2,1)S(1)}, u32[]{:S(2)}, u32[]{:S(2)}) async-start(bf16[16,96,128]{2,1,0:T(8,128)(2,1)} %get-tuple-element.20), calls=%async_computation.1 | async-start | bytes 786432 | tf_op jit(solution)/shard_map/all_to_all | solution.py:416

commit v14 on v11

--- a/solution.py
+++ b/solution.py
@@ -76,7 +76,7 @@
         keys.wait()
 
 
-def pack_kernel(samples, _, received_ref, packed_ref, slots_ref, counts_ref):
+def pack_kernel(samples, received_ref, packed_ref, slots_ref, counts_ref):
     prompts, part = packed_ref.shape[0], packed_ref.shape[1] // CAPE
     packed_ref[...] = jnp.zeros(packed_ref.shape, packed_ref.dtype)
     for prompt in range(prompts):
@@ -118,7 +118,7 @@
     return code.astype(jnp.int32), power.astype(jnp.int32)
 
 
-def prefix_kernel(chunk, q_ref, *refs):
+def prefix_kernel(chunk, _, q_ref, *refs):
     blocks, reply_ref = refs[:-1], refs[-1]
     slots, per = q_ref.shape[0], q_ref.shape[1]
     rows_of = per // 2
@@ -405,22 +405,23 @@
             pltpu.HBM((engine_count, CAPE * per, HD), jnp.bfloat16),
             shape((seq_count * samples,), jnp.int32),
         ),
-        in_specs=[pl.BlockSpec(memory_space=pl.ANY), VMEM],
+        in_specs=[VMEM],
         out_specs=(VMEM, SMEM),
         scratch_shapes=[pltpu.SMEM((engine_count,), jnp.int32)],
         compiler_params=params(16),
         name="pack",
-    )(suffix_log, received)
+    )(received)
     dispatched = lax.all_to_all(packed, "engine", split_axis=0, concat_axis=0, tiled=True)
 
     reply = pl.pallas_call(
         functools.partial(prefix_kernel, 16),
         out_shape=shape((engine_count, CAPE * per // 8 + 1, 4, HD), jnp.int32),
-        in_specs=[VMEM] * (1 + KVH),
+        in_specs=[pl.BlockSpec(memory_space=pl.ANY)] + [VMEM] * (1 + KVH),
         out_specs=VMEM,
         compiler_params=params(16),
         name="prefix",
     )(
+        suffix_log,
         dispatched.reshape(engine_count * CAPE, per, HD),
         *[pltpu.with_memory_space_constraint(block, pltpu.VMEM) for block in blocks],
     )

time: 81.8 us -> 83 us (1.015)
  Pallas kernels: 18 us -> 19.5 us
    all_to_all x1, waiting for transfers between devices: 10.5 us -> 7.1 us  [local(): lax.all_to_all(packed, 'engine', split_axis=0, concat_axis=0, tiled=True)]
    all_to_all x1, waiting for transfers between devices: 4.72 us -> 7.37 us  [local(): lax.all_to_all(payload, 'seq', split_axis=0, concat_axis=0, tiled=True)]
    pallas_call x1, Pallas kernels: 8.13 us -> 9.41 us  [local(): pl.pallas_call(functools.partial(prefix_kernel, 16), out_shape=shape((eng...]
where the time goes in v14:
time: 83 us; the launch traced here: 82.6 us
  blocking collectives  28.9 us (35%)
  Pallas kernels  19.5 us (23%)
  starting transfers between devices  19 us (23%)
  waiting for transfers between devices  14.5 us (17%)
    all_to_all x1, blocking collectives, local(): lax.all_to_all(chosen, 'seq', split_axis=0, concat_axis=0, tiled=True)  16.8 us
    all_to_all x1, blocking collectives, local(): lax.all_to_all(reply, 'engine', split_axis=0, concat_axis=0, tiled=True)  12 us
    all_to_all x1, starting transfers between devices, local(): lax.all_to_all(payload, 'seq', split_axis=0, concat_axis=0, tiled=True)  9.98 us
    pallas_call x1, Pallas kernels, local(): pl.pallas_call(functools.partial(prefix_kernel, 16), out_shape=shape((eng...  9.41 us
    all_to_all x1, waiting for transfers between devices, local(): lax.all_to_all(payload, 'seq', split_axis=0, concat_axis=0, tiled=True)  7.37 us
    all_to_all x1, waiting for transfers between devices, local(): lax.all_to_all(packed, 'engine', split_axis=0, concat_axis=0, tiled=True)  7.1 us
    all_to_all x1, starting transfers between devices, local(): lax.all_to_all(packed, 'engine', split_axis=0, concat_axis=0, tiled=True)  6.77 us
    pallas_call x1, Pallas kernels, local(): pl.pallas_call(split_kernel, out_shape=[shape((2, positions, HD), jnp.bfl...  2.89 us
  transfers between devices with their start and end apart: 5, of which 2 were waited for; matrix products, arithmetic and copies ran while one was open for 0% of the time, Pallas kernels for 8%

profile of v14, /device:TPU:1, one launch (start us, length us, event | category | flops | bytes accessed | tf_op | source)
XLA Modules:
  0.0 82.6 jit_solution(6724067309059017256)
XLA Ops:
  0.0 1.6 %prepare.1 = (bf16[2,128,128]{2,1,0:T(8,128)(2,1)}, bf16[16,72,128]{2,1,0:T(8,128)(2,1)}) custom-call(s32[2]{0:T(128)} %bitcast.4, bf16[2,4,4096]{2,1,0:T(4,128)(2,1)} %queries_ref.1), custom_call_target="tpu_custom_call" | custom-call | tf_op jit(solution)/shard_map/prepare/pallas_call | solution.py:352
  1.6 10.0 %all-to-all-start = ((bf16[16,72,128]{2,1,0:T(8,128)(2,1)}), bf16[16,72,128]{2,1,0:T(8,128)(2,1)S(1)}, u32[]{:S(2)}, u32[]{:S(2)}) async-start(bf16[16,72,128]{2,1,0:T(8,128)(2,1)} %get-tuple-element.15), calls=%async_computation | async-start | bytes 589824 | tf_op jit(solution)/shard_map/all_to_all | solution.py:362
  11.6 0.0 copy-start.1
  11.6 0.0 copy-start.2
  11.6 2.9 %split.1 = (bf16[2,1024,128]{2,1,0:T(8,128)(2,1)S(1)}, bf16[2,1024,128]{2,1,0:T(8,128)(2,1)}, bf16[2,1024,128]{2,1,0:T(8,128)(2,1)}, bf16[2,1024,128]{2,1,0:T(8,128)(2,1)}) custom-call(s32[1]{0:T(128)} %bitcast.2.head_ref, bf16[1,1024,512]{2,1,0:T(8,128)(2,1)} %k_ref.3, bf16[1,1024,512]{2,1,0:T(8,128)(2,1)} %v_ref.3), custom_call_target="tpu_custom_call" | custom-call | tf_op jit(solution)/shard_map/split/pallas_call | solution.py:320
  14.5 0.0 copy-start
  14.5 0.2 collective-permute-start
  14.7 1.6 %collective-permute-start.1 = (bf16[2,1024,128]{2,1,0:T(8,128)(2,1)}, bf16[2,1024,128]{2,1,0:T(8,128)(2,1)}, u32[]{:S(2)}, u32[]{:S(2)}) collective-permute-start(bf16[2,1024,128]{2,1,0:T(8,128)(2,1)} %get-tuple-element.22), channel_id=1, source_target_pairs={{0,14},{1,3},{2,0},{3,5},{4,2},{5,7},{6,4},{7,9},{8,6},{9,11},{10,... | collective-permute-start | bytes 1572872 | tf_op jit(solution)/shard_map/ppermute | solution.py:343
  16.4 0.4 collective-permute-start.2
  16.8 7.4 %all-to-all-done.received_ref = bf16[16,72,128]{2,1,0:T(8,128)(2,1)S(1)} async-done(((bf16[16,72,128]{2,1,0:T(8,128)(2,1)}), bf16[16,72,128]{2,1,0:T(8,128)(2,1)S(1)}, u32[]{:S(2)}, u32[]{:S(2)}) %all-to-all-start) | async-done | bytes 294944 | tf_op jit(solution)/shard_map/all_to_all | solution.py:362
  24.1 1.0 %pack.1 = (bf16[16,96,128]{2,1,0:T(8,128)(2,1)}, s32[32]{0:T(128)S(1)}) custom-call(bf16[16,72,128]{2,1,0:T(8,128)(2,1)S(1)} %all-to-all-done.received_ref), custom_call_target="tpu_custom_call" | custom-call | tf_op jit(solution)/shard_map/pack/pallas_call | solution.py:402
  25.2 0.0 copy-start.3
  25.2 0.0 copy-start.4
  25.2 6.8 %all-to-all-start.1 = ((bf16[16,96,128]{2,1,0:T(8,128)(2,1)}), bf16[16,96,128]{2,1,0:T(8,128)(2,1)S(1)}, u32[]{:S(2)}, u32[]{:S(2)}) async-start(bf16[16,96,128]{2,1,0:T(8,128)(2,1)} %get-tuple-element.19), calls=%async_computation.1 | async-start | bytes 786432 | tf_op jit(solution)/shard_map/all_to_all | solution.py:414
  32.0 0.0 copy-start.5
  32.0 0.0 copy-done.1
  32.0 0.0 copy-done.2
  32.0 0.0 copy-done
  32.0 0.0 copy-done.3
  32.0 0.0 copy-done.4
  32.0 0.6 copy-done.5
  32.6 2.7 %suffix.1 = (f32[2,128,128]{2,1,0:T(8,128)S(1)}, f32[2,128,128]{2,1,0:T(8,128)S(1)}) custom-call(s32[2]{0:T(128)S(1)} %copy-done.5, bf16[2,128,128]{2,1,0:T(8,128)(2,1)S(1)} %copy-done.2, bf16[2,4,512]{2,1,0:T(4,128)(2,1)S(1)} %copy-done.3, bf16[2,4,512]{2,1,0:T(4,128)(2,1)S(1)} %copy-done.4, bf16[2,512,512]{2,1,0:T(8,128)(2,1)S(1)} %copy-done, ...), custom_call_target="tpu_custom_call" | custom-call | tf_op jit(solution)/shard_map/suffix/pallas_call | solution.py:383
  35.4 0.0 collective-permute-done.refs_1_
  35.4 0.0 collective-permute-done.1.refs_2_
  35.4 0.0 collective-permute-done.2.refs_3_
  35.4 7.1 %all-to-all-done.1 = bf16[16,96,128]{2,1,0:T(8,128)(2,1)S(1)} async-done(((bf16[16,96,128]{2,1,0:T(8,128)(2,1)}), bf16[16,96,128]{2,1,0:T(8,128)(2,1)S(1)}, u32[]{:S(2)}, u32[]{:S(2)}) %all-to-all-start.1) | async-done | bytes 393248 | tf_op jit(solution)/shard_map/all_to_all | solution.py:414
  42.5 9.4 %prefix.1 = s32[16,13,4,128]{3,2,1,0:T(4,128)S(1)} custom-call(f32[2,128,128]{2,1,0:T(8,128)S(1)} %get-tuple-element.18._.suffix_log_ref, bf16[48,32,128]{2,1,0:T(8,128)(2,1)S(1)} %bitcast.3, bf16[2,1024,128]{2,1,0:T(8,128)(2,1)S(1)} %get-tuple-element.20.refs_0_, bf16[2,1024,128]{2,1,0:T(8,128)(2,1)} %collective-permute-done.refs_1_, ...), custom_call_target="tpu_custom_call" | custom-call | tf_op jit(solution)/shard_map/prefix/pallas_call | solution.py:416
  51.9 12.0 %all_to_all.20.reply_ref = s32[16,13,4,128]{3,2,1,0:T(4,128)S(1)} all-to-all(s32[16,13,4,128]{3,2,1,0:T(4,128)S(1)} %prefix.1), channel_id=1, replica_groups=mesh['engine'=16,'seq'=16] {'engine'}, dimensions={0} | all-to-all | bytes 851968 | tf_op jit(solution)/shard_map/all_to_all | solution.py:428
  63.9 0.6 select.3
  64.6 16.8 %all_to_all.21.chosen_ref = s32[16,9,4,128]{3,2,1,0:T(4,128)S(1)} all-to-all(s32[16,9,4,128]{3,2,1,0:T(4,128)S(1)} %select.3), channel_id=1, replica_groups=mesh['engine'=16,'seq'=16] {'seq'}, dimensions={0} | all-to-all | bytes 589824 | tf_op jit(solution)/shard_map/all_to_all | solution.py:438
  81.4 1.1 %combine.1 = bf16[2,4,4096]{2,1,0:T(4,128)(2,1)} custom-call(s32[16,9,4,128]{3,2,1,0:T(4,128)S(1)} %all_to_all.21.chosen_ref, f32[2,128,128]{2,1,0:T(8,128)S(1)} %get-tuple-element.24.suffix_out_ref, f32[2,128,128]{2,1,0:T(8,128)S(1)} %get-tuple-element.18._.suffix_log_ref), custom_call_target="tpu_custom_call" | custom-call | tf_op jit(solution)/shard_map/combine/pallas_call | solution.py:440
Async XLA Ops:
  1.6 22.5 %all-to-all-start = ((bf16[16,72,128]{2,1,0:T(8,128)(2,1)}), bf16[16,72,128]{2,1,0:T(8,128)(2,1)S(1)}, u32[]{:S(2)}, u32[]{:S(2)}) async-start(bf16[16,72,128]{2,1,0:T(8,128)(2,1)} %get-tuple-element.15), calls=%async_computation | async-start | bytes 589824 | tf_op jit(solution)/shard_map/all_to_all | solution.py:362
  11.6 20.4 %copy-start.1 = (bf16[2,512,512]{2,1,0:T(8,128)(2,1)S(1)}, bf16[2,512,512]{2,1,0:T(8,128)(2,1)}, u32[]{:S(2)}) copy-start(bf16[2,512,512]{2,1,0:T(8,128)(2,1)} %v_ref.2) | copy-start | bytes 3145732
  11.6 20.4 %copy-start.2 = (bf16[2,128,128]{2,1,0:T(8,128)(2,1)S(1)}, bf16[2,128,128]{2,1,0:T(8,128)(2,1)}, u32[]{:S(2)}) copy-start(bf16[2,128,128]{2,1,0:T(8,128)(2,1)} %get-tuple-element.17.rows_ref) | copy-start | bytes 196612
  14.5 17.5 %copy-start = (bf16[2,512,512]{2,1,0:T(8,128)(2,1)S(1)}, bf16[2,512,512]{2,1,0:T(8,128)(2,1)}, u32[]{:S(2)}) copy-start(bf16[2,512,512]{2,1,0:T(8,128)(2,1)} %k_ref.2) | copy-start | bytes 3145732
  14.5 20.8 %collective-permute-start = (bf16[2,1024,128]{2,1,0:T(8,128)(2,1)}, bf16[2,1024,128]{2,1,0:T(8,128)(2,1)}, u32[]{:S(2)}, u32[]{:S(2)}) collective-permute-start(bf16[2,1024,128]{2,1,0:T(8,128)(2,1)} %get-tuple-element.21), channel_id=1, source_target_pairs={{0,1},{1,0},{2,3},{3,2},{4,5},{5,4},{6,7},{7,6},{8,9},{9,8},{10,11... | collective-permute-start | bytes 1572872 | tf_op jit(solution)/shard_map/ppermute | solution.py:343
  14.7 20.7 %collective-permute-start.1 = (bf16[2,1024,128]{2,1,0:T(8,128)(2,1)}, bf16[2,1024,128]{2,1,0:T(8,128)(2,1)}, u32[]{:S(2)}, u32[]{:S(2)}) collective-permute-start(bf16[2,1024,128]{2,1,0:T(8,128)(2,1)} %get-tuple-element.22), channel_id=1, source_target_pairs={{0,14},{1,3},{2,0},{3,5},{4,2},{5,7},{6,4},{7,9},{8,6},{9,11},{10,... | collective-permute-start | bytes 1572872 | tf_op jit(solution)/shard_map/ppermute | solution.py:343
  16.4 19.0 %collective-permute-start.2 = (bf16[2,1024,128]{2,1,0:T(8,128)(2,1)}, bf16[2,1024,128]{2,1,0:T(8,128)(2,1)}, u32[]{:S(2)}, u32[]{:S(2)}) collective-permute-start(bf16[2,1024,128]{2,1,0:T(8,128)(2,1)} %get-tuple-element.23), channel_id=1, source_target_pairs={{0,15},{1,2},{2,1},{3,4},{4,3},{5,6},{6,5},{7,8},{8,7},{9,10},{10,... | collective-permute-start | bytes 1572872 | tf_op jit(solution)/shard_map/ppermute | solution.py:343
  25.2 6.8 %copy-start.3 = (bf16[2,4,512]{2,1,0:T(4,128)(2,1)S(1)}, bf16[2,4,512]{2,1,0:T(4,128)(2,1)}, u32[]{:S(2)}) copy-start(bf16[2,4,512]{2,1,0:T(4,128)(2,1)} %fresh_k_ref.1) | copy-start | bytes 24580
  25.2 6.8 %copy-start.4 = (bf16[2,4,512]{2,1,0:T(4,128)(2,1)S(1)}, bf16[2,4,512]{2,1,0:T(4,128)(2,1)}, u32[]{:S(2)}) copy-start(bf16[2,4,512]{2,1,0:T(4,128)(2,1)} %fresh_v_ref.1) | copy-start | bytes 24580
  25.2 17.3 %all-to-all-start.1 = ((bf16[16,96,128]{2,1,0:T(8,128)(2,1)}), bf16[16,96,128]{2,1,0:T(8,128)(2,1)S(1)}, u32[]{:S(2)}, u32[]{:S(2)}) async-start(bf16[16,96,128]{2,1,0:T(8,128)(2,1)} %get-tuple-element.19), calls=%async_computation.1 | async-start | bytes 786432 | tf_op jit(solution)/shard_map/all_to_all | solution.py:414
  32.0 0.7 copy-start.5

commit v15 on v11

--- a/solution.py
+++ b/solution.py
@@ -114,7 +114,7 @@
 def encode(out):
     largest = jnp.max(jnp.abs(out), axis=0, keepdims=True)
     power = jnp.floor(jnp.log2(jnp.maximum(largest, 2.0**-112) * 1.0001)) + 1.0
-    code = jnp.clip(jnp.round(out * jnp.exp2(15.0 - power)), -32767.0, 32767.0)
+    code = jnp.round(out * jnp.exp2(15.0 - power))
     return code.astype(jnp.int32), power.astype(jnp.int32)
 
 
@@ -414,7 +414,7 @@
     dispatched = lax.all_to_all(packed, "engine", split_axis=0, concat_axis=0, tiled=True)
 
     reply = pl.pallas_call(
-        functools.partial(prefix_kernel, 16),
+        functools.partial(prefix_kernel, 8 * CAPE),
         out_shape=shape((engine_count, CAPE * per // 8 + 1, 4, HD), jnp.int32),
         in_specs=[VMEM] * (1 + KVH),
         out_specs=VMEM,

time: 81.8 us -> 82.3 us (level)
  no operation moved by 1% of the time
where the time goes in v15:
time: 82.3 us; the launch traced here: 81.9 us
  blocking collectives  28.9 us (35%)
  starting transfers between devices  19.1 us (23%)
  Pallas kernels  18.5 us (22%)
  waiting for transfers between devices  15.2 us (18%)
    all_to_all x1, blocking collectives, local(): lax.all_to_all(chosen, 'seq', split_axis=0, concat_axis=0, tiled=True)  16.9 us
    all_to_all x1, blocking collectives, local(): lax.all_to_all(reply, 'engine', split_axis=0, concat_axis=0, tiled=True)  12 us
    all_to_all x1, waiting for transfers between devices, local(): lax.all_to_all(packed, 'engine', split_axis=0, concat_axis=0, tiled=True)  10.5 us
    all_to_all x1, starting transfers between devices, local(): lax.all_to_all(payload, 'seq', split_axis=0, concat_axis=0, tiled=True)  10.1 us
    pallas_call x1, Pallas kernels, local(): pl.pallas_call(functools.partial(prefix_kernel, 8 * CAPE), out_shape=shap...  8.61 us
    all_to_all x1, starting transfers between devices, local(): lax.all_to_all(packed, 'engine', split_axis=0, concat_axis=0, tiled=True)  6.77 us
    all_to_all x1, waiting for transfers between devices, local(): lax.all_to_all(payload, 'seq', split_axis=0, concat_axis=0, tiled=True)  4.72 us
    pallas_call x1, Pallas kernels, local(): pl.pallas_call(suffix_kernel, out_shape=(shape((samples, heads * steps, H...  2.75 us
  transfers between devices with their start and end apart: 5, of which 2 were waited for; matrix products, arithmetic and copies ran while one was open for 0% of the time, Pallas kernels for 8%

profile of v15, /device:TPU:1, one launch (start us, length us, event | category | flops | bytes accessed | tf_op | source)
XLA Modules:
  0.0 81.9 jit_solution(6450390887373486151)
XLA Ops:
  0.0 1.6 %prepare.1 = (bf16[2,128,128]{2,1,0:T(8,128)(2,1)}, bf16[16,72,128]{2,1,0:T(8,128)(2,1)}) custom-call(s32[2]{0:T(128)} %bitcast.4, bf16[2,4,4096]{2,1,0:T(4,128)(2,1)} %queries_ref.1), custom_call_target="tpu_custom_call" | custom-call | tf_op jit(solution)/shard_map/prepare/pallas_call | solution.py:352
  1.6 0.0 copy-start.2
  1.6 0.0 copy-start.4
  1.6 0.0 copy-start.5
  1.6 10.1 %all-to-all-start = ((bf16[16,72,128]{2,1,0:T(8,128)(2,1)}), bf16[16,72,128]{2,1,0:T(8,128)(2,1)S(1)}, u32[]{:S(2)}, u32[]{:S(2)}) async-start(bf16[16,72,128]{2,1,0:T(8,128)(2,1)} %get-tuple-element.17), calls=%async_computation | async-start | bytes 589824 | tf_op jit(solution)/shard_map/all_to_all | solution.py:362
  11.8 0.0 copy-start
  11.8 0.0 copy-start.1
  11.8 0.0 copy-start.3
  11.8 2.8 %split.1 = (bf16[2,1024,128]{2,1,0:T(8,128)(2,1)S(1)}, bf16[2,1024,128]{2,1,0:T(8,128)(2,1)}, bf16[2,1024,128]{2,1,0:T(8,128)(2,1)}, bf16[2,1024,128]{2,1,0:T(8,128)(2,1)S(1)}) custom-call(s32[1]{0:T(128)} %bitcast.2.head_ref, bf16[1,1024,512]{2,1,0:T(8,128)(2,1)} %k_ref.3, bf16[1,1024,512]{2,1,0:T(8,128)(2,1)} %v_ref.3), custom_call_target="tpu_custom_call" | custom-call | tf_op jit(solution)/shard_map/split/pallas_call | solution.py:320
  14.5 0.2 collective-permute-start
  14.7 1.6 %collective-permute-start.1 = (bf16[2,1024,128]{2,1,0:T(8,128)(2,1)}, bf16[2,1024,128]{2,1,0:T(8,128)(2,1)S(1)}, u32[]{:S(2)}, u32[]{:S(2)}) collective-permute-start(bf16[2,1024,128]{2,1,0:T(8,128)(2,1)} %get-tuple-element.22), channel_id=1, source_target_pairs={{0,14},{1,3},{2,0},{3,5},{4,2},{5,7},{6,4},{7,9},{8,6},{9,11},{10,... | collective-permute-start | bytes 1572872 | tf_op jit(solution)/shard_map/ppermute | solution.py:343
  16.4 0.4 collective-permute-start.2
  16.8 0.0 copy-done.2
  16.8 0.0 copy-done.4
  16.8 0.0 copy-done.5
  16.8 0.0 copy-done
  16.8 0.0 copy-done.1
  16.8 0.0 copy-done.3
  16.8 2.8 %suffix.1 = (f32[2,128,128]{2,1,0:T(8,128)S(1)}, f32[2,128,128]{2,1,0:T(8,128)S(1)}) custom-call(s32[2]{0:T(128)S(1)} %copy-done.5, bf16[2,128,128]{2,1,0:T(8,128)(2,1)S(1)} %copy-done.2, bf16[2,4,512]{2,1,0:T(4,128)(2,1)S(1)} %copy-done.3, bf16[2,4,512]{2,1,0:T(4,128)(2,1)S(1)} %copy-done.4, bf16[2,512,512]{2,1,0:T(8,128)(2,1)S(1)} %copy-done, ...), custom_call_target="tpu_custom_call" | custom-call | tf_op jit(solution)/shard_map/suffix/pallas_call | solution.py:383
  19.6 4.7 %all-to-all-done.received_ref = bf16[16,72,128]{2,1,0:T(8,128)(2,1)S(1)} async-done(((bf16[16,72,128]{2,1,0:T(8,128)(2,1)}), bf16[16,72,128]{2,1,0:T(8,128)(2,1)S(1)}, u32[]{:S(2)}, u32[]{:S(2)}) %all-to-all-start) | async-done | bytes 294944 | tf_op jit(solution)/shard_map/all_to_all | solution.py:362
  24.3 1.0 %pack.1 = (bf16[16,96,128]{2,1,0:T(8,128)(2,1)}, s32[32]{0:T(128)S(1)}) custom-call(f32[2,128,128]{2,1,0:T(8,128)S(1)} %get-tuple-element.16._.suffix_log_ref, bf16[16,72,128]{2,1,0:T(8,128)(2,1)S(1)} %all-to-all-done.received_ref), custom_call_target="tpu_custom_call" | custom-call | tf_op jit(solution)/shard_map/pack/pallas_call | solution.py:402
  25.3 6.8 %all-to-all-start.1 = ((bf16[16,96,128]{2,1,0:T(8,128)(2,1)}), bf16[16,96,128]{2,1,0:T(8,128)(2,1)S(1)}, u32[]{:S(2)}, u32[]{:S(2)}) async-start(bf16[16,96,128]{2,1,0:T(8,128)(2,1)} %get-tuple-element.19), calls=%async_computation.1 | async-start | bytes 786432 | tf_op jit(solution)/shard_map/all_to_all | solution.py:414
  32.1 0.0 collective-permute-done.refs_1_
  32.1 0.0 collective-permute-done.1.refs_2_
  32.1 0.0 collective-permute-done.2.refs_3_
  32.1 10.5 %all-to-all-done.1 = bf16[16,96,128]{2,1,0:T(8,128)(2,1)S(1)} async-done(((bf16[16,96,128]{2,1,0:T(8,128)(2,1)}), bf16[16,96,128]{2,1,0:T(8,128)(2,1)S(1)}, u32[]{:S(2)}, u32[]{:S(2)}) %all-to-all-start.1) | async-done | bytes 393248 | tf_op jit(solution)/shard_map/all_to_all | solution.py:414
  42.6 8.6 %prefix.1 = s32[16,13,4,128]{3,2,1,0:T(4,128)S(1)} custom-call(bf16[48,32,128]{2,1,0:T(8,128)(2,1)S(1)} %bitcast.3, bf16[2,1024,128]{2,1,0:T(8,128)(2,1)S(1)} %get-tuple-element.20.refs_0_, bf16[2,1024,128]{2,1,0:T(8,128)(2,1)S(1)} %collective-permute-done.refs_1_, bf16[2,1024,128]{2,1,0:T(8,128)(2,1)S(1)} %collective-permute-done.1.refs_2_, ...), custom_call_target="tpu_custom_call" | custom-call | tf_op jit(solution)/shard_map/prefix/pallas_call | solution.py:416
  51.2 12.0 %all_to_all.20.reply_ref = s32[16,13,4,128]{3,2,1,0:T(4,128)S(1)} all-to-all(s32[16,13,4,128]{3,2,1,0:T(4,128)S(1)} %prefix.1), channel_id=1, replica_groups=mesh['engine'=16,'seq'=16] {'engine'}, dimensions={0} | all-to-all | bytes 851968 | tf_op jit(solution)/shard_map/all_to_all | solution.py:427
  63.3 0.6 select.3
  63.9 16.9 %all_to_all.21.chosen_ref = s32[16,9,4,128]{3,2,1,0:T(4,128)S(1)} all-to-all(s32[16,9,4,128]{3,2,1,0:T(4,128)S(1)} %select.3), channel_id=1, replica_groups=mesh['engine'=16,'seq'=16] {'seq'}, dimensions={0} | all-to-all | bytes 589824 | tf_op jit(solution)/shard_map/all_to_all | solution.py:437
  80.7 1.1 %combine.1 = bf16[2,4,4096]{2,1,0:T(4,128)(2,1)} custom-call(s32[16,9,4,128]{3,2,1,0:T(4,128)S(1)} %all_to_all.21.chosen_ref, f32[2,128,128]{2,1,0:T(8,128)S(1)} %get-tuple-element.24.suffix_out_ref, f32[2,128,128]{2,1,0:T(8,128)S(1)} %get-tuple-element.16._.suffix_log_ref), custom_call_target="tpu_custom_call" | custom-call | tf_op jit(solution)/shard_map/combine/pallas_call | solution.py:439
Async XLA Ops:
  1.6 15.1 %copy-start.2 = (bf16[2,128,128]{2,1,0:T(8,128)(2,1)S(1)}, bf16[2,128,128]{2,1,0:T(8,128)(2,1)}, u32[]{:S(2)}) copy-start(bf16[2,128,128]{2,1,0:T(8,128)(2,1)} %get-tuple-element.15.rows_ref) | copy-start | bytes 196612
  1.6 15.1 %copy-start.4 = (bf16[2,4,512]{2,1,0:T(4,128)(2,1)S(1)}, bf16[2,4,512]{2,1,0:T(4,128)(2,1)}, u32[]{:S(2)}) copy-start(bf16[2,4,512]{2,1,0:T(4,128)(2,1)} %fresh_v_ref.1) | copy-start | bytes 24580
  1.6 15.1 %copy-start.5 = (s32[2]{0:T(128)S(1)}, s32[2]{0:T(128)}, u32[]{:S(2)}) copy-start(s32[2]{0:T(128)} %length_ref.1) | copy-start | bytes 28
  1.6 22.6 %all-to-all-start = ((bf16[16,72,128]{2,1,0:T(8,128)(2,1)}), bf16[16,72,128]{2,1,0:T(8,128)(2,1)S(1)}, u32[]{:S(2)}, u32[]{:S(2)}) async-start(bf16[16,72,128]{2,1,0:T(8,128)(2,1)} %get-tuple-element.17), calls=%async_computation | async-start | bytes 589824 | tf_op jit(solution)/shard_map/all_to_all | solution.py:362
  11.8 5.0 %copy-start = (bf16[2,512,512]{2,1,0:T(8,128)(2,1)S(1)}, bf16[2,512,512]{2,1,0:T(8,128)(2,1)}, u32[]{:S(2)}) copy-start(bf16[2,512,512]{2,1,0:T(8,128)(2,1)} %k_ref.2) | copy-start | bytes 3145732
  11.8 5.0 %copy-start.1 = (bf16[2,512,512]{2,1,0:T(8,128)(2,1)S(1)}, bf16[2,512,512]{2,1,0:T(8,128)(2,1)}, u32[]{:S(2)}) copy-start(bf16[2,512,512]{2,1,0:T(8,128)(2,1)} %v_ref.2) | copy-start | bytes 3145732
  11.8 5.0 %copy-start.3 = (bf16[2,4,512]{2,1,0:T(4,128)(2,1)S(1)}, bf16[2,4,512]{2,1,0:T(4,128)(2,1)}, u32[]{:S(2)}) copy-start(bf16[2,4,512]{2,1,0:T(4,128)(2,1)} %fresh_k_ref.1) | copy-start | bytes 24580
  14.5 17.5 %collective-permute-start = (bf16[2,1024,128]{2,1,0:T(8,128)(2,1)}, bf16[2,1024,128]{2,1,0:T(8,128)(2,1)S(1)}, u32[]{:S(2)}, u32[]{:S(2)}) collective-permute-start(bf16[2,1024,128]{2,1,0:T(8,128)(2,1)} %get-tuple-element.21), channel_id=1, source_target_pairs={{0,1},{1,0},{2,3},{3,2},{4,5},{5,4},{6,7},{7,6},{8,9},{9,8},{10,11... | collective-permute-start | bytes 1572872 | tf_op jit(solution)/shard_map/ppermute | solution.py:343
  14.7 17.4 %collective-permute-start.1 = (bf16[2,1024,128]{2,1,0:T(8,128)(2,1)}, bf16[2,1024,128]{2,1,0:T(8,128)(2,1)S(1)}, u32[]{:S(2)}, u32[]{:S(2)}) collective-permute-start(bf16[2,1024,128]{2,1,0:T(8,128)(2,1)} %get-tuple-element.22), channel_id=1, source_target_pairs={{0,14},{1,3},{2,0},{3,5},{4,2},{5,7},{6,4},{7,9},{8,6},{9,11},{10,... | collective-permute-start | bytes 1572872 | tf_op jit(solution)/shard_map/ppermute | solution.py:343
  16.4 15.8 %collective-permute-start.2 = (bf16[2,1024,128]{2,1,0:T(8,128)(2,1)S(1)}, bf16[2,1024,128]{2,1,0:T(8,128)(2,1)S(1)}, u32[]{:S(2)}, u32[]{:S(2)}) collective-permute-start(bf16[2,1024,128]{2,1,0:T(8,128)(2,1)S(1)} %get-tuple-element.23), channel_id=1, source_target_pairs={{0,15},{1,2},{2,1},{3,4},{4,3},{5,6},{6,5},{7,8},{8,7},{9,10},{10,... | collective-permute-start | bytes 1572872 | tf_op jit(solution)/shard_map/ppermute | solution.py:343
  25.3 17.3 %all-to-all-start.1 = ((bf16[16,96,128]{2,1,0:T(8,128)(2,1)}), bf16[16,96,128]{2,1,0:T(8,128)(2,1)S(1)}, u32[]{:S(2)}, u32[]{:S(2)}) async-start(bf16[16,96,128]{2,1,0:T(8,128)(2,1)} %get-tuple-element.19), calls=%async_computation.1 | async-start | bytes 786432 | tf_op jit(solution)/shard_map/all_to_all | solution.py:414

commit v16 on v11

--- a/solution.py
+++ b/solution.py
@@ -164,7 +164,8 @@
     starts = range(0, slots, chunk)
     stages = [(start, place) for start in starts for place in range(len(blocks))]
     rows = {start: rows_from(start) for start in starts}
-    raw, waiting, parts = block_scores(rows[0], blocks[0][0]), None, []
+    scored = lambda stage: block_scores(rows[stage[0]], blocks[stage[1]][0])
+    raws, waiting, parts = [scored(stage) for stage in stages[:2]], None, []
 
     def product():
         (start, place), (probs, top, total) = waiting
@@ -174,10 +175,9 @@
             parts.clear()
 
     for number, stage in enumerate(stages):
-        ready = raw
-        if number + 1 < len(stages):
-            later, block = stages[number + 1]
-            raw = block_scores(rows[later], blocks[block][0])
+        ready = raws.pop(0)
+        if number + 2 < len(stages):
+            raws.append(scored(stages[number + 2]))
         if waiting is not None:
             product()
         waiting = (stage, block_softmax(ready))

time: 81.8 us -> 82.3 us (level)
  no operation moved by 1% of the time
where the time goes in v16:
time: 82.3 us; the launch traced here: 81.9 us
  blocking collectives  28.9 us (35%)
  starting transfers between devices  19.1 us (23%)
  Pallas kernels  18.6 us (23%)
  waiting for transfers between devices  15.2 us (18%)
    all_to_all x1, blocking collectives, local(): lax.all_to_all(chosen, 'seq', split_axis=0, concat_axis=0, tiled=True)  16.8 us
    all_to_all x1, blocking collectives, local(): lax.all_to_all(reply, 'engine', split_axis=0, concat_axis=0, tiled=True)  12 us
    all_to_all x1, waiting for transfers between devices, local(): lax.all_to_all(packed, 'engine', split_axis=0, concat_axis=0, tiled=True)  10.5 us
    all_to_all x1, starting transfers between devices, local(): lax.all_to_all(payload, 'seq', split_axis=0, concat_axis=0, tiled=True)  10.1 us
    pallas_call x1, Pallas kernels, local(): pl.pallas_call(functools.partial(prefix_kernel, 16), out_shape=shape((eng...  8.64 us
    all_to_all x1, starting transfers between devices, local(): lax.all_to_all(packed, 'engine', split_axis=0, concat_axis=0, tiled=True)  6.77 us
    all_to_all x1, waiting for transfers between devices, local(): lax.all_to_all(payload, 'seq', split_axis=0, concat_axis=0, tiled=True)  4.72 us
    pallas_call x1, Pallas kernels, local(): pl.pallas_call(suffix_kernel, out_shape=(shape((samples, heads * steps, H...  2.75 us
  transfers between devices with their start and end apart: 5, of which 2 were waited for; matrix products, arithmetic and copies ran while one was open for 0% of the time, Pallas kernels for 8%

profile of v16, /device:TPU:1, one launch (start us, length us, event | category | flops | bytes accessed | tf_op | source)
XLA Modules:
  0.0 81.9 jit_solution(17297041735326899825)
XLA Ops:
  0.0 1.6 %prepare.1 = (bf16[2,128,128]{2,1,0:T(8,128)(2,1)}, bf16[16,72,128]{2,1,0:T(8,128)(2,1)}) custom-call(s32[2]{0:T(128)} %bitcast.4, bf16[2,4,4096]{2,1,0:T(4,128)(2,1)} %queries_ref.1), custom_call_target="tpu_custom_call" | custom-call | tf_op jit(solution)/shard_map/prepare/pallas_call | solution.py:352
  1.6 0.0 copy-start.2
  1.6 0.0 copy-start.4
  1.6 0.0 copy-start.5
  1.6 10.1 %all-to-all-start = ((bf16[16,72,128]{2,1,0:T(8,128)(2,1)}), bf16[16,72,128]{2,1,0:T(8,128)(2,1)S(1)}, u32[]{:S(2)}, u32[]{:S(2)}) async-start(bf16[16,72,128]{2,1,0:T(8,128)(2,1)} %get-tuple-element.17), calls=%async_computation | async-start | bytes 589824 | tf_op jit(solution)/shard_map/all_to_all | solution.py:362
  11.8 0.0 copy-start
  11.8 0.0 copy-start.1
  11.8 0.0 copy-start.3
  11.8 2.8 %split.1 = (bf16[2,1024,128]{2,1,0:T(8,128)(2,1)S(1)}, bf16[2,1024,128]{2,1,0:T(8,128)(2,1)}, bf16[2,1024,128]{2,1,0:T(8,128)(2,1)}, bf16[2,1024,128]{2,1,0:T(8,128)(2,1)S(1)}) custom-call(s32[1]{0:T(128)} %bitcast.2.head_ref, bf16[1,1024,512]{2,1,0:T(8,128)(2,1)} %k_ref.3, bf16[1,1024,512]{2,1,0:T(8,128)(2,1)} %v_ref.3), custom_call_target="tpu_custom_call" | custom-call | tf_op jit(solution)/shard_map/split/pallas_call | solution.py:320
  14.5 0.2 collective-permute-start
  14.7 1.6 %collective-permute-start.1 = (bf16[2,1024,128]{2,1,0:T(8,128)(2,1)}, bf16[2,1024,128]{2,1,0:T(8,128)(2,1)S(1)}, u32[]{:S(2)}, u32[]{:S(2)}) collective-permute-start(bf16[2,1024,128]{2,1,0:T(8,128)(2,1)} %get-tuple-element.22), channel_id=1, source_target_pairs={{0,14},{1,3},{2,0},{3,5},{4,2},{5,7},{6,4},{7,9},{8,6},{9,11},{10,... | collective-permute-start | bytes 1572872 | tf_op jit(solution)/shard_map/ppermute | solution.py:343
  16.4 0.4 collective-permute-start.2
  16.8 0.0 copy-done.2
  16.8 0.0 copy-done.4
  16.8 0.0 copy-done.5
  16.8 0.0 copy-done
  16.8 0.0 copy-done.1
  16.8 0.0 copy-done.3
  16.8 2.8 %suffix.1 = (f32[2,128,128]{2,1,0:T(8,128)S(1)}, f32[2,128,128]{2,1,0:T(8,128)S(1)}) custom-call(s32[2]{0:T(128)S(1)} %copy-done.5, bf16[2,128,128]{2,1,0:T(8,128)(2,1)S(1)} %copy-done.2, bf16[2,4,512]{2,1,0:T(4,128)(2,1)S(1)} %copy-done.3, bf16[2,4,512]{2,1,0:T(4,128)(2,1)S(1)} %copy-done.4, bf16[2,512,512]{2,1,0:T(8,128)(2,1)S(1)} %copy-done, ...), custom_call_target="tpu_custom_call" | custom-call | tf_op jit(solution)/shard_map/suffix/pallas_call | solution.py:383
  19.6 4.7 %all-to-all-done.received_ref = bf16[16,72,128]{2,1,0:T(8,128)(2,1)S(1)} async-done(((bf16[16,72,128]{2,1,0:T(8,128)(2,1)}), bf16[16,72,128]{2,1,0:T(8,128)(2,1)S(1)}, u32[]{:S(2)}, u32[]{:S(2)}) %all-to-all-start) | async-done | bytes 294944 | tf_op jit(solution)/shard_map/all_to_all | solution.py:362
  24.3 1.0 %pack.1 = (bf16[16,96,128]{2,1,0:T(8,128)(2,1)}, s32[32]{0:T(128)S(1)}) custom-call(f32[2,128,128]{2,1,0:T(8,128)S(1)} %get-tuple-element.16._.suffix_log_ref, bf16[16,72,128]{2,1,0:T(8,128)(2,1)S(1)} %all-to-all-done.received_ref), custom_call_target="tpu_custom_call" | custom-call | tf_op jit(solution)/shard_map/pack/pallas_call | solution.py:402
  25.3 6.8 %all-to-all-start.1 = ((bf16[16,96,128]{2,1,0:T(8,128)(2,1)}), bf16[16,96,128]{2,1,0:T(8,128)(2,1)S(1)}, u32[]{:S(2)}, u32[]{:S(2)}) async-start(bf16[16,96,128]{2,1,0:T(8,128)(2,1)} %get-tuple-element.19), calls=%async_computation.1 | async-start | bytes 786432 | tf_op jit(solution)/shard_map/all_to_all | solution.py:414
  32.1 0.0 collective-permute-done.refs_1_
  32.1 0.0 collective-permute-done.1.refs_2_
  32.1 0.0 collective-permute-done.2.refs_3_
  32.1 10.5 %all-to-all-done.1 = bf16[16,96,128]{2,1,0:T(8,128)(2,1)S(1)} async-done(((bf16[16,96,128]{2,1,0:T(8,128)(2,1)}), bf16[16,96,128]{2,1,0:T(8,128)(2,1)S(1)}, u32[]{:S(2)}, u32[]{:S(2)}) %all-to-all-start.1) | async-done | bytes 393248 | tf_op jit(solution)/shard_map/all_to_all | solution.py:414
  42.6 8.6 %prefix.1 = s32[16,13,4,128]{3,2,1,0:T(4,128)S(1)} custom-call(bf16[48,32,128]{2,1,0:T(8,128)(2,1)S(1)} %bitcast.3, bf16[2,1024,128]{2,1,0:T(8,128)(2,1)S(1)} %get-tuple-element.20.refs_0_, bf16[2,1024,128]{2,1,0:T(8,128)(2,1)S(1)} %collective-permute-done.refs_1_, bf16[2,1024,128]{2,1,0:T(8,128)(2,1)S(1)} %collective-permute-done.1.refs_2_, ...), custom_call_target="tpu_custom_call" | custom-call | tf_op jit(solution)/shard_map/prefix/pallas_call | solution.py:416
  51.3 12.0 %all_to_all.20.reply_ref = s32[16,13,4,128]{3,2,1,0:T(4,128)S(1)} all-to-all(s32[16,13,4,128]{3,2,1,0:T(4,128)S(1)} %prefix.1), channel_id=1, replica_groups=mesh['engine'=16,'seq'=16] {'engine'}, dimensions={0} | all-to-all | bytes 851968 | tf_op jit(solution)/shard_map/all_to_all | solution.py:427
  63.3 0.6 select.3
  63.9 16.8 %all_to_all.21.chosen_ref = s32[16,9,4,128]{3,2,1,0:T(4,128)S(1)} all-to-all(s32[16,9,4,128]{3,2,1,0:T(4,128)S(1)} %select.3), channel_id=1, replica_groups=mesh['engine'=16,'seq'=16] {'seq'}, dimensions={0} | all-to-all | bytes 589824 | tf_op jit(solution)/shard_map/all_to_all | solution.py:437
  80.8 1.1 %combine.1 = bf16[2,4,4096]{2,1,0:T(4,128)(2,1)} custom-call(s32[16,9,4,128]{3,2,1,0:T(4,128)S(1)} %all_to_all.21.chosen_ref, f32[2,128,128]{2,1,0:T(8,128)S(1)} %get-tuple-element.24.suffix_out_ref, f32[2,128,128]{2,1,0:T(8,128)S(1)} %get-tuple-element.16._.suffix_log_ref), custom_call_target="tpu_custom_call" | custom-call | tf_op jit(solution)/shard_map/combine/pallas_call | solution.py:439
Async XLA Ops:
  1.6 15.1 %copy-start.2 = (bf16[2,128,128]{2,1,0:T(8,128)(2,1)S(1)}, bf16[2,128,128]{2,1,0:T(8,128)(2,1)}, u32[]{:S(2)}) copy-start(bf16[2,128,128]{2,1,0:T(8,128)(2,1)} %get-tuple-element.15.rows_ref) | copy-start | bytes 196612
  1.6 15.1 %copy-start.4 = (bf16[2,4,512]{2,1,0:T(4,128)(2,1)S(1)}, bf16[2,4,512]{2,1,0:T(4,128)(2,1)}, u32[]{:S(2)}) copy-start(bf16[2,4,512]{2,1,0:T(4,128)(2,1)} %fresh_v_ref.1) | copy-start | bytes 24580
  1.6 15.1 %copy-start.5 = (s32[2]{0:T(128)S(1)}, s32[2]{0:T(128)}, u32[]{:S(2)}) copy-start(s32[2]{0:T(128)} %length_ref.1) | copy-start | bytes 28
  1.6 22.6 %all-to-all-start = ((bf16[16,72,128]{2,1,0:T(8,128)(2,1)}), bf16[16,72,128]{2,1,0:T(8,128)(2,1)S(1)}, u32[]{:S(2)}, u32[]{:S(2)}) async-start(bf16[16,72,128]{2,1,0:T(8,128)(2,1)} %get-tuple-element.17), calls=%async_computation | async-start | bytes 589824 | tf_op jit(solution)/shard_map/all_to_all | solution.py:362
  11.8 5.0 %copy-start = (bf16[2,512,512]{2,1,0:T(8,128)(2,1)S(1)}, bf16[2,512,512]{2,1,0:T(8,128)(2,1)}, u32[]{:S(2)}) copy-start(bf16[2,512,512]{2,1,0:T(8,128)(2,1)} %k_ref.2) | copy-start | bytes 3145732
  11.8 5.0 %copy-start.1 = (bf16[2,512,512]{2,1,0:T(8,128)(2,1)S(1)}, bf16[2,512,512]{2,1,0:T(8,128)(2,1)}, u32[]{:S(2)}) copy-start(bf16[2,512,512]{2,1,0:T(8,128)(2,1)} %v_ref.2) | copy-start | bytes 3145732
  11.8 5.0 %copy-start.3 = (bf16[2,4,512]{2,1,0:T(4,128)(2,1)S(1)}, bf16[2,4,512]{2,1,0:T(4,128)(2,1)}, u32[]{:S(2)}) copy-start(bf16[2,4,512]{2,1,0:T(4,128)(2,1)} %fresh_k_ref.1) | copy-start | bytes 24580
  14.5 17.6 %collective-permute-start = (bf16[2,1024,128]{2,1,0:T(8,128)(2,1)}, bf16[2,1024,128]{2,1,0:T(8,128)(2,1)S(1)}, u32[]{:S(2)}, u32[]{:S(2)}) collective-permute-start(bf16[2,1024,128]{2,1,0:T(8,128)(2,1)} %get-tuple-element.21), channel_id=1, source_target_pairs={{0,1},{1,0},{2,3},{3,2},{4,5},{5,4},{6,7},{7,6},{8,9},{9,8},{10,11... | collective-permute-start | bytes 1572872 | tf_op jit(solution)/shard_map/ppermute | solution.py:343
  14.7 17.4 %collective-permute-start.1 = (bf16[2,1024,128]{2,1,0:T(8,128)(2,1)}, bf16[2,1024,128]{2,1,0:T(8,128)(2,1)S(1)}, u32[]{:S(2)}, u32[]{:S(2)}) collective-permute-start(bf16[2,1024,128]{2,1,0:T(8,128)(2,1)} %get-tuple-element.22), channel_id=1, source_target_pairs={{0,14},{1,3},{2,0},{3,5},{4,2},{5,7},{6,4},{7,9},{8,6},{9,11},{10,... | collective-permute-start | bytes 1572872 | tf_op jit(solution)/shard_map/ppermute | solution.py:343
  16.4 15.8 %collective-permute-start.2 = (bf16[2,1024,128]{2,1,0:T(8,128)(2,1)S(1)}, bf16[2,1024,128]{2,1,0:T(8,128)(2,1)S(1)}, u32[]{:S(2)}, u32[]{:S(2)}) collective-permute-start(bf16[2,1024,128]{2,1,0:T(8,128)(2,1)S(1)} %get-tuple-element.23), channel_id=1, source_target_pairs={{0,15},{1,2},{2,1},{3,4},{4,3},{5,6},{6,5},{7,8},{8,7},{9,10},{10,... | collective-permute-start | bytes 1572872 | tf_op jit(solution)/shard_map/ppermute | solution.py:343
  25.3 17.3 %all-to-all-start.1 = ((bf16[16,96,128]{2,1,0:T(8,128)(2,1)}), bf16[16,96,128]{2,1,0:T(8,128)(2,1)S(1)}, u32[]{:S(2)}, u32[]{:S(2)}) async-start(bf16[16,96,128]{2,1,0:T(8,128)(2,1)} %get-tuple-element.19), calls=%async_computation.1 | async-start | bytes 786432 | tf_op jit(solution)/shard_map/all_to_all | solution.py:414
